TPU v7x, 256 devices: a whole 4x4x8 slice. The times are simulated.
256 devices in a mesh: pme: 8 (over z), dom: 32 (over x, y, core).
Axes of the slice: x: 4, y: 4, z: 8, core: 2. Of those that a mesh axis runs over, the one named last changes fastest.
Arguments:
- group_column: int32 [16384, 1], P(('pme', 'dom')), may hold values from 0 to 31, as said below
- group_corner: int32 [3, 16384], P(None, ('pme', 'dom')), may hold values from 0 to 16, as said below
- atom_cell: int32 [3, 524288], P(None, ('pme', 'dom')), may hold values from 0 to 7, as said below
- fraction: float32 [3, 524288], P(None, ('pme', 'dom')), may hold values from 0.25 to 0.75
- charge: float32 [524288], P(('pme', 'dom')), may hold values from -4 to 4
- cluster_pairs: int32 [2, 262144], P(None, ('pme', 'dom')), may hold values from 0 to 263, as said below
Outputs:
- forces: float32 [3, 524288], P(None, ('pme', 'dom'))
Inputs may be any that keep to these rules, and one draw needn't show every extreme that they name: `group_column`: in each aligned block of 64 rows (the groups of one device) no column is named by more than 4 rows, and in every block one column is named by exactly 4. `group_corner`: row 0 lies in 0 to 16, row 1 in 0 to 16, row 2 in 0 to 0. `atom_cell`: row 0 is below 8, row 1 below 8, row 2 below 4; within each group of 32 consecutive atoms the three rows form distinct triples. `cluster_pairs`: row 0 names one of the 256 clusters of the device that holds the column. Row 1 names either another cluster of the same block of 4 clusters (clusters 4 * k to 4 * k + 3) of that device, or 256 + c with c below 8, cluster c of the next device along dom.
All inputs are finite; a program needn't handle non-finite values.
Results may differ from a plain program's by a relative error of at most 0.0003.
Values sent between devices are 32-bit elements; how exact they have to be, the bound alone decides.
No kernel may reach another device: no remote copies, remote signals or barrier semaphores. Data moves between devices by JAX's collectives and lax.ppermute only.
A program may use at most 128 MiB of HBM per device.

v0:
```python
import math

import jax
import jax.numpy as jnp
import ml_dtypes
import numpy as np
from jax import lax
from jax.experimental import pallas as pl
from jax.experimental.pallas import tpu as pltpu
from jax.sharding import PartitionSpec as P

NX = 768
NY = 768
NZ = 32
N_DOM = 32
N_PME = 8
DEVICES = 256
XD = 24
YP = 24
ZP = 4
GROUPS = 64
ATOMS = 2048
PAIRS = 1024
CLUSTERS = 256
HALO_CLUSTERS = 8
HALO_ATOMS = 64
XW = 32
MODES = 3
BLOCKS = 98
BETA = 0.35
VMEM_LIMIT = 24 * 1024 * 1024

F32 = jnp.float32
BF16 = jnp.bfloat16

ERFC_Q = (
    0.2820947951,
    0.2820937768,
    0.2468838798,
    0.1753240754,
    0.0934147485,
    -0.05905091002,
    0.1318500403,
    -0.4545637183,
    0.493385742,
    -0.2346054907,
    0.04317306594,
)


def real_basis(length):
    point = np.arange(length)
    rows = np.zeros((length, length))
    waves = np.zeros(length, np.int64)
    rows[0] = 1.0 / math.sqrt(length)
    for k in range(1, length // 2):
        angle = 2.0 * math.pi * (k * point % length) / length
        rows[2 * k - 1] = math.sqrt(2.0 / length) * np.cos(angle)
        rows[2 * k] = math.sqrt(2.0 / length) * np.sin(angle)
        waves[2 * k - 1] = k
        waves[2 * k] = k
    rows[length - 1] = (1.0 - 2.0 * (point % 2)) / math.sqrt(length)
    waves[length - 1] = length // 2
    return rows, waves


def wave_factors(waves, length):
    freq = waves / length
    modulus = 1.0 / (2.0 / 3.0 + np.cos(2.0 * math.pi * waves / length) / 3.0) ** 2
    return freq * freq, np.exp(-((math.pi / BETA) ** 2) * freq * freq) * modulus


def halves(table):
    table = table.astype(np.float32)
    high = table.astype(ml_dtypes.bfloat16)
    low = (table - high.astype(np.float32)).astype(ml_dtypes.bfloat16)
    return high, low


def split(value):
    high = value.astype(BF16)
    low = (value - high.astype(F32)).astype(BF16)
    return high, low


def dot(a, b):
    return jnp.dot(a, b, preferred_element_type=F32)


def dot_nt(a, b):
    return lax.dot_general(a, b, (((1,), (1,)), ((), ())), preferred_element_type=F32)


def dot_tn(a, b):
    return lax.dot_general(a, b, (((0,), (0,)), ((), ())), preferred_element_type=F32)


def iota(shape, dim):
    return lax.broadcasted_iota(jnp.int32, shape, dim)


def spline(u):
    d = jnp.abs(u)
    a = jnp.maximum(2.0 - d, 0.0)
    b = jnp.maximum(1.0 - d, 0.0)
    return (a * a * a - 4.0 * (b * b * b)) * (1.0 / 6.0)


def spline_slope(u):
    d = jnp.abs(u)
    a = jnp.maximum(2.0 - d, 0.0)
    b = jnp.maximum(1.0 - d, 0.0)
    slope = 0.5 * (a * a) - 2.0 * (b * b)
    return slope, (a * a * a - 4.0 * (b * b * b)) * (1.0 / 6.0)


def weights_of(u):
    slope, value = spline_slope(u)
    return value, jnp.where(u < 0.0, -slope, slope)


def prepare_kernel(place, col, corner, cell, fraction, charge, atoms, edge):
    group = iota((GROUPS, ATOMS), 0)
    hot = jnp.where((iota((GROUPS, ATOMS), 1) >> 5) == group, 1.0, 0.0).astype(BF16)
    rep_corner = dot(corner[...].astype(F32).astype(BF16), hot)
    rep_col = dot(
        jnp.broadcast_to(col[...].astype(F32), (8, GROUPS)).astype(BF16), hot
    )[0:1]
    base = rep_corner + cell[...].astype(F32)
    first = (place[0] * XD).astype(F32)
    third = (place[1] * ZP).astype(F32)
    along_x = (base[0:1] + first) + fraction[0:1, :]
    along_y = (base[1:2] + rep_col * float(YP)) + fraction[1:2, :]
    along_z = (base[2:3] + third) + fraction[2:3, :]
    atoms[...] = jnp.zeros((8, ATOMS), F32)
    atoms[0:1, :] = along_x
    atoms[1:2, :] = along_y
    atoms[2:3, :] = along_z
    atoms[3:4, :] = charge[...]
    lowest = (col[...] * YP + corner[1:2, :]).astype(F32)
    atoms[4:5, 0:GROUPS] = lowest
    edge[...] = atoms[:, 0:128]


def y_blocks(ya, batch, lane):
    starts = [ya[4 * batch + j] for j in range(4)]
    row = jnp.where(
        lane < 64,
        jnp.where(lane < 32, starts[0], starts[1]),
        jnp.where(lane < 96, starts[2], starts[3]),
    )
    return starts, (row * 8).astype(F32)


def masked_blocks(weights, lane):
    return jnp.concatenate(
        [jnp.where((lane >> 5) == j, weights, 0.0) for j in range(4)], axis=0
    )


def spread_batches(origin_x, origin_z, ya, atoms, grid):
    lane = iota((1, 128), 1)
    step_x = iota((XW, 128), 0).astype(F32)
    step_y = iota((24, 128), 0).astype(F32)
    step_z = iota((8, 128), 0).astype(F32)
    for batch in range(ATOMS // 128):
        own = slice(128 * batch, 128 * batch + 128)
        starts, base_y = y_blocks(ya, batch, lane)
        xs = (atoms[0:1, own] - origin_x) + 1.0
        ys = (atoms[1:2, own] - base_y) + 1.0
        zs = (atoms[2:3, own] - origin_z) + 1.0
        wx = spline(step_x - xs)
        wz = spline(step_z - zs) * atoms[3:4, own]
        wy = masked_blocks(spline(step_y - ys), lane)
        charged = jnp.concatenate([wx * wz[z : z + 1] for z in range(ZP)], axis=0)
        c_high, c_low = split(charged)
        y_high, y_low = split(wy)
        added = dot_nt(y_high, c_high) + (dot_nt(y_high, c_low) + dot_nt(y_low, c_high))
        for j in range(4):
            part = added[24 * j : 24 * j + 24].reshape(3, 8, 128)
            grid[pl.ds(starts[j], 3)] = grid[pl.ds(starts[j], 3)] + part


def spread_own_kernel(place, ya, atoms, grid):
    grid[...] = jnp.zeros((BLOCKS, 8, 128), F32)
    origin_x = (place[0] * XD).astype(F32)
    origin_z = (place[1] * ZP).astype(F32)
    spread_batches(origin_x, origin_z, ya, atoms, grid)


def neighbour_origin(place):
    behind = (place[1] + (N_PME - 1)) & (N_PME - 1)
    return (place[0] * XD).astype(F32), (behind * ZP + ZP).astype(F32)


def spread_rest_kernel(place, ya, atoms, own, table_high, table_low, out, grid):
    grid[...] = own[...]
    origin_x, origin_z = neighbour_origin(place)
    spread_batches(origin_x, origin_z, ya, atoms, grid)
    grid[0:2] = grid[0:2] + grid[96:98]
    g_high, g_low = split(grid[0:96].reshape(NY, 128))
    both = dot(table_high[...], jnp.concatenate([g_high, g_low], axis=1))
    out[...] = both[:, :128] + (both[:, 128:] + dot(table_low[...], g_high))


def filter_kernel(
    place, y_square, y_factor, held, fx_high, fx_low, kz_high, kz_low, tz_high, tz_low,
    x_square, x_factor, z_square, z_factor, out, work,
):
    lane = iota((8, 128), 1) >> 5
    for m in range(MODES):
        for a in range(8):
            blocks = [held[pl.ds((4 * a + b) * 24 + m, 8, stride=3), :] for b in range(4)]
            for z in range(ZP):
                tile = None
                for b in range(4):
                    shift = (32 * (b - z)) % 128
                    moved = blocks[b] if shift == 0 else pltpu.roll(blocks[b], shift, 1)
                    tile = moved if tile is None else jnp.where(lane == b, moved, tile)
                row = m * NZ + z * 8
                work[row : row + 8, 128 * a : 128 * a + 128] = tile
    x_high, x_low = split(work[...])
    waves = dot(x_high, fx_high[...]) + (dot(x_low, fx_high[...]) + dot(x_high, fx_low[...]))
    w_high, w_low = split(waves)
    full = dot(kz_high[...], w_high) + (dot(kz_high[...], w_low) + dot(kz_low[...], w_high))
    device = place[0] * N_PME + place[1]
    scaled = []
    for m in range(MODES):
        mode = device * MODES + m
        square = (x_square[...] + z_square[:, 0:1]) + y_square[mode]
        factor = (x_factor[...] * z_factor[:, 0:1]) * y_factor[mode]
        nonzero = jnp.where(square > 0.0, square, 1.0)
        influence = jnp.where(square > 0.0, factor / nonzero, 0.0)
        scaled.append(full[m * NZ : m * NZ + NZ] * influence)
    s_high, s_low = split(jnp.concatenate(scaled, axis=0))
    back = dot(tz_high[...], s_high) + (dot(tz_high[...], s_low) + dot(tz_low[...], s_high))
    b_high, b_low = split(back)
    work[...] = dot_nt(b_high, fx_high[...]) + (
        dot_nt(b_low, fx_high[...]) + dot_nt(b_high, fx_low[...])
    )
    for m in range(MODES):
        for a in range(8):
            tiles = [
                work[m * NZ + z * 8 : m * NZ + z * 8 + 8, 128 * a : 128 * a + 128]
                for z in range(ZP)
            ]
            for b in range(4):
                block = None
                for z in range(ZP):
                    shift = (32 * (z - b)) % 128
                    moved = tiles[z] if shift == 0 else pltpu.roll(tiles[z], shift, 1)
                    block = moved if block is None else jnp.where(lane == z, moved, block)
                out[pl.ds((4 * a + b) * 24 + m, 8, stride=3), :] = block


def gather_batches(origin_x, origin_z, ya, atoms, grid, store):
    lane = iota((1, 128), 1)
    step_x = iota((XW, 128), 0).astype(F32)
    step_y = iota((24, 128), 0).astype(F32)
    step_z = iota((8, 128), 0).astype(F32)
    for batch in range(ATOMS // 128):
        own = slice(128 * batch, 128 * batch + 128)
        starts, base_y = y_blocks(ya, batch, lane)
        xs = (atoms[0:1, own] - origin_x) + 1.0
        ys = (atoms[1:2, own] - base_y) + 1.0
        zs = (atoms[2:3, own] - origin_z) + 1.0
        wx, sx = weights_of(step_x - xs)
        wy, sy = weights_of(step_y - ys)
        wz, sz = weights_of(step_z - zs)
        block = jnp.concatenate(
            [grid[pl.ds(starts[j], 3)].reshape(24, 128) for j in range(4)], axis=0
        )
        b_high, b_low = split(block)
        y_both = jnp.concatenate([masked_blocks(wy, lane), masked_blocks(sy, lane)], axis=1)
        y_high, y_low = split(y_both)
        sampled = dot_tn(b_high, y_high) + (dot_tn(b_low, y_high) + dot_tn(b_high, y_low))
        along_x = along_y = along_z = jnp.zeros((XW, 128), F32)
        for z in range(ZP):
            value = sampled[XW * z : XW * z + XW, :128]
            slope = sampled[XW * z : XW * z + XW, 128:]
            along_x = along_x + value * wz[z : z + 1]
            along_y = along_y + slope * wz[z : z + 1]
            along_z = along_z + value * sz[z : z + 1]
        minus = -atoms[3:4, own]
        store(
            own,
            minus * jnp.sum(along_x * sx, axis=0, keepdims=True),
            minus * jnp.sum(along_y * wx, axis=0, keepdims=True),
            minus * jnp.sum(along_z * wx, axis=0, keepdims=True),
        )


def gather_rest_kernel(place, ya, atoms, held, table_high, table_low, grid, out):
    h_high, h_low = split(held[...])
    both = dot(table_high[...], jnp.concatenate([h_high, h_low], axis=1))
    potential = both[:, :128] + (both[:, 128:] + dot(table_low[...], h_high))
    grid[0:96] = potential.reshape(96, 8, 128)
    grid[96:98] = potential[0:16].reshape(2, 8, 128)
    origin_x, origin_z = neighbour_origin(place)

    def store(own, fx, fy, fz):
        out[0:1, own] = fx
        out[1:2, own] = fy
        out[2:3, own] = fz

    gather_batches(origin_x, origin_z, ya, atoms, grid, store)


def gather_own_kernel(place, ya, atoms, grid, near, halo, out):
    origin_x = (place[0] * XD).astype(F32)
    origin_z = (place[1] * ZP).astype(F32)

    def store(own, fx, fy, fz):
        forces = [fx, fy, fz]
        for f in range(3):
            total = forces[f] + near[f : f + 1, own]
            if own.start == 0:
                total = total + halo[f : f + 1, :]
            out[f : f + 1, own] = total

    gather_batches(origin_x, origin_z, ya, atoms, grid, store)


def pair_strength(dist_sq):
    inverse = lax.rsqrt(dist_sq)
    inverse = inverse * (1.5 - 0.5 * dist_sq * inverse * inverse)
    scaled = BETA * (dist_sq * inverse)
    t = 1.0 / (1.0 + 0.5 * scaled)
    poly = jnp.full_like(t, ERFC_Q[-1])
    for coefficient in ERFC_Q[-2::-1]:
        poly = poly * t + coefficient
    fall = jnp.exp(-(BETA * BETA) * dist_sq)
    bracket = t * poly * inverse + 2.0 * BETA / math.sqrt(math.pi)
    return fall * bracket * (inverse * inverse)


def nonbonded_kernel(place, atoms, turned, pairs, beyond, near, halo, weight, repeated, columns):
    left = pairs[0:1, :]
    right = pairs[1:2, :]
    inside = right < CLUSTERS
    cluster = iota((CLUSTERS, PAIRS), 0)
    hot_left = jnp.where(cluster == left, 1.0, 0.0).astype(BF16)
    hot_right = jnp.where(cluster == right, 1.0, 0.0).astype(BF16)
    code = iota((16, PAIRS), 0)
    code_left = jnp.where(
        code == jnp.where(inside, right & 3, right - (CLUSTERS - 4)), 1.0, 0.0
    ).astype(BF16)
    code_right = jnp.where(
        code == jnp.where(inside, left & 3, -1), 1.0, 0.0
    ).astype(BF16)
    count = dot_nt(code_left, hot_left) + dot_nt(code_right, hot_right)
    n_high, n_low = split(count)
    expand = jnp.where(
        (iota((CLUSTERS, ATOMS), 1) >> 3) == iota((CLUSTERS, ATOMS), 0), 1.0, 0.0
    ).astype(BF16)
    weight[...] = dot(n_high, expand) + dot(n_low, expand)
    turn_1 = turned[...].astype(BF16)
    rest = turned[...] - turn_1.astype(F32)
    turn_2 = rest.astype(BF16)
    turn_3 = (rest - turn_2.astype(F32)).astype(BF16)
    spreading = jnp.where(
        (iota((GROUPS, ATOMS), 1) >> 5) == iota((GROUPS, ATOMS), 0), 1.0, 0.0
    ).astype(BF16)
    repeated[...] = (dot(turn_1, spreading) + dot(turn_2, spreading)) + dot(turn_3, spreading)
    row = iota((8, 128), 0)
    lane = iota((8, 128), 1)
    for tile in range(ATOMS // 128):
        own = slice(128 * tile, 128 * tile + 128)
        px, py, pz = atoms[0:1, own], atoms[1:2, own], atoms[2:3, own]
        sum_x = sum_y = sum_z = jnp.zeros((8, 128), F32)
        for i in range(4):
            dx = px - repeated[8 * i : 8 * i + 8, own]
            dy = py - repeated[32 + 8 * i : 40 + 8 * i, own]
            dz = pz - repeated[64 + 8 * i : 72 + 8 * i, own]
            other = repeated[96 + 8 * i : 104 + 8 * i, own]
            dist_sq = (dx * dx + dy * dy) + dz * dz
            itself = (lane & 31) == (row + 8 * i)
            dist_sq = jnp.where(itself, 1.0, dist_sq)
            strength = pair_strength(dist_sq) * (other * weight[i : i + 1, own])
            sum_x = sum_x + strength * dx
            sum_y = sum_y + strength * dy
            sum_z = sum_z + strength * dz
        near[0:1, own] = jnp.sum(sum_x, axis=0, keepdims=True)
        near[1:2, own] = jnp.sum(sum_y, axis=0, keepdims=True)
        near[2:3, own] = jnp.sum(sum_z, axis=0, keepdims=True)
    lift = jnp.where(place[0] == N_DOM - 1, float(NX), 0.0)
    upright = jnp.transpose(jnp.concatenate([beyond[...]] * 16, axis=0))
    columns[...] = jnp.zeros((128, 128), F32)
    for c in range(HALO_CLUSTERS):
        part = upright[8 * c : 8 * c + 8]
        hx = part[:, 0:1] + lift
        hy = part[:, 1:2]
        hz = part[:, 2:3]
        hq = part[:, 3:4]
        sum_x = sum_y = sum_z = jnp.zeros((8, 128), F32)
        for tile in range(ATOMS // 128):
            own = slice(128 * tile, 128 * tile + 128)
            dx = atoms[0:1, own] - hx
            dy = atoms[1:2, own] - hy
            dz = atoms[2:3, own] - hz
            dist_sq = (dx * dx + dy * dy) + dz * dz
            both = weight[4 + c : 5 + c, own]
            strength = pair_strength(dist_sq) * both
            on_own = strength * hq
            near[0:1, own] = near[0:1, own] + jnp.sum(on_own * dx, axis=0, keepdims=True)
            near[1:2, own] = near[1:2, own] + jnp.sum(on_own * dy, axis=0, keepdims=True)
            near[2:3, own] = near[2:3, own] + jnp.sum(on_own * dz, axis=0, keepdims=True)
            on_halo = strength * atoms[3:4, own]
            sum_x = sum_x - on_halo * dx
            sum_y = sum_y - on_halo * dy
            sum_z = sum_z - on_halo * dz
        force_x = jnp.sum(sum_x, axis=1, keepdims=True) * hq
        force_y = jnp.sum(sum_y, axis=1, keepdims=True) * hq
        force_z = jnp.sum(sum_z, axis=1, keepdims=True) * hq
        columns[8 * c : 8 * c + 8, :] = jnp.where(
            lane == 0, force_x, jnp.where(lane == 1, force_y, jnp.where(lane == 2, force_z, 0.0))
        )
    halo[...] = jnp.transpose(columns[...])[0:8]
    for f in range(3):
        near[f : f + 1, :] = near[f : f + 1, :] * atoms[3:4, :]


def call(kernel, outs, ins, scratch=(), flops=1_000_000):
    vmem = pl.BlockSpec(memory_space=pltpu.VMEM)
    smem = pl.BlockSpec(memory_space=pltpu.SMEM)
    in_specs = [smem if kind == "s" else vmem for kind, _ in ins]
    many = isinstance(outs, list)
    return pl.pallas_call(
        kernel,
        out_shape=outs,
        in_specs=in_specs,
        out_specs=[vmem] * len(outs) if many else vmem,
        scratch_shapes=list(scratch),
        compiler_params=pltpu.CompilerParams(vmem_limit_bytes=VMEM_LIMIT),
        cost_estimate=pl.CostEstimate(flops=flops, bytes_accessed=1_000_000, transcendentals=0),
    )(*[x for _, x in ins])


def shape(*dims):
    return jax.ShapeDtypeStruct(dims, F32)


def permuted(x, axis, by):
    length = lax.axis_size(axis)
    return lax.ppermute(x, axis, [(i, (i + by) % length) for i in range(length)])


def exchange(x):
    sent = x.reshape(DEVICES, 1, MODES * 128)
    return lax.all_to_all(sent, ("dom", "pme"), 0, 0).reshape(DEVICES * MODES, 128)


def tables():
    along_y, y_waves = real_basis(NY)
    along_x, x_waves = real_basis(NX)
    along_z, z_waves = real_basis(NZ)
    folded = np.zeros((N_DOM * XW, NX))
    for q in range(N_DOM):
        for x in range(XD + 3):
            folded[q * XW + x] = along_x[:, (q * XD + x) % NX]
    order = np.array([4 * p + z for z in range(ZP) for p in range(N_PME)])
    z_rows = np.kron(np.eye(MODES), along_z[:, order])
    y_square, y_factor = wave_factors(y_waves, NY)
    x_square, x_factor = wave_factors(x_waves, NX)
    z_square, z_factor = wave_factors(z_waves, NZ)
    f32 = np.float32
    return {
        "y": halves(along_y),
        "y_back": halves(along_y.T),
        "x": halves(folded),
        "z": halves(z_rows),
        "z_back": halves(z_rows.T),
        "y_square": y_square.astype(f32),
        "y_factor": y_factor.astype(f32),
        "x_square": x_square.astype(f32)[None, :],
        "x_factor": (x_factor / math.pi).astype(f32)[None, :],
        "z_square": np.repeat(z_square.astype(f32)[:, None], 128, axis=1),
        "z_factor": np.repeat(z_factor.astype(f32)[:, None], 128, axis=1),
    }


def make_shards(table):
    def shards(group_column, group_corner, atom_cell, fraction, charge, cluster_pairs):
        slot = jnp.arange(8, dtype=jnp.int32)
        place = jnp.where(slot == 0, lax.axis_index("dom"), lax.axis_index("pme"))
        place = place.astype(jnp.int32)
        column = group_column.reshape(1, GROUPS)
        atoms, edge = call(
            prepare_kernel,
            [shape(8, ATOMS), shape(8, 128)],
            [
                ("s", place), ("v", column), ("v", group_corner), ("v", atom_cell),
                ("v", fraction), ("v", charge.reshape(1, ATOMS)),
            ],
        )
        behind = permuted(atoms, "pme", 1)
        beyond = permuted(edge, "dom", -1)
        ya = (column[0] * YP + group_corner[1]) >> 3
        own_grid = call(
            spread_own_kernel,
            shape(BLOCKS, 8, 128),
            [("s", place), ("s", ya), ("v", atoms)],
            flops=3_000_000_000,
        )
        ya_behind = behind[4, :GROUPS].astype(jnp.int32) >> 3
        spectrum = call(
            spread_rest_kernel,
            shape(NY, 128),
            [
                ("s", place), ("s", ya_behind), ("v", behind), ("v", own_grid),
                ("v", table["y"][0]), ("v", table["y"][1]),
            ],
            scratch=[pltpu.VMEM((BLOCKS, 8, 128), F32)],
        )
        held = exchange(spectrum)
        turned = atoms[:4].reshape(4, GROUPS, 32).transpose(0, 2, 1).reshape(128, GROUPS)
        near, halo = call(
            nonbonded_kernel,
            [shape(3, ATOMS), shape(8, 128)],
            [("s", place), ("v", atoms), ("v", turned), ("v", cluster_pairs), ("v", beyond)],
            scratch=[
                pltpu.VMEM((16, ATOMS), F32),
                pltpu.VMEM((128, ATOMS), F32),
                pltpu.VMEM((128, 128), F32),
            ],
            flops=8_000_000_000,
        )
        halo_back = permuted(halo, "dom", 1)
        filtered = call(
            filter_kernel,
            shape(DEVICES * MODES, 128),
            [
                ("s", place), ("s", table["y_square"]), ("s", table["y_factor"]), ("v", held),
                ("v", table["x"][0]), ("v", table["x"][1]),
                ("v", table["z"][0]), ("v", table["z"][1]),
                ("v", table["z_back"][0]), ("v", table["z_back"][1]),
                ("v", table["x_square"]), ("v", table["x_factor"]),
                ("v", table["z_square"]), ("v", table["z_factor"]),
            ],
            scratch=[pltpu.VMEM((MODES * NZ, N_DOM * XW), F32)],
        )
        returned = exchange(filtered)
        grid, rest = call(
            gather_rest_kernel,
            [shape(BLOCKS, 8, 128), shape(3, ATOMS)],
            [
                ("s", place), ("s", ya_behind), ("v", behind), ("v", returned),
                ("v", table["y_back"][0]), ("v", table["y_back"][1]),
            ],
        )
        rest_back = permuted(rest, "pme", -1)
        forces = call(
            gather_own_kernel,
            shape(3, ATOMS),
            [
                ("s", place), ("s", ya), ("v", atoms), ("v", grid), ("v", near),
                ("v", halo_back),
            ],
            flops=3_000_000_000,
        )
        return forces + rest_back

    return shards


def solution(mesh):
    in_specs = (
        P(("pme", "dom"), None),
        P(None, ("pme", "dom")),
        P(None, ("pme", "dom")),
        P(None, ("pme", "dom")),
        P(("pme", "dom")),
        P(None, ("pme", "dom")),
    )
    out_specs = P(None, ("pme", "dom"))
    return jax.shard_map(
        make_shards(tables()), mesh=mesh, in_specs=in_specs, out_specs=out_specs, check_vma=False
    )
```

profile of v0, /device:TPU:1, one launch (start us, length us, event | category | flops | bytes accessed | tf_op | source)
XLA Modules:
  0.0 81.7 jit_solution(11882530783433842115)
XLA Ops:
  0.0 0.0 copy-start.6
  0.0 0.8 copy-done.6
  0.8 0.0 copy-start.7
  0.8 0.8 copy-done.7
  1.5 0.0 copy-start.14
  1.5 0.7 copy-done.14
  2.2 0.0 copy-start.19
  2.2 0.7 copy-done.19
  2.9 0.0 copy-start.20
  2.9 0.7 copy-done.20
  3.6 0.8 shard_map.208
  4.3 2.5 %collective-permute-start = (f32[8,2048]{1,0:T(8,128)S(1)}, f32[8,2048]{1,0:T(8,128)S(1)}, u32[]{:S(2)}, u32[]{:S(2)}) collective-permute-start(f32[8,2048]{1,0:T(8,128)S(1)} %get-tuple-element.11.atoms), channel_id=1, source_target_pairs={{0,32},{32,64},{64,96},{96,128},{128,160},{160,192},{192,224},{224... | collective-permute-start | bytes 196616 | tf_op jit(solution)/shard_map/ppermute | solution.py:445
  6.9 0.0 copy-start.4
  6.9 0.0 copy-start.5
  6.9 1.8 %shard_map.209.own = f32[98,8,128]{2,1,0:T(8,128)S(1)} custom-call(s32[8]{0:T(128)S(1)} %compare_select_fusion.place, s32[64]{0:T(128)S(1)} %fusion.2.ya, f32[8,2048]{1,0:T(8,128)S(1)} %get-tuple-element.11.atoms), custom_call_target="tpu_custom_call" | custom-call | flops 3000000000 | bytes 1000000 | tf_op jit(solution)/shard_map/pallas_call | solution.py:428
  8.7 3.8 %collective-permute-done.atoms = f32[8,2048]{1,0:T(8,128)S(1)} collective-permute-done((f32[8,2048]{1,0:T(8,128)S(1)}, f32[8,2048]{1,0:T(8,128)S(1)}, u32[]{:S(2)}, u32[]{:S(2)}) %collective-permute-start) | collective-permute-done | bytes 65568 | tf_op jit(solution)/shard_map/ppermute | solution.py:445
  12.5 0.0 copy-done.4
  12.5 0.0 copy-done.5
  12.5 0.0 copy-start
  12.5 0.0 copy-start.1
  12.5 0.0 copy-start.8
  12.5 0.0 copy-start.9
  12.5 0.0 copy-start.10
  12.5 0.0 copy-start.11
  12.6 0.0 copy-start.12
  12.6 0.0 copy-start.13
  12.6 0.0 copy-start.15
  12.6 0.0 copy-start.16
  12.6 0.0 copy-start.17
  12.6 0.0 copy-start.18
  12.6 2.6 %shard_map.210 = f32[768,128]{1,0:T(8,128)S(1)} custom-call(s32[8]{0:T(128)S(1)} %compare_select_fusion.place, s32[64]{0:T(128)S(1)} %fusion.1.ya, f32[8,2048]{1,0:T(8,128)S(1)} %collective-permute-done.atoms, f32[98,8,128]{2,1,0:T(8,128)S(1)} %shard_map.209.own, bf16[768,768]{1,0:T(8,128)(2,1)S(1)} %copy-done.4, bf16[768,768]{1,0:T(8,128)(2,1)S(1)} %copy-done.5), custom_call_target="tpu_custom_call" | custom-call | flops 1000000 | bytes 1000000 | tf_op jit(solution)/shard_map/pallas_call | solution.py:428
  15.2 31.2 %all_to_all.10 = f32[256,1,384]{2,1,0:T(1,128)S(1)} all-to-all(f32[256,1,384]{2,1,0:T(1,128)S(1)} %bitcast.18), channel_id=1, replica_groups=mesh['pme'=8,'dom'=32] {'dom','pme'}, dimensions={0} | all-to-all | bytes 786432 | tf_op jit(solution)/shard_map/all_to_all | solution.py:450
  46.4 0.0 copy-done
  46.4 0.0 copy-done.1
  46.4 0.0 copy-done.8
  46.5 0.0 copy-done.9
  46.5 0.0 copy-done.10
  46.5 0.0 copy-done.11
  46.5 0.0 copy-done.12
  46.5 0.0 copy-done.13
  46.5 0.0 copy-done.15
  46.5 0.0 copy-done.16
  46.5 0.0 copy-done.17
  46.5 0.0 copy-done.18
  46.5 4.8 %shard_map.211 = f32[768,128]{1,0:T(8,128)} custom-call(s32[8]{0:T(128)S(1)} %compare_select_fusion.place, f32[768]{0:T(1024)S(1)} %copy-done.15, f32[768]{0:T(1024)S(1)} %copy-done.16, f32[768,128]{1,0:T(8,128)S(1)} %bitcast.17, bf16[1024,768]{1,0:T(8,128)(2,1)S(1)} %copy-done, bf16[1024,768]{1,0:T(8,128)(2,1)S(1)} %copy-done.1, ...), custom_call_target="tpu_custom_call" | custom-call | flops 1000000 | bytes 1000000 | tf_op jit(solution)/shard_map/pallas_call | solution.py:428
  51.4 0.0 copy-start.21
  51.4 5.9 %all-to-all-start.1 = ((f32[256,1,384]{2,1,0:T(1,128)}), f32[256,1,384]{2,1,0:T(1,128)S(1)}, u32[]{:S(2)}, u32[]{:S(2)}) async-start(f32[256,1,384]{2,1,0:T(1,128)} %bitcast.7), calls=%async_computation.1 | async-start | bytes 786432 | tf_op jit(solution)/shard_map/all_to_all | solution.py:450
  57.3 2.5 %collective-permute-start.1 = (f32[8,128]{1,0:T(8,128)S(1)}, f32[8,128]{1,0:T(8,128)S(1)}, u32[]{:S(2)}, u32[]{:S(2)}) collective-permute-start(f32[8,128]{1,0:T(8,128)S(1)} %get-tuple-element.13), channel_id=1, source_target_pairs={{0,31},{1,0},{2,1},{3,2},{4,3},{5,4},{6,5},{7,6},{8,7},{9,8},{10,9... | collective-permute-start | bytes 12296 | tf_op jit(solution)/shard_map/ppermute | solution.py:445
  59.8 0.1 reshape.35
  59.9 0.1 copy.27
  60.0 0.9 %collective-permute-done.1.beyond = f32[8,128]{1,0:T(8,128)S(1)} collective-permute-done((f32[8,128]{1,0:T(8,128)S(1)}, f32[8,128]{1,0:T(8,128)S(1)}, u32[]{:S(2)}, u32[]{:S(2)}) %collective-permute-start.1) | collective-permute-done | bytes 4128 | tf_op jit(solution)/shard_map/ppermute | solution.py:445
  60.9 0.0 copy-done.21
  60.9 0.0 copy-start.2
  60.9 3.7 %shard_map.213 = (f32[3,2048]{1,0:T(4,128)S(1)}, f32[8,128]{1,0:T(8,128)S(1)}) custom-call(s32[8]{0:T(128)S(1)} %compare_select_fusion.place, f32[8,2048]{1,0:T(8,128)S(1)} %get-tuple-element.11.atoms, f32[128,64]{1,0:T(8,128)S(1)} %bitcast.19, s32[2,1024]{1,0:T(2,128)S(1)} %copy-done.21, f32[8,128]{1,0:T(8,128)S(1)} %collective-permute-done.1.beyond), custom_call_target="tpu_custom_call" | custom-call | flops 8000000000 | bytes 1000000 | tf_op jit(solution)/shard_map/pallas_call | solution.py:428
  64.6 0.1 collective-permute-start.2
  64.7 11.1 %all-to-all-done.1 = f32[256,1,384]{2,1,0:T(1,128)S(1)} async-done(((f32[256,1,384]{2,1,0:T(1,128)}), f32[256,1,384]{2,1,0:T(1,128)S(1)}, u32[]{:S(2)}, u32[]{:S(2)}) %all-to-all-start.1) | async-done | bytes 393248 | tf_op jit(solution)/shard_map/all_to_all | solution.py:450
  75.7 0.0 copy-done.2
  75.7 0.0 copy-done.3
  75.7 2.4 %shard_map.212 = (f32[98,8,128]{2,1,0:T(8,128)S(1)}, f32[3,2048]{1,0:T(4,128)S(1)}) custom-call(s32[8]{0:T(128)S(1)} %compare_select_fusion.place, s32[64]{0:T(128)S(1)} %fusion.1.ya, f32[8,2048]{1,0:T(8,128)S(1)} %collective-permute-done.atoms, f32[768,128]{1,0:T(8,128)S(1)} %bitcast.16, bf16[768,768]{1,0:T(8,128)(2,1)S(1)} %copy-done.2, ...), custom_call_target="tpu_custom_call" | custom-call | flops 1000000 | bytes 1000000 | tf_op jit(solution)/shard_map/pallas_call | solution.py:428
  78.2 0.2 collective-permute-start.3
  78.4 0.0 collective-permute-done.2.halo
  78.4 1.8 %shard_map.214 = f32[3,2048]{1,0:T(4,128)S(1)} custom-call(s32[8]{0:T(128)S(1)} %compare_select_fusion.place, s32[64]{0:T(128)S(1)} %fusion.2.ya, f32[8,2048]{1,0:T(8,128)S(1)} %get-tuple-element.11.atoms, f32[98,8,128]{2,1,0:T(8,128)S(1)} %get-tuple-element.12.grid, f32[3,2048]{1,0:T(4,128)S(1)} %get-tuple-element.14.near, ...), custom_call_target="tpu_custom_call" | custom-call | flops 3000000000 | bytes 1000000 | tf_op jit(solution)/shard_map/pallas_call | solution.py:428
  80.2 0.8 %collective-permute-done.3 = f32[3,2048]{1,0:T(4,128)S(1)} collective-permute-done((f32[3,2048]{1,0:T(4,128)S(1)}, f32[3,2048]{1,0:T(4,128)S(1)}, u32[]{:S(2)}, u32[]{:S(2)}) %collective-permute-start.3) | collective-permute-done | bytes 24608 | tf_op jit(solution)/shard_map/ppermute | solution.py:445
  81.0 0.6 add.7
  (5 shorter events, 0.0 us)
Async XLA Ops:
  0.0 0.8 copy-start.6
  0.8 0.8 copy-start.7
  1.5 0.7 copy-start.14
  2.2 0.7 copy-start.19
  2.9 0.7 copy-start.20
  4.3 8.1 %collective-permute-start = (f32[8,2048]{1,0:T(8,128)S(1)}, f32[8,2048]{1,0:T(8,128)S(1)}, u32[]{:S(2)}, u32[]{:S(2)}) collective-permute-start(f32[8,2048]{1,0:T(8,128)S(1)} %get-tuple-element.11.atoms), channel_id=1, source_target_pairs={{0,32},{32,64},{64,96},{96,128},{128,160},{160,192},{192,224},{224... | collective-permute-start | bytes 196616 | tf_op jit(solution)/shard_map/ppermute | solution.py:445
  6.9 5.6 %copy-start.4 = (bf16[768,768]{1,0:T(8,128)(2,1)S(1)}, bf16[768,768]{1,0:T(8,128)(2,1)}, u32[]{:S(2)}) copy-start(bf16[768,768]{1,0:T(8,128)(2,1)} %constant.47.clone.table_high) | copy-start | bytes 3538948
  6.9 5.6 %copy-start.5 = (bf16[768,768]{1,0:T(8,128)(2,1)S(1)}, bf16[768,768]{1,0:T(8,128)(2,1)}, u32[]{:S(2)}) copy-start(bf16[768,768]{1,0:T(8,128)(2,1)} %constant.48.clone.table_low) | copy-start | bytes 3538948
  12.5 34.0 %copy-start = (bf16[1024,768]{1,0:T(8,128)(2,1)S(1)}, bf16[1024,768]{1,0:T(8,128)(2,1)}, u32[]{:S(2)}) copy-start(bf16[1024,768]{1,0:T(8,128)(2,1)} %constant.51.clone.fx_high) | copy-start | bytes 4718596
  12.5 34.0 %copy-start.1 = (bf16[1024,768]{1,0:T(8,128)(2,1)S(1)}, bf16[1024,768]{1,0:T(8,128)(2,1)}, u32[]{:S(2)}) copy-start(bf16[1024,768]{1,0:T(8,128)(2,1)} %constant.52.clone.fx_low) | copy-start | bytes 4718596
  12.5 33.9 %copy-start.8 = (bf16[96,96]{1,0:T(8,128)(2,1)S(1)}, bf16[96,96]{1,0:T(8,128)(2,1)}, u32[]{:S(2)}) copy-start(bf16[96,96]{1,0:T(8,128)(2,1)} %constant.53.clone.kz_high) | copy-start | bytes 55300
  12.5 33.9 %copy-start.9 = (bf16[96,96]{1,0:T(8,128)(2,1)S(1)}, bf16[96,96]{1,0:T(8,128)(2,1)}, u32[]{:S(2)}) copy-start(bf16[96,96]{1,0:T(8,128)(2,1)} %constant.54.clone.kz_low) | copy-start | bytes 55300
  12.5 33.9 %copy-start.10 = (bf16[96,96]{1,0:T(8,128)(2,1)S(1)}, bf16[96,96]{1,0:T(8,128)(2,1)}, u32[]{:S(2)}) copy-start(bf16[96,96]{1,0:T(8,128)(2,1)} %constant.55.clone.tz_high) | copy-start | bytes 55300
  12.5 33.9 %copy-start.11 = (bf16[96,96]{1,0:T(8,128)(2,1)S(1)}, bf16[96,96]{1,0:T(8,128)(2,1)}, u32[]{:S(2)}) copy-start(bf16[96,96]{1,0:T(8,128)(2,1)} %constant.56.clone.tz_low) | copy-start | bytes 55300
  12.6 33.9 %copy-start.12 = (f32[32,128]{1,0:T(8,128)S(1)}, f32[32,128]{1,0:T(8,128)}, u32[]{:S(2)}) copy-start(f32[32,128]{1,0:T(8,128)} %constant.59.clone.z_square) | copy-start | bytes 49156
  12.6 33.9 %copy-start.13 = (f32[32,128]{1,0:T(8,128)S(1)}, f32[32,128]{1,0:T(8,128)}, u32[]{:S(2)}) copy-start(f32[32,128]{1,0:T(8,128)} %constant.60.clone.z_factor) | copy-start | bytes 49156
  12.6 33.9 %copy-start.15 = (f32[768]{0:T(1024)S(1)}, f32[768]{0:T(1024)}, u32[]{:S(2)}) copy-start(f32[768]{0:T(1024)} %constant.49.clone.y_square) | copy-start | bytes 9220
  12.6 33.9 %copy-start.16 = (f32[768]{0:T(1024)S(1)}, f32[768]{0:T(1024)}, u32[]{:S(2)}) copy-start(f32[768]{0:T(1024)} %constant.50.clone.y_factor) | copy-start | bytes 9220
  12.6 33.9 %copy-start.17 = (f32[1,768]{1,0:T(1,128)S(1)}, f32[1,768]{1,0:T(1,128)}, u32[]{:S(2)}) copy-start(f32[1,768]{1,0:T(1,128)} %constant.57.clone.x_square) | copy-start | bytes 9220
  12.6 33.9 %copy-start.18 = (f32[1,768]{1,0:T(1,128)S(1)}, f32[1,768]{1,0:T(1,128)}, u32[]{:S(2)}) copy-start(f32[1,768]{1,0:T(1,128)} %constant.58.clone.x_factor) | copy-start | bytes 9220
  51.4 9.5 %copy-start.21 = (s32[2,1024]{1,0:T(2,128)S(1)}, s32[2,1024]{1,0:T(2,128)}, u32[]{:S(2)}) copy-start(s32[2,1024]{1,0:T(2,128)} %pairs.1) | copy-start | bytes 24580
  51.4 24.4 %all-to-all-start.1 = ((f32[256,1,384]{2,1,0:T(1,128)}), f32[256,1,384]{2,1,0:T(1,128)S(1)}, u32[]{:S(2)}, u32[]{:S(2)}) async-start(f32[256,1,384]{2,1,0:T(1,128)} %bitcast.7), calls=%async_computation.1 | async-start | bytes 786432 | tf_op jit(solution)/shard_map/all_to_all | solution.py:450
  57.3 3.6 %collective-permute-start.1 = (f32[8,128]{1,0:T(8,128)S(1)}, f32[8,128]{1,0:T(8,128)S(1)}, u32[]{:S(2)}, u32[]{:S(2)}) collective-permute-start(f32[8,128]{1,0:T(8,128)S(1)} %get-tuple-element.13), channel_id=1, source_target_pairs={{0,31},{1,0},{2,1},{3,2},{4,3},{5,4},{6,5},{7,6},{8,7},{9,8},{10,9... | collective-permute-start | bytes 12296 | tf_op jit(solution)/shard_map/ppermute | solution.py:445
  60.9 14.8 %copy-start.2 = (bf16[768,768]{1,0:T(8,128)(2,1)S(1)}, bf16[768,768]{1,0:T(8,128)(2,1)}, u32[]{:S(2)}) copy-start(bf16[768,768]{1,0:T(8,128)(2,1)} %constant.61.clone.table_high) | copy-start | bytes 3538948
  60.9 14.8 %copy-start.3 = (bf16[768,768]{1,0:T(8,128)(2,1)S(1)}, bf16[768,768]{1,0:T(8,128)(2,1)}, u32[]{:S(2)}) copy-start(bf16[768,768]{1,0:T(8,128)(2,1)} %constant.62.clone.table_low) | copy-start | bytes 3538948
  64.6 13.8 %collective-permute-start.2 = (f32[8,128]{1,0:T(8,128)S(1)}, f32[8,128]{1,0:T(8,128)S(1)}, u32[]{:S(2)}, u32[]{:S(2)}) collective-permute-start(f32[8,128]{1,0:T(8,128)S(1)} %get-tuple-element.15), channel_id=1, source_target_pairs={{0,1},{1,2},{2,3},{3,4},{4,5},{5,6},{6,7},{7,8},{8,9},{9,10},{10,1... | collective-permute-start | bytes 12296 | tf_op jit(solution)/shard_map/ppermute | solution.py:445
  78.2 2.8 %collective-permute-start.3 = (f32[3,2048]{1,0:T(4,128)S(1)}, f32[3,2048]{1,0:T(4,128)S(1)}, u32[]{:S(2)}, u32[]{:S(2)}) collective-permute-start(f32[3,2048]{1,0:T(4,128)S(1)} %get-tuple-element.16), channel_id=1, source_target_pairs={{0,224},{32,0},{64,32},{96,64},{128,96},{160,128},{192,160},{224,1... | collective-permute-start | bytes 73736 | tf_op jit(solution)/shard_map/ppermute | solution.py:445
where the time goes:
time: 82.1 us; the launch traced here: 81.7 us
  blocking collectives  31.2 us (38%)
  Pallas kernels  17.8 us (22%)
  waiting for transfers between devices  16.6 us (20%)
  starting transfers between devices  11.3 us (14%)
  local copies, waits for them, and re-layouts  3.83 us (5%)
    all_to_all x1, blocking collectives, exchange(): lax.all_to_all(sent, ('dom', 'pme'), 0, 0).reshape(DEVICES * MODES, 128)  31.2 us
    pallas_call x7, Pallas kernels, call(): pl.pallas_call(kernel, out_shape=outs, in_specs=in_specs, out_specs=[vmem...  17.8 us
    all_to_all x1, waiting for transfers between devices, exchange(): lax.all_to_all(sent, ('dom', 'pme'), 0, 0).reshape(DEVICES * MODES, 128)  11.1 us
    all_to_all x1, starting transfers between devices, exchange(): lax.all_to_all(sent, ('dom', 'pme'), 0, 0).reshape(DEVICES * MODES, 128)  5.88 us
    ppermute x4, waiting for transfers between devices, permuted(): lax.ppermute(x, axis, [(i, (i + by) % length) for i in range(length)])  5.51 us
    ppermute x4, starting transfers between devices, permuted(): lax.ppermute(x, axis, [(i, (i + by) % length) for i in range(length)])  5.41 us
    unnamed x44, local copies, waits for them, and re-layouts  3.64 us
  transfers between devices with their start and end apart: 5, of which 4 were waited for; matrix products, arithmetic and copies ran while one was open for 0% of the time, Pallas kernels for 12%

commit v1 on v0

--- a/solution.py
+++ b/solution.py
@@ -61,7 +61,8 @@
         waves[2 * k] = k
     rows[length - 1] = (1.0 - 2.0 * (point % 2)) / math.sqrt(length)
     waves[length - 1] = length // 2
-    return rows, waves
+    order = np.argsort(waves % 2, kind="stable")
+    return rows[order], waves[order]
 
 
 def wave_factors(waves, length):
@@ -93,6 +94,12 @@
 
 def dot_tn(a, b):
     return lax.dot_general(a, b, (((0,), (0,)), ((), ())), preferred_element_type=F32)
+
+
+def times_table(table_high, table_low, value):
+    high, low = split(value)
+    both = dot(table_high, jnp.concatenate([high, low], axis=1))
+    return both[:, :128] + (both[:, 128:] + dot(table_low, high))
 
 
 def iota(shape, dim):
@@ -119,7 +126,23 @@
     return value, jnp.where(u < 0.0, -slope, slope)
 
 
-def prepare_kernel(place, col, corner, cell, fraction, charge, atoms, edge):
+def prepare_kernel(
+    col_in, corner_in, cell_in, fraction_in, charge_in, atoms, edge,
+    col, corner, cell, fraction, charge, arrived,
+):
+    copies = [
+        pltpu.make_async_copy(source, target, arrived.at[i])
+        for i, (source, target) in enumerate(
+            (
+                (col_in, col), (corner_in, corner), (cell_in, cell),
+                (fraction_in, fraction), (charge_in, charge),
+            )
+        )
+    ]
+    for copy in copies:
+        copy.start()
+    for copy in copies:
+        copy.wait()
     group = iota((GROUPS, ATOMS), 0)
     hot = jnp.where((iota((GROUPS, ATOMS), 1) >> 5) == group, 1.0, 0.0).astype(BF16)
     rep_corner = dot(corner[...].astype(F32).astype(BF16), hot)
@@ -127,8 +150,8 @@
         jnp.broadcast_to(col[...].astype(F32), (8, GROUPS)).astype(BF16), hot
     )[0:1]
     base = rep_corner + cell[...].astype(F32)
-    first = (place[0] * XD).astype(F32)
-    third = (place[1] * ZP).astype(F32)
+    first = (lax.axis_index("dom") * XD).astype(F32)
+    third = (lax.axis_index("pme") * ZP).astype(F32)
     along_x = (base[0:1] + first) + fraction[0:1, :]
     along_y = (base[1:2] + rep_col * float(YP)) + fraction[1:2, :]
     along_z = (base[2:3] + third) + fraction[2:3, :]
@@ -175,36 +198,39 @@
         charged = jnp.concatenate([wx * wz[z : z + 1] for z in range(ZP)], axis=0)
         c_high, c_low = split(charged)
         y_high, y_low = split(wy)
-        added = dot_nt(y_high, c_high) + (dot_nt(y_high, c_low) + dot_nt(y_low, c_high))
+        added = dot_nt(
+            jnp.concatenate([y_high, y_low], axis=1), jnp.concatenate([c_high, c_high], axis=1)
+        ) + dot_nt(y_high, c_low)
         for j in range(4):
             part = added[24 * j : 24 * j + 24].reshape(3, 8, 128)
             grid[pl.ds(starts[j], 3)] = grid[pl.ds(starts[j], 3)] + part
 
 
-def spread_own_kernel(place, ya, atoms, grid):
+def spread_own_kernel(ya, atoms, grid):
     grid[...] = jnp.zeros((BLOCKS, 8, 128), F32)
-    origin_x = (place[0] * XD).astype(F32)
-    origin_z = (place[1] * ZP).astype(F32)
+    origin_x = (lax.axis_index("dom") * XD).astype(F32)
+    origin_z = (lax.axis_index("pme") * ZP).astype(F32)
     spread_batches(origin_x, origin_z, ya, atoms, grid)
 
 
-def neighbour_origin(place):
-    behind = (place[1] + (N_PME - 1)) & (N_PME - 1)
-    return (place[0] * XD).astype(F32), (behind * ZP + ZP).astype(F32)
-
-
-def spread_rest_kernel(place, ya, atoms, own, table_high, table_low, out, grid):
+def neighbour_origin():
+    behind = (lax.axis_index("pme") + (N_PME - 1)) & (N_PME - 1)
+    return (lax.axis_index("dom") * XD).astype(F32), (behind * ZP + ZP).astype(F32)
+
+
+def spread_rest_kernel(ya, atoms, own, even_high, even_low, odd_high, odd_low, out, grid):
     grid[...] = own[...]
-    origin_x, origin_z = neighbour_origin(place)
+    origin_x, origin_z = neighbour_origin()
     spread_batches(origin_x, origin_z, ya, atoms, grid)
     grid[0:2] = grid[0:2] + grid[96:98]
-    g_high, g_low = split(grid[0:96].reshape(NY, 128))
-    both = dot(table_high[...], jnp.concatenate([g_high, g_low], axis=1))
-    out[...] = both[:, :128] + (both[:, 128:] + dot(table_low[...], g_high))
+    lower = grid[0:48].reshape(NY // 2, 128)
+    upper = grid[48:96].reshape(NY // 2, 128)
+    out[0 : NY // 2, :] = times_table(even_high[...], even_low[...], lower + upper)
+    out[NY // 2 :, :] = times_table(odd_high[...], odd_low[...], lower - upper)
 
 
 def filter_kernel(
-    place, y_square, y_factor, held, fx_high, fx_low, kz_high, kz_low, tz_high, tz_low,
+    y_info, held, even_high, even_low, odd_high, odd_low, kz_high, kz_low, tz_high, tz_low,
     x_square, x_factor, z_square, z_factor, out, work,
 ):
     lane = iota((8, 128), 1) >> 5
@@ -219,25 +245,36 @@
                     tile = moved if tile is None else jnp.where(lane == b, moved, tile)
                 row = m * NZ + z * 8
                 work[row : row + 8, 128 * a : 128 * a + 128] = tile
-    x_high, x_low = split(work[...])
-    waves = dot(x_high, fx_high[...]) + (dot(x_low, fx_high[...]) + dot(x_high, fx_low[...]))
-    w_high, w_low = split(waves)
+    rows = MODES * NZ
+    half = N_DOM // 2 * XW
+    lower, upper = work[:, :half], work[:, half:]
+    waves = []
+    for value, high, low in ((lower + upper, even_high, even_low), (lower - upper, odd_high, odd_low)):
+        v_high, v_low = split(value)
+        both = dot(jnp.concatenate([v_high, v_low], axis=0), high[...])
+        waves.append(both[:rows] + (both[rows:] + dot(v_high, low[...])))
+    w_high, w_low = split(jnp.concatenate(waves, axis=1))
     full = dot(kz_high[...], w_high) + (dot(kz_high[...], w_low) + dot(kz_low[...], w_high))
-    device = place[0] * N_PME + place[1]
+    device = lax.axis_index("dom") * N_PME + lax.axis_index("pme")
+    info = y_info[pl.ds(device, 1), :]
     scaled = []
     for m in range(MODES):
-        mode = device * MODES + m
-        square = (x_square[...] + z_square[:, 0:1]) + y_square[mode]
-        factor = (x_factor[...] * z_factor[:, 0:1]) * y_factor[mode]
+        square = (x_square[...] + z_square[:, 0:1]) + info[:, m : m + 1]
+        factor = (x_factor[...] * z_factor[:, 0:1]) * info[:, MODES + m : MODES + m + 1]
         nonzero = jnp.where(square > 0.0, square, 1.0)
         influence = jnp.where(square > 0.0, factor / nonzero, 0.0)
         scaled.append(full[m * NZ : m * NZ + NZ] * influence)
     s_high, s_low = split(jnp.concatenate(scaled, axis=0))
     back = dot(tz_high[...], s_high) + (dot(tz_high[...], s_low) + dot(tz_low[...], s_high))
-    b_high, b_low = split(back)
-    work[...] = dot_nt(b_high, fx_high[...]) + (
-        dot_nt(b_low, fx_high[...]) + dot_nt(b_high, fx_low[...])
-    )
+    parts = []
+    for value, high, low in (
+        (back[:, : NX // 2], even_high, even_low), (back[:, NX // 2 :], odd_high, odd_low),
+    ):
+        v_high, v_low = split(value)
+        both = dot_nt(jnp.concatenate([v_high, v_low], axis=0), high[...])
+        parts.append(both[:rows] + (both[rows:] + dot_nt(v_high, low[...])))
+    work[:, :half] = parts[0] + parts[1]
+    work[:, half:] = parts[0] - parts[1]
     for m in range(MODES):
         for a in range(8):
             tiles = [
@@ -273,7 +310,9 @@
         b_high, b_low = split(block)
         y_both = jnp.concatenate([masked_blocks(wy, lane), masked_blocks(sy, lane)], axis=1)
         y_high, y_low = split(y_both)
-        sampled = dot_tn(b_high, y_high) + (dot_tn(b_low, y_high) + dot_tn(b_high, y_low))
+        sampled = dot_tn(
+            jnp.concatenate([b_high, b_low], axis=0), jnp.concatenate([y_high, y_high], axis=0)
+        ) + dot_tn(b_high, y_low)
         along_x = along_y = along_z = jnp.zeros((XW, 128), F32)
         for z in range(ZP):
             value = sampled[XW * z : XW * z + XW, :128]
@@ -290,13 +329,13 @@
         )
 
 
-def gather_rest_kernel(place, ya, atoms, held, table_high, table_low, grid, out):
-    h_high, h_low = split(held[...])
-    both = dot(table_high[...], jnp.concatenate([h_high, h_low], axis=1))
-    potential = both[:, :128] + (both[:, 128:] + dot(table_low[...], h_high))
-    grid[0:96] = potential.reshape(96, 8, 128)
-    grid[96:98] = potential[0:16].reshape(2, 8, 128)
-    origin_x, origin_z = neighbour_origin(place)
+def gather_rest_kernel(ya, atoms, held, even_high, even_low, odd_high, odd_low, grid, out):
+    even = times_table(even_high[...], even_low[...], held[0 : NY // 2, :])
+    odd = times_table(odd_high[...], odd_low[...], held[NY // 2 :, :])
+    grid[0:48] = (even + odd).reshape(48, 8, 128)
+    grid[48:96] = (even - odd).reshape(48, 8, 128)
+    grid[96:98] = grid[0:2]
+    origin_x, origin_z = neighbour_origin()
 
     def store(own, fx, fy, fz):
         out[0:1, own] = fx
@@ -306,9 +345,9 @@
     gather_batches(origin_x, origin_z, ya, atoms, grid, store)
 
 
-def gather_own_kernel(place, ya, atoms, grid, near, halo, out):
-    origin_x = (place[0] * XD).astype(F32)
-    origin_z = (place[1] * ZP).astype(F32)
+def gather_own_kernel(ya, atoms, grid, near, halo, out):
+    origin_x = (lax.axis_index("dom") * XD).astype(F32)
+    origin_z = (lax.axis_index("pme") * ZP).astype(F32)
 
     def store(own, fx, fy, fz):
         forces = [fx, fy, fz]
@@ -334,7 +373,7 @@
     return fall * bracket * (inverse * inverse)
 
 
-def nonbonded_kernel(place, atoms, turned, pairs, beyond, near, halo, weight, repeated, columns):
+def nonbonded_kernel(atoms, turned, pairs, beyond, near, halo, weight, repeated, columns):
     left = pairs[0:1, :]
     right = pairs[1:2, :]
     inside = right < CLUSTERS
@@ -383,7 +422,7 @@
         near[0:1, own] = jnp.sum(sum_x, axis=0, keepdims=True)
         near[1:2, own] = jnp.sum(sum_y, axis=0, keepdims=True)
         near[2:3, own] = jnp.sum(sum_z, axis=0, keepdims=True)
-    lift = jnp.where(place[0] == N_DOM - 1, float(NX), 0.0)
+    lift = jnp.where(lax.axis_index("dom") == N_DOM - 1, float(NX), 0.0)
     upright = jnp.transpose(jnp.concatenate([beyond[...]] * 16, axis=0))
     columns[...] = jnp.zeros((128, 128), F32)
     for c in range(HALO_CLUSTERS):
@@ -423,7 +462,8 @@
 def call(kernel, outs, ins, scratch=(), flops=1_000_000):
     vmem = pl.BlockSpec(memory_space=pltpu.VMEM)
     smem = pl.BlockSpec(memory_space=pltpu.SMEM)
-    in_specs = [smem if kind == "s" else vmem for kind, _ in ins]
+    spaces = {"s": smem, "v": vmem, "h": pl.BlockSpec(memory_space=pltpu.HBM)}
+    in_specs = [spaces[kind] for kind, _ in ins]
     many = isinstance(outs, list)
     return pl.pallas_call(
         kernel,
@@ -461,17 +501,22 @@
     order = np.array([4 * p + z for z in range(ZP) for p in range(N_PME)])
     z_rows = np.kron(np.eye(MODES), along_z[:, order])
     y_square, y_factor = wave_factors(y_waves, NY)
+    y_info = np.zeros((DEVICES, 128))
+    y_info[:, 0:MODES] = y_square.reshape(DEVICES, MODES)
+    y_info[:, MODES : 2 * MODES] = y_factor.reshape(DEVICES, MODES)
     x_square, x_factor = wave_factors(x_waves, NX)
     z_square, z_factor = wave_factors(z_waves, NZ)
     f32 = np.float32
     return {
-        "y": halves(along_y),
-        "y_back": halves(along_y.T),
-        "x": halves(folded),
+        "y_even": halves(along_y[: NY // 2, : NY // 2]),
+        "y_odd": halves(along_y[NY // 2 :, : NY // 2]),
+        "y_even_back": halves(along_y[: NY // 2, : NY // 2].T),
+        "y_odd_back": halves(along_y[NY // 2 :, : NY // 2].T),
+        "x_even": halves(folded[: N_DOM // 2 * XW, : NX // 2]),
+        "x_odd": halves(folded[: N_DOM // 2 * XW, NX // 2 :]),
         "z": halves(z_rows),
         "z_back": halves(z_rows.T),
-        "y_square": y_square.astype(f32),
-        "y_factor": y_factor.astype(f32),
+        "y_info": y_info.astype(f32),
         "x_square": x_square.astype(f32)[None, :],
         "x_factor": (x_factor / math.pi).astype(f32)[None, :],
         "z_square": np.repeat(z_square.astype(f32)[:, None], 128, axis=1),
@@ -481,16 +526,24 @@
 
 def make_shards(table):
     def shards(group_column, group_corner, atom_cell, fraction, charge, cluster_pairs):
-        slot = jnp.arange(8, dtype=jnp.int32)
-        place = jnp.where(slot == 0, lax.axis_index("dom"), lax.axis_index("pme"))
-        place = place.astype(jnp.int32)
         column = group_column.reshape(1, GROUPS)
         atoms, edge = call(
             prepare_kernel,
             [shape(8, ATOMS), shape(8, 128)],
             [
-                ("s", place), ("v", column), ("v", group_corner), ("v", atom_cell),
-                ("v", fraction), ("v", charge.reshape(1, ATOMS)),
+                ("h", pltpu.with_memory_space_constraint(column, pltpu.HBM)),
+                ("h", pltpu.with_memory_space_constraint(group_corner, pltpu.HBM)),
+                ("h", pltpu.with_memory_space_constraint(atom_cell, pltpu.HBM)),
+                ("h", pltpu.with_memory_space_constraint(fraction, pltpu.HBM)),
+                ("h", pltpu.with_memory_space_constraint(charge.reshape(1, ATOMS), pltpu.HBM)),
+            ],
+            scratch=[
+                pltpu.VMEM((1, GROUPS), jnp.int32),
+                pltpu.VMEM((3, GROUPS), jnp.int32),
+                pltpu.VMEM((3, ATOMS), jnp.int32),
+                pltpu.VMEM((3, ATOMS), F32),
+                pltpu.VMEM((1, ATOMS), F32),
+                pltpu.SemaphoreType.DMA((5,)),
             ],
         )
         behind = permuted(atoms, "pme", 1)
@@ -499,7 +552,7 @@
         own_grid = call(
             spread_own_kernel,
             shape(BLOCKS, 8, 128),
-            [("s", place), ("s", ya), ("v", atoms)],
+            [("s", ya), ("v", atoms)],
             flops=3_000_000_000,
         )
         ya_behind = behind[4, :GROUPS].astype(jnp.int32) >> 3
@@ -507,8 +560,8 @@
             spread_rest_kernel,
             shape(NY, 128),
             [
-                ("s", place), ("s", ya_behind), ("v", behind), ("v", own_grid),
-                ("v", table["y"][0]), ("v", table["y"][1]),
+                ("s", ya_behind), ("v", behind), ("v", own_grid),
+                *[("v", x) for x in table["y_even"] + table["y_odd"]],
             ],
             scratch=[pltpu.VMEM((BLOCKS, 8, 128), F32)],
         )
@@ -517,7 +570,7 @@
         near, halo = call(
             nonbonded_kernel,
             [shape(3, ATOMS), shape(8, 128)],
-            [("s", place), ("v", atoms), ("v", turned), ("v", cluster_pairs), ("v", beyond)],
+            [("v", atoms), ("v", turned), ("v", cluster_pairs), ("v", beyond)],
             scratch=[
                 pltpu.VMEM((16, ATOMS), F32),
                 pltpu.VMEM((128, ATOMS), F32),
@@ -530,8 +583,8 @@
             filter_kernel,
             shape(DEVICES * MODES, 128),
             [
-                ("s", place), ("s", table["y_square"]), ("s", table["y_factor"]), ("v", held),
-                ("v", table["x"][0]), ("v", table["x"][1]),
+                ("v", table["y_info"]), ("v", held),
+                *[("v", x) for x in table["x_even"] + table["x_odd"]],
                 ("v", table["z"][0]), ("v", table["z"][1]),
                 ("v", table["z_back"][0]), ("v", table["z_back"][1]),
                 ("v", table["x_square"]), ("v", table["x_factor"]),
@@ -544,8 +597,8 @@
             gather_rest_kernel,
             [shape(BLOCKS, 8, 128), shape(3, ATOMS)],
             [
-                ("s", place), ("s", ya_behind), ("v", behind), ("v", returned),
-                ("v", table["y_back"][0]), ("v", table["y_back"][1]),
+                ("s", ya_behind), ("v", behind), ("v", returned),
+                *[("v", x) for x in table["y_even_back"] + table["y_odd_back"]],
             ],
         )
         rest_back = permuted(rest, "pme", -1)
@@ -553,7 +606,7 @@
             gather_own_kernel,
             shape(3, ATOMS),
             [
-                ("s", place), ("s", ya), ("v", atoms), ("v", grid), ("v", near),
+                ("s", ya), ("v", atoms), ("v", grid), ("v", near),
                 ("v", halo_back),
             ],
             flops=3_000_000_000,

time: 82.1 us -> 76 us (0.926)
  local copies, waits for them, and re-layouts: 3.83 us -> 0.32 us
  Pallas kernels: 17.8 us -> 14.5 us
    unnamed x44 -> x46, local copies, waits for them, and re-layouts: 3.64 us -> 0.13 us
    pallas_call x7, Pallas kernels: 17.8 us -> 14.5 us  [call(): pl.pallas_call(kernel, out_shape=outs, in_specs=in_specs, out_specs=[vmem...]
  transfers between devices with their start and end apart: 5 -> 5, of which waited for: 4 -> 4; matrix products, arithmetic and copies ran while one was open for 0% -> 1% of each run, Pallas kernels for 12% -> 11%
where the time goes in v1:
time: 76 us; the launch traced here: 75.7 us
  blocking collectives  31.2 us (41%)
  waiting for transfers between devices  16.8 us (22%)
  Pallas kernels  14.5 us (19%)
  starting transfers between devices  11.2 us (15%)
  other arithmetic  1.32 us (2%)
    all_to_all x1, blocking collectives, exchange(): lax.all_to_all(sent, ('dom', 'pme'), 0, 0).reshape(DEVICES * MODES, 128)  31.2 us
    pallas_call x7, Pallas kernels, call(): pl.pallas_call(kernel, out_shape=outs, in_specs=in_specs, out_specs=[vmem...  14.5 us
    all_to_all x1, waiting for transfers between devices, exchange(): lax.all_to_all(sent, ('dom', 'pme'), 0, 0).reshape(DEVICES * MODES, 128)  11.6 us
    all_to_all x1, starting transfers between devices, exchange(): lax.all_to_all(sent, ('dom', 'pme'), 0, 0).reshape(DEVICES * MODES, 128)  5.8 us
    ppermute x4, starting transfers between devices, permuted(): lax.ppermute(x, axis, [(i, (i + by) % length) for i in range(length)])  5.41 us
    ppermute x4, waiting for transfers between devices, permuted(): lax.ppermute(x, axis, [(i, (i + by) % length) for i in range(length)])  5.17 us
  transfers between devices with their start and end apart: 5, of which 4 were waited for; matrix products, arithmetic and copies ran while one was open for 1% of the time, Pallas kernels for 11%

profile of v1, /device:TPU:1, one launch (start us, length us, event | category | flops | bytes accessed | tf_op | source)
XLA Modules:
  0.0 75.7 jit_solution(7689258902914971300)
XLA Ops:
  0.0 1.1 %shard_map.253 = (f32[8,2048]{1,0:T(8,128)S(1)}, f32[8,128]{1,0:T(8,128)S(1)}) custom-call(s32[1,64]{1,0:T(1,128)} %bitcast.22, s32[3,64]{1,0:T(4,128)} %corner_in.1, s32[3,2048]{1,0:T(4,128)} %cell_in.1, f32[3,2048]{1,0:T(4,128)} %fraction_in.1, f32[1,2048]{1,0:T(1,128)} %bitcast.21), custom_call_target="tpu_custom_call" | custom-call | flops 1000000 | bytes 1000000 | tf_op jit(solution)/shard_map/pallas_call | solution.py:468
  1.1 0.0 copy-start.22
  1.1 2.5 %collective-permute-start = (f32[8,2048]{1,0:T(8,128)S(1)}, f32[8,2048]{1,0:T(8,128)S(1)}, u32[]{:S(2)}, u32[]{:S(2)}) collective-permute-start(f32[8,2048]{1,0:T(8,128)S(1)} %get-tuple-element.11.atoms), channel_id=1, source_target_pairs={{0,32},{32,64},{64,96},{96,128},{128,160},{160,192},{192,224},{224... | collective-permute-start | bytes 196616 | tf_op jit(solution)/shard_map/ppermute | solution.py:485
  3.6 0.0 copy-done.22
  3.6 0.7 fusion.2.ya
  4.3 0.0 copy-start.8
  4.3 0.0 copy-start.9
  4.3 0.0 copy-start.10
  4.3 0.0 copy-start.11
  4.3 1.4 %shard_map.254.own = f32[98,8,128]{2,1,0:T(8,128)S(1)} custom-call(s32[64]{0:T(128)S(1)} %fusion.2.ya, f32[8,2048]{1,0:T(8,128)S(1)} %get-tuple-element.11.atoms), custom_call_target="tpu_custom_call" | custom-call | flops 3000000000 | bytes 1000000 | tf_op jit(solution)/shard_map/pallas_call | solution.py:468
  5.8 3.5 %collective-permute-done.atoms = f32[8,2048]{1,0:T(8,128)S(1)} collective-permute-done((f32[8,2048]{1,0:T(8,128)S(1)}, f32[8,2048]{1,0:T(8,128)S(1)}, u32[]{:S(2)}, u32[]{:S(2)}) %collective-permute-start) | collective-permute-done | bytes 65568 | tf_op jit(solution)/shard_map/ppermute | solution.py:485
  9.2 0.0 copy-done.8
  9.2 0.0 copy-done.9
  9.3 0.0 copy-done.10
  9.3 0.0 copy-done.11
  9.3 0.0 copy-start.2
  9.3 0.0 copy-start.3
  9.3 0.0 copy-start.12
  9.3 0.0 copy-start.13
  9.3 0.0 copy-start.14
  9.3 0.0 copy-start.15
  9.3 0.0 copy-start.16
  9.4 0.0 copy-start.17
  9.4 0.0 copy-start.18
  9.4 0.0 copy-start.19
  9.4 0.0 copy-start.20
  9.4 1.9 %shard_map.255 = f32[768,128]{1,0:T(8,128)S(1)} custom-call(s32[64]{0:T(128)S(1)} %fusion.1.ya, f32[8,2048]{1,0:T(8,128)S(1)} %collective-permute-done.atoms, f32[98,8,128]{2,1,0:T(8,128)S(1)} %shard_map.254.own, bf16[384,384]{1,0:T(8,128)(2,1)S(1)} %copy-done.8, bf16[384,384]{1,0:T(8,128)(2,1)S(1)} %copy-done.9, bf16[384,384]{1,0:T(8,128)(2,1)S(1)} %copy-done.10, ...), custom_call_target="tpu_custom_call" | custom-call | flops 1000000 | bytes 1000000 | tf_op jit(solution)/shard_map/pallas_call | solution.py:468
  11.4 0.0 copy-start
  11.4 0.0 copy-start.1
  11.4 31.2 %all_to_all.10 = f32[256,1,384]{2,1,0:T(1,128)S(1)} all-to-all(f32[256,1,384]{2,1,0:T(1,128)S(1)} %bitcast.16), channel_id=1, replica_groups=mesh['pme'=8,'dom'=32] {'dom','pme'}, dimensions={0} | all-to-all | bytes 786432 | tf_op jit(solution)/shard_map/all_to_all | solution.py:490
  42.6 0.0 copy-done.2
  42.6 0.0 copy-done.3
  42.6 0.0 copy-done.12
  42.6 0.0 copy-done.13
  42.6 0.0 copy-done.14
  42.6 0.0 copy-done.15
  42.7 0.0 copy-done.16
  42.7 0.0 copy-done.17
  42.7 0.0 copy-done.18
  42.7 0.0 copy-done.19
  42.7 0.0 copy-done.20
  42.7 0.0 copy-done
  42.7 0.0 copy-done.1
  42.7 3.0 %shard_map.256 = f32[768,128]{1,0:T(8,128)} custom-call(f32[256,128]{1,0:T(8,128)S(1)} %copy-done.12, f32[768,128]{1,0:T(8,128)S(1)} %bitcast.18, bf16[512,384]{1,0:T(8,128)(2,1)S(1)} %copy-done, bf16[512,384]{1,0:T(8,128)(2,1)S(1)} %copy-done.1, bf16[512,384]{1,0:T(8,128)(2,1)S(1)} %copy-done.2, bf16[512,384]{1,0:T(8,128)(2,1)S(1)} %copy-done.3, ...), custom_call_target="tpu_custom_call" | custom-call | flops 1000000 | bytes 1000000 | tf_op jit(solution)/shard_map/pallas_call | solution.py:468
  45.7 5.8 %all-to-all-start.1 = ((f32[256,1,384]{2,1,0:T(1,128)}), f32[256,1,384]{2,1,0:T(1,128)S(1)}, u32[]{:S(2)}, u32[]{:S(2)}) async-start(f32[256,1,384]{2,1,0:T(1,128)} %bitcast.7), calls=%async_computation.1 | async-start | bytes 786432 | tf_op jit(solution)/shard_map/all_to_all | solution.py:490
  51.5 2.4 %collective-permute-start.1 = (f32[8,128]{1,0:T(8,128)S(1)}, f32[8,128]{1,0:T(8,128)S(1)}, u32[]{:S(2)}, u32[]{:S(2)}) collective-permute-start(f32[8,128]{1,0:T(8,128)S(1)} %get-tuple-element.13), channel_id=1, source_target_pairs={{0,31},{1,0},{2,1},{3,2},{4,3},{5,4},{6,5},{7,6},{8,7},{9,8},{10,9... | collective-permute-start | bytes 12296 | tf_op jit(solution)/shard_map/ppermute | solution.py:485
  53.9 0.1 reshape.35
  54.0 0.1 copy.32
  54.1 0.9 %collective-permute-done.1.beyond = f32[8,128]{1,0:T(8,128)S(1)} collective-permute-done((f32[8,128]{1,0:T(8,128)S(1)}, f32[8,128]{1,0:T(8,128)S(1)}, u32[]{:S(2)}, u32[]{:S(2)}) %collective-permute-start.1) | collective-permute-done | bytes 4128 | tf_op jit(solution)/shard_map/ppermute | solution.py:485
  54.9 0.0 copy-done.21
  54.9 0.0 copy-start.7
  55.0 3.2 %shard_map.258 = (f32[3,2048]{1,0:T(4,128)S(1)}, f32[8,128]{1,0:T(8,128)S(1)}) custom-call(f32[8,2048]{1,0:T(8,128)S(1)} %get-tuple-element.11.atoms, f32[128,64]{1,0:T(8,128)S(1)} %bitcast.19, s32[2,1024]{1,0:T(2,128)S(1)} %copy-done.21, f32[8,128]{1,0:T(8,128)S(1)} %collective-permute-done.1.beyond), custom_call_target="tpu_custom_call" | custom-call | flops 8000000000 | bytes 1000000 | tf_op jit(solution)/shard_map/pallas_call | solution.py:468
  58.1 0.3 collective-permute-start.2
  58.4 11.6 %all-to-all-done.1 = f32[256,1,384]{2,1,0:T(1,128)S(1)} async-done(((f32[256,1,384]{2,1,0:T(1,128)}), f32[256,1,384]{2,1,0:T(1,128)S(1)}, u32[]{:S(2)}, u32[]{:S(2)}) %all-to-all-start.1) | async-done | bytes 393248 | tf_op jit(solution)/shard_map/all_to_all | solution.py:490
  70.0 0.0 copy-done.4
  70.0 0.0 copy-done.5
  70.0 0.0 copy-done.6
  70.0 0.0 copy-done.7
  70.0 2.2 %shard_map.257 = (f32[98,8,128]{2,1,0:T(8,128)S(1)}, f32[3,2048]{1,0:T(4,128)S(1)}) custom-call(s32[64]{0:T(128)S(1)} %fusion.1.ya, f32[8,2048]{1,0:T(8,128)S(1)} %collective-permute-done.atoms, f32[768,128]{1,0:T(8,128)S(1)} %bitcast.17, bf16[384,384]{1,0:T(8,128)(2,1)S(1)} %copy-done.4, bf16[384,384]{1,0:T(8,128)(2,1)S(1)} %copy-done.5, ...), custom_call_target="tpu_custom_call" | custom-call | flops 1000000 | bytes 1000000 | tf_op jit(solution)/shard_map/pallas_call | solution.py:468
  72.2 0.2 collective-permute-start.3
  72.5 0.0 collective-permute-done.2.halo
  72.5 1.7 %shard_map.259 = f32[3,2048]{1,0:T(4,128)S(1)} custom-call(s32[64]{0:T(128)S(1)} %fusion.2.ya, f32[8,2048]{1,0:T(8,128)S(1)} %get-tuple-element.11.atoms, f32[98,8,128]{2,1,0:T(8,128)S(1)} %get-tuple-element.12.grid, f32[3,2048]{1,0:T(4,128)S(1)} %get-tuple-element.14.near, f32[8,128]{1,0:T(8,128)S(1)} %collective-permute-done.2.halo), custom_call_target="tpu_custom_call" | custom-call | flops 3000000000 | bytes 1000000 | tf_op jit(solution)/shard_map/pallas_call | solution.py:468
  74.2 0.9 %collective-permute-done.3 = f32[3,2048]{1,0:T(4,128)S(1)} collective-permute-done((f32[3,2048]{1,0:T(4,128)S(1)}, f32[3,2048]{1,0:T(4,128)S(1)}, u32[]{:S(2)}, u32[]{:S(2)}) %collective-permute-start.3) | collective-permute-done | bytes 24608 | tf_op jit(solution)/shard_map/ppermute | solution.py:485
  75.1 0.6 add.7
  (6 shorter events, 0.0 us)
Async XLA Ops:
  1.1 2.6 %copy-start.22 = (s32[64,1]{0,1:T(1,128)S(1)}, s32[64,1]{0,1:T(1,128)}, u32[]{:S(2)}) copy-start(s32[64,1]{0,1:T(1,128)} %param.27) | copy-start | bytes 772
  1.1 8.1 %collective-permute-start = (f32[8,2048]{1,0:T(8,128)S(1)}, f32[8,2048]{1,0:T(8,128)S(1)}, u32[]{:S(2)}, u32[]{:S(2)}) collective-permute-start(f32[8,2048]{1,0:T(8,128)S(1)} %get-tuple-element.11.atoms), channel_id=1, source_target_pairs={{0,32},{32,64},{64,96},{96,128},{128,160},{160,192},{192,224},{224... | collective-permute-start | bytes 196616 | tf_op jit(solution)/shard_map/ppermute | solution.py:485
  4.3 4.9 %copy-start.8 = (bf16[384,384]{1,0:T(8,128)(2,1)S(1)}, bf16[384,384]{1,0:T(8,128)(2,1)}, u32[]{:S(2)}) copy-start(bf16[384,384]{1,0:T(8,128)(2,1)} %constant.46.clone.even_high) | copy-start | bytes 884740
  4.3 4.9 %copy-start.9 = (bf16[384,384]{1,0:T(8,128)(2,1)S(1)}, bf16[384,384]{1,0:T(8,128)(2,1)}, u32[]{:S(2)}) copy-start(bf16[384,384]{1,0:T(8,128)(2,1)} %constant.47.clone.even_low) | copy-start | bytes 884740
  4.3 4.9 %copy-start.10 = (bf16[384,384]{1,0:T(8,128)(2,1)S(1)}, bf16[384,384]{1,0:T(8,128)(2,1)}, u32[]{:S(2)}) copy-start(bf16[384,384]{1,0:T(8,128)(2,1)} %constant.48.clone.odd_high) | copy-start | bytes 884740
  4.3 4.9 %copy-start.11 = (bf16[384,384]{1,0:T(8,128)(2,1)S(1)}, bf16[384,384]{1,0:T(8,128)(2,1)}, u32[]{:S(2)}) copy-start(bf16[384,384]{1,0:T(8,128)(2,1)} %constant.49.clone.odd_low) | copy-start | bytes 884740
  9.3 33.3 %copy-start.2 = (bf16[512,384]{1,0:T(8,128)(2,1)S(1)}, bf16[512,384]{1,0:T(8,128)(2,1)}, u32[]{:S(2)}) copy-start(bf16[512,384]{1,0:T(8,128)(2,1)} %constant.53.clone.odd_high) | copy-start | bytes 1179652
  9.3 33.3 %copy-start.3 = (bf16[512,384]{1,0:T(8,128)(2,1)S(1)}, bf16[512,384]{1,0:T(8,128)(2,1)}, u32[]{:S(2)}) copy-start(bf16[512,384]{1,0:T(8,128)(2,1)} %constant.54.clone.odd_low) | copy-start | bytes 1179652
  9.3 33.3 %copy-start.12 = (f32[256,128]{1,0:T(8,128)S(1)}, f32[256,128]{1,0:T(8,128)}, u32[]{:S(2)}) copy-start(f32[256,128]{1,0:T(8,128)} %constant.50.clone.y_info) | copy-start | bytes 393220
  9.3 33.3 %copy-start.13 = (bf16[96,96]{1,0:T(8,128)(2,1)S(1)}, bf16[96,96]{1,0:T(8,128)(2,1)}, u32[]{:S(2)}) copy-start(bf16[96,96]{1,0:T(8,128)(2,1)} %constant.55.clone.kz_high) | copy-start | bytes 55300
  9.3 33.3 %copy-start.14 = (bf16[96,96]{1,0:T(8,128)(2,1)S(1)}, bf16[96,96]{1,0:T(8,128)(2,1)}, u32[]{:S(2)}) copy-start(bf16[96,96]{1,0:T(8,128)(2,1)} %constant.56.clone.kz_low) | copy-start | bytes 55300
  9.3 33.3 %copy-start.15 = (bf16[96,96]{1,0:T(8,128)(2,1)S(1)}, bf16[96,96]{1,0:T(8,128)(2,1)}, u32[]{:S(2)}) copy-start(bf16[96,96]{1,0:T(8,128)(2,1)} %constant.57.clone.tz_high) | copy-start | bytes 55300
  9.3 33.3 %copy-start.16 = (bf16[96,96]{1,0:T(8,128)(2,1)S(1)}, bf16[96,96]{1,0:T(8,128)(2,1)}, u32[]{:S(2)}) copy-start(bf16[96,96]{1,0:T(8,128)(2,1)} %constant.58.clone.tz_low) | copy-start | bytes 55300
  9.4 33.3 %copy-start.17 = (f32[32,128]{1,0:T(8,128)S(1)}, f32[32,128]{1,0:T(8,128)}, u32[]{:S(2)}) copy-start(f32[32,128]{1,0:T(8,128)} %constant.61.clone.z_square) | copy-start | bytes 49156
  9.4 33.3 %copy-start.18 = (f32[32,128]{1,0:T(8,128)S(1)}, f32[32,128]{1,0:T(8,128)}, u32[]{:S(2)}) copy-start(f32[32,128]{1,0:T(8,128)} %constant.62.clone.z_factor) | copy-start | bytes 49156
  9.4 33.3 %copy-start.19 = (f32[1,768]{1,0:T(1,128)S(1)}, f32[1,768]{1,0:T(1,128)}, u32[]{:S(2)}) copy-start(f32[1,768]{1,0:T(1,128)} %constant.59.clone.x_square) | copy-start | bytes 9220
  9.4 33.3 %copy-start.20 = (f32[1,768]{1,0:T(1,128)S(1)}, f32[1,768]{1,0:T(1,128)}, u32[]{:S(2)}) copy-start(f32[1,768]{1,0:T(1,128)} %constant.60.clone.x_factor) | copy-start | bytes 9220
  11.4 31.3 %copy-start = (bf16[512,384]{1,0:T(8,128)(2,1)S(1)}, bf16[512,384]{1,0:T(8,128)(2,1)}, u32[]{:S(2)}) copy-start(bf16[512,384]{1,0:T(8,128)(2,1)} %constant.51.clone.even_high) | copy-start | bytes 1179652
  11.4 31.3 %copy-start.1 = (bf16[512,384]{1,0:T(8,128)(2,1)S(1)}, bf16[512,384]{1,0:T(8,128)(2,1)}, u32[]{:S(2)}) copy-start(bf16[512,384]{1,0:T(8,128)(2,1)} %constant.52.clone.even_low) | copy-start | bytes 1179652
  45.7 24.3 %all-to-all-start.1 = ((f32[256,1,384]{2,1,0:T(1,128)}), f32[256,1,384]{2,1,0:T(1,128)S(1)}, u32[]{:S(2)}, u32[]{:S(2)}) async-start(f32[256,1,384]{2,1,0:T(1,128)} %bitcast.7), calls=%async_computation.1 | async-start | bytes 786432 | tf_op jit(solution)/shard_map/all_to_all | solution.py:490
  51.5 3.4 %collective-permute-start.1 = (f32[8,128]{1,0:T(8,128)S(1)}, f32[8,128]{1,0:T(8,128)S(1)}, u32[]{:S(2)}, u32[]{:S(2)}) collective-permute-start(f32[8,128]{1,0:T(8,128)S(1)} %get-tuple-element.13), channel_id=1, source_target_pairs={{0,31},{1,0},{2,1},{3,2},{4,3},{5,4},{6,5},{7,6},{8,7},{9,8},{10,9... | collective-permute-start | bytes 12296 | tf_op jit(solution)/shard_map/ppermute | solution.py:485
  54.0 1.0 %copy-start.21 = (s32[2,1024]{1,0:T(2,128)S(1)}, s32[2,1024]{1,0:T(2,128)}, u32[]{:S(2)}) copy-start(s32[2,1024]{1,0:T(2,128)} %pairs.1) | copy-start | bytes 24580
  54.9 15.1 %copy-start.4 = (bf16[384,384]{1,0:T(8,128)(2,1)S(1)}, bf16[384,384]{1,0:T(8,128)(2,1)}, u32[]{:S(2)}) copy-start(bf16[384,384]{1,0:T(8,128)(2,1)} %constant.63.clone.even_high) | copy-start | bytes 884740
  54.9 15.1 %copy-start.5 = (bf16[384,384]{1,0:T(8,128)(2,1)S(1)}, bf16[384,384]{1,0:T(8,128)(2,1)}, u32[]{:S(2)}) copy-start(bf16[384,384]{1,0:T(8,128)(2,1)} %constant.64.clone.even_low) | copy-start | bytes 884740
  54.9 15.1 %copy-start.6 = (bf16[384,384]{1,0:T(8,128)(2,1)S(1)}, bf16[384,384]{1,0:T(8,128)(2,1)}, u32[]{:S(2)}) copy-start(bf16[384,384]{1,0:T(8,128)(2,1)} %constant.65.clone.odd_high) | copy-start | bytes 884740
  54.9 15.1 %copy-start.7 = (bf16[384,384]{1,0:T(8,128)(2,1)S(1)}, bf16[384,384]{1,0:T(8,128)(2,1)}, u32[]{:S(2)}) copy-start(bf16[384,384]{1,0:T(8,128)(2,1)} %constant.66.clone.odd_low) | copy-start | bytes 884740
  58.1 14.4 %collective-permute-start.2 = (f32[8,128]{1,0:T(8,128)S(1)}, f32[8,128]{1,0:T(8,128)S(1)}, u32[]{:S(2)}, u32[]{:S(2)}) collective-permute-start(f32[8,128]{1,0:T(8,128)S(1)} %get-tuple-element.15), channel_id=1, source_target_pairs={{0,1},{1,2},{2,3},{3,4},{4,5},{5,6},{6,7},{7,8},{8,9},{9,10},{10,1... | collective-permute-start | bytes 12296 | tf_op jit(solution)/shard_map/ppermute | solution.py:485
  72.2 2.8 %collective-permute-start.3 = (f32[3,2048]{1,0:T(4,128)S(1)}, f32[3,2048]{1,0:T(4,128)S(1)}, u32[]{:S(2)}, u32[]{:S(2)}) collective-permute-start(f32[3,2048]{1,0:T(4,128)S(1)} %get-tuple-element.16), channel_id=1, source_target_pairs={{0,224},{32,0},{64,32},{96,64},{128,96},{160,128},{192,160},{224,1... | collective-permute-start | bytes 73736 | tf_op jit(solution)/shard_map/ppermute | solution.py:485

commit v2 on v1

--- a/solution.py
+++ b/solution.py
@@ -20,12 +20,15 @@
 ZP = 4
 GROUPS = 64
 ATOMS = 2048
+CARRIED = ATOMS + 128
 PAIRS = 1024
 CLUSTERS = 256
 HALO_CLUSTERS = 8
 HALO_ATOMS = 64
 XW = 32
 MODES = 3
+LOW_Y = 64
+LOW_X = 128
 BLOCKS = 98
 BETA = 0.35
 VMEM_LIMIT = 24 * 1024 * 1024
@@ -76,6 +79,21 @@
     high = table.astype(ml_dtypes.bfloat16)
     low = (table - high.astype(np.float32)).astype(ml_dtypes.bfloat16)
     return high, low
+
+
+def thirds(table, axis):
+    table = table.astype(np.float32)
+    high, middle = halves(table)
+    low = (table - high.astype(np.float32)) - middle.astype(np.float32)
+    return np.concatenate([low.astype(ml_dtypes.bfloat16), high, middle], axis=axis)
+
+
+def finest(value, axis):
+    high = value.astype(BF16)
+    rest = value - high.astype(F32)
+    middle = rest.astype(BF16)
+    low = (rest - middle.astype(F32)).astype(BF16)
+    return jnp.concatenate([high, low, middle], axis=axis)
 
 
 def split(value):
@@ -155,13 +173,13 @@
     along_x = (base[0:1] + first) + fraction[0:1, :]
     along_y = (base[1:2] + rep_col * float(YP)) + fraction[1:2, :]
     along_z = (base[2:3] + third) + fraction[2:3, :]
-    atoms[...] = jnp.zeros((8, ATOMS), F32)
-    atoms[0:1, :] = along_x
-    atoms[1:2, :] = along_y
-    atoms[2:3, :] = along_z
-    atoms[3:4, :] = charge[...]
+    atoms[0:1, 0:ATOMS] = along_x
+    atoms[1:2, 0:ATOMS] = along_y
+    atoms[2:3, 0:ATOMS] = along_z
+    atoms[3:4, 0:ATOMS] = charge[...]
+    atoms[:, ATOMS:] = jnp.zeros((4, 128), F32)
     lowest = (col[...] * YP + corner[1:2, :]).astype(F32)
-    atoms[4:5, 0:GROUPS] = lowest
+    atoms[0:1, ATOMS : ATOMS + GROUPS] = lowest
     edge[...] = atoms[:, 0:128]
 
 
@@ -181,7 +199,7 @@
     )
 
 
-def spread_batches(origin_x, origin_z, ya, atoms, grid):
+def spread_batches(origin_x, origin_z, planes, ya, atoms, grid):
     lane = iota((1, 128), 1)
     step_x = iota((XW, 128), 0).astype(F32)
     step_y = iota((24, 128), 0).astype(F32)
@@ -195,22 +213,23 @@
         wx = spline(step_x - xs)
         wz = spline(step_z - zs) * atoms[3:4, own]
         wy = masked_blocks(spline(step_y - ys), lane)
-        charged = jnp.concatenate([wx * wz[z : z + 1] for z in range(ZP)], axis=0)
+        charged = jnp.concatenate([wx * wz[z : z + 1] for z in range(planes)], axis=0)
         c_high, c_low = split(charged)
         y_high, y_low = split(wy)
         added = dot_nt(
             jnp.concatenate([y_high, y_low], axis=1), jnp.concatenate([c_high, c_high], axis=1)
         ) + dot_nt(y_high, c_low)
         for j in range(4):
-            part = added[24 * j : 24 * j + 24].reshape(3, 8, 128)
-            grid[pl.ds(starts[j], 3)] = grid[pl.ds(starts[j], 3)] + part
+            part = added[24 * j : 24 * j + 24].reshape(3, 8, XW * planes)
+            where = (pl.ds(starts[j], 3), slice(None), slice(0, XW * planes))
+            grid[where] = grid[where] + part
 
 
 def spread_own_kernel(ya, atoms, grid):
     grid[...] = jnp.zeros((BLOCKS, 8, 128), F32)
     origin_x = (lax.axis_index("dom") * XD).astype(F32)
     origin_z = (lax.axis_index("pme") * ZP).astype(F32)
-    spread_batches(origin_x, origin_z, ya, atoms, grid)
+    spread_batches(origin_x, origin_z, ZP, ya, atoms, grid)
 
 
 def neighbour_origin():
@@ -221,7 +240,7 @@
 def spread_rest_kernel(ya, atoms, own, even_high, even_low, odd_high, odd_low, out, grid):
     grid[...] = own[...]
     origin_x, origin_z = neighbour_origin()
-    spread_batches(origin_x, origin_z, ya, atoms, grid)
+    spread_batches(origin_x, origin_z, ZP - 1, ya, atoms, grid)
     grid[0:2] = grid[0:2] + grid[96:98]
     lower = grid[0:48].reshape(NY // 2, 128)
     upper = grid[48:96].reshape(NY // 2, 128)
@@ -230,7 +249,7 @@
 
 
 def filter_kernel(
-    y_info, held, even_high, even_low, odd_high, odd_low, kz_high, kz_low, tz_high, tz_low,
+    y_info, held, even_high, even_low, odd_high, odd_low, even_fine, odd_fine, kz_high, kz_low, tz_high, tz_low, tz_fine,
     x_square, x_factor, z_square, z_factor, out, work,
 ):
     lane = iota((8, 128), 1) >> 5
@@ -264,15 +283,21 @@
         nonzero = jnp.where(square > 0.0, square, 1.0)
         influence = jnp.where(square > 0.0, factor / nonzero, 0.0)
         scaled.append(full[m * NZ : m * NZ + NZ] * influence)
-    s_high, s_low = split(jnp.concatenate(scaled, axis=0))
-    back = dot(tz_high[...], s_high) + (dot(tz_high[...], s_low) + dot(tz_low[...], s_high))
+    scaled = jnp.concatenate(scaled, axis=0)
+    s_high, s_low = split(scaled)
+    back = dot(tz_high[...], s_high) + (
+        dot(tz_high[...], s_low)
+        + (dot(tz_low[...], s_high) + dot(tz_fine[...], finest(scaled, 0)))
+    )
     parts = []
-    for value, high, low in (
-        (back[:, : NX // 2], even_high, even_low), (back[:, NX // 2 :], odd_high, odd_low),
+    for value, high, low, fine in (
+        (back[:, : NX // 2], even_high, even_low, even_fine),
+        (back[:, NX // 2 :], odd_high, odd_low, odd_fine),
     ):
         v_high, v_low = split(value)
         both = dot_nt(jnp.concatenate([v_high, v_low], axis=0), high[...])
-        parts.append(both[:rows] + (both[rows:] + dot_nt(v_high, low[...])))
+        small = dot_nt(v_high, low[...]) + dot_nt(finest(value[:, :LOW_X], 1), fine[...])
+        parts.append(both[:rows] + (both[rows:] + small))
     work[:, :half] = parts[0] + parts[1]
     work[:, half:] = parts[0] - parts[1]
     for m in range(MODES):
@@ -290,7 +315,7 @@
                 out[pl.ds((4 * a + b) * 24 + m, 8, stride=3), :] = block
 
 
-def gather_batches(origin_x, origin_z, ya, atoms, grid, store):
+def gather_batches(origin_x, origin_z, planes, ya, atoms, grid, store):
     lane = iota((1, 128), 1)
     step_x = iota((XW, 128), 0).astype(F32)
     step_y = iota((24, 128), 0).astype(F32)
@@ -304,34 +329,47 @@
         wx, sx = weights_of(step_x - xs)
         wy, sy = weights_of(step_y - ys)
         wz, sz = weights_of(step_z - zs)
-        block = jnp.concatenate(
-            [grid[pl.ds(starts[j], 3)].reshape(24, 128) for j in range(4)], axis=0
-        )
-        b_high, b_low = split(block)
+        blocks = []
+        level = jnp.zeros((1, 128), F32)
+        for j in range(4):
+            block = grid[pl.ds(starts[j], 3)].reshape(24, 128)
+            middle = block[8:9, 44:45]
+            level = jnp.where((lane >> 5) == j, middle, level)
+            blocks.append((block - middle)[:, : XW * planes])
+        b_high, b_low = split(jnp.concatenate(blocks, axis=0))
         y_both = jnp.concatenate([masked_blocks(wy, lane), masked_blocks(sy, lane)], axis=1)
         y_high, y_low = split(y_both)
         sampled = dot_tn(
             jnp.concatenate([b_high, b_low], axis=0), jnp.concatenate([y_high, y_high], axis=0)
         ) + dot_tn(b_high, y_low)
         along_x = along_y = along_z = jnp.zeros((XW, 128), F32)
-        for z in range(ZP):
+        for z in range(planes):
             value = sampled[XW * z : XW * z + XW, :128]
             slope = sampled[XW * z : XW * z + XW, 128:]
             along_x = along_x + value * wz[z : z + 1]
             along_y = along_y + slope * wz[z : z + 1]
             along_z = along_z + value * sz[z : z + 1]
         minus = -atoms[3:4, own]
+        kept = sz[0:1]
+        for z in range(1, planes):
+            kept = kept + sz[z : z + 1]
         store(
             own,
             minus * jnp.sum(along_x * sx, axis=0, keepdims=True),
             minus * jnp.sum(along_y * wx, axis=0, keepdims=True),
-            minus * jnp.sum(along_z * wx, axis=0, keepdims=True),
-        )
-
-
-def gather_rest_kernel(ya, atoms, held, even_high, even_low, odd_high, odd_low, grid, out):
-    even = times_table(even_high[...], even_low[...], held[0 : NY // 2, :])
-    odd = times_table(odd_high[...], odd_low[...], held[NY // 2 :, :])
+            minus * (jnp.sum(along_z * wx, axis=0, keepdims=True) + level * kept),
+        )
+
+
+def gather_rest_kernel(
+    ya, atoms, held, even_high, even_low, even_fine, odd_high, odd_low, odd_fine, grid, out
+):
+    even = times_table(even_high[...], even_low[...], held[0 : NY // 2, :]) + dot(
+        even_fine[...], finest(held[0:LOW_Y, :], 0)
+    )
+    odd = times_table(odd_high[...], odd_low[...], held[NY // 2 :, :]) + dot(
+        odd_fine[...], finest(held[NY // 2 : NY // 2 + LOW_Y, :], 0)
+    )
     grid[0:48] = (even + odd).reshape(48, 8, 128)
     grid[48:96] = (even - odd).reshape(48, 8, 128)
     grid[96:98] = grid[0:2]
@@ -342,7 +380,7 @@
         out[1:2, own] = fy
         out[2:3, own] = fz
 
-    gather_batches(origin_x, origin_z, ya, atoms, grid, store)
+    gather_batches(origin_x, origin_z, ZP - 1, ya, atoms, grid, store)
 
 
 def gather_own_kernel(ya, atoms, grid, near, halo, out):
@@ -357,7 +395,7 @@
                 total = total + halo[f : f + 1, :]
             out[f : f + 1, own] = total
 
-    gather_batches(origin_x, origin_z, ya, atoms, grid, store)
+    gather_batches(origin_x, origin_z, ZP, ya, atoms, grid, store)
 
 
 def pair_strength(dist_sq):
@@ -423,7 +461,7 @@
         near[1:2, own] = jnp.sum(sum_y, axis=0, keepdims=True)
         near[2:3, own] = jnp.sum(sum_z, axis=0, keepdims=True)
     lift = jnp.where(lax.axis_index("dom") == N_DOM - 1, float(NX), 0.0)
-    upright = jnp.transpose(jnp.concatenate([beyond[...]] * 16, axis=0))
+    upright = jnp.transpose(jnp.concatenate([beyond[...]] * 32, axis=0))
     columns[...] = jnp.zeros((128, 128), F32)
     for c in range(HALO_CLUSTERS):
         part = upright[8 * c : 8 * c + 8]
@@ -456,7 +494,7 @@
         )
     halo[...] = jnp.transpose(columns[...])[0:8]
     for f in range(3):
-        near[f : f + 1, :] = near[f : f + 1, :] * atoms[3:4, :]
+        near[f : f + 1, :] = near[f : f + 1, :] * atoms[3:4, 0:ATOMS]
 
 
 def call(kernel, outs, ins, scratch=(), flops=1_000_000):
@@ -507,15 +545,19 @@
     x_square, x_factor = wave_factors(x_waves, NX)
     z_square, z_factor = wave_factors(z_waves, NZ)
     f32 = np.float32
+
+    def back(table, low):
+        return (*halves(table), thirds(table[:, :low], 1))
+
     return {
         "y_even": halves(along_y[: NY // 2, : NY // 2]),
         "y_odd": halves(along_y[NY // 2 :, : NY // 2]),
-        "y_even_back": halves(along_y[: NY // 2, : NY // 2].T),
-        "y_odd_back": halves(along_y[NY // 2 :, : NY // 2].T),
-        "x_even": halves(folded[: N_DOM // 2 * XW, : NX // 2]),
-        "x_odd": halves(folded[: N_DOM // 2 * XW, NX // 2 :]),
+        "y_even_back": back(along_y[: NY // 2, : NY // 2].T, LOW_Y),
+        "y_odd_back": back(along_y[NY // 2 :, : NY // 2].T, LOW_Y),
+        "x_even": back(folded[: N_DOM // 2 * XW, : NX // 2], LOW_X),
+        "x_odd": back(folded[: N_DOM // 2 * XW, NX // 2 :], LOW_X),
         "z": halves(z_rows),
-        "z_back": halves(z_rows.T),
+        "z_back": back(z_rows.T, MODES * NZ),
         "y_info": y_info.astype(f32),
         "x_square": x_square.astype(f32)[None, :],
         "x_factor": (x_factor / math.pi).astype(f32)[None, :],
@@ -529,7 +571,7 @@
         column = group_column.reshape(1, GROUPS)
         atoms, edge = call(
             prepare_kernel,
-            [shape(8, ATOMS), shape(8, 128)],
+            [shape(4, CARRIED), shape(4, 128)],
             [
                 ("h", pltpu.with_memory_space_constraint(column, pltpu.HBM)),
                 ("h", pltpu.with_memory_space_constraint(group_corner, pltpu.HBM)),
@@ -555,7 +597,7 @@
             [("s", ya), ("v", atoms)],
             flops=3_000_000_000,
         )
-        ya_behind = behind[4, :GROUPS].astype(jnp.int32) >> 3
+        ya_behind = behind[0, ATOMS : ATOMS + GROUPS].astype(jnp.int32) >> 3
         spectrum = call(
             spread_rest_kernel,
             shape(NY, 128),
@@ -566,7 +608,7 @@
             scratch=[pltpu.VMEM((BLOCKS, 8, 128), F32)],
         )
         held = exchange(spectrum)
-        turned = atoms[:4].reshape(4, GROUPS, 32).transpose(0, 2, 1).reshape(128, GROUPS)
+        turned = atoms[:, :ATOMS].reshape(4, GROUPS, 32).transpose(0, 2, 1).reshape(128, GROUPS)
         near, halo = call(
             nonbonded_kernel,
             [shape(3, ATOMS), shape(8, 128)],
@@ -584,9 +626,9 @@
             shape(DEVICES * MODES, 128),
             [
                 ("v", table["y_info"]), ("v", held),
-                *[("v", x) for x in table["x_even"] + table["x_odd"]],
-                ("v", table["z"][0]), ("v", table["z"][1]),
-                ("v", table["z_back"][0]), ("v", table["z_back"][1]),
+                *[("v", x) for x in table["x_even"][:2] + table["x_odd"][:2]],
+                ("v", table["x_even"][2]), ("v", table["x_odd"][2]),
+                *[("v", x) for x in table["z"] + table["z_back"]],
                 ("v", table["x_square"]), ("v", table["x_factor"]),
                 ("v", table["z_square"]), ("v", table["z_factor"]),
             ],

time: 76 us -> 76.3 us (level)
  Pallas kernels: 14.5 us -> 15.3 us
    pallas_call x7, Pallas kernels: 14.5 us -> 15.3 us  [call(): pl.pallas_call(kernel, out_shape=outs, in_specs=in_specs, out_specs=[vmem...]
  transfers between devices with their start and end apart: 5 -> 5, of which waited for: 4 -> 4; matrix products, arithmetic and copies ran while one was open for 1% -> 1% of each run, Pallas kernels for 11% -> 12%
where the time goes in v2:
time: 76.3 us; the launch traced here: 76.1 us
  blocking collectives  31.2 us (41%)
  waiting for transfers between devices  16.3 us (21%)
  Pallas kernels  15.3 us (20%)
  starting transfers between devices  11.1 us (15%)
  other arithmetic  1.32 us (2%)
    all_to_all x1, blocking collectives, exchange(): lax.all_to_all(sent, ('dom', 'pme'), 0, 0).reshape(DEVICES * MODES, 128)  31.2 us
    pallas_call x7, Pallas kernels, call(): pl.pallas_call(kernel, out_shape=outs, in_specs=in_specs, out_specs=[vmem...  15.3 us
    all_to_all x1, waiting for transfers between devices, exchange(): lax.all_to_all(sent, ('dom', 'pme'), 0, 0).reshape(DEVICES * MODES, 128)  11.6 us
    all_to_all x1, starting transfers between devices, exchange(): lax.all_to_all(sent, ('dom', 'pme'), 0, 0).reshape(DEVICES * MODES, 128)  5.78 us
    ppermute x4, starting transfers between devices, permuted(): lax.ppermute(x, axis, [(i, (i + by) % length) for i in range(length)])  5.36 us
    ppermute x4, waiting for transfers between devices, permuted(): lax.ppermute(x, axis, [(i, (i + by) % length) for i in range(length)])  4.73 us
  transfers between devices with their start and end apart: 5, of which 4 were waited for; matrix products, arithmetic and copies ran while one was open for 1% of the time, Pallas kernels for 12%

profile of v2, /device:TPU:1, one launch (start us, length us, event | category | flops | bytes accessed | tf_op | source)
XLA Modules:
  0.0 76.1 jit_solution(1256054895378791123)
XLA Ops:
  0.0 1.1 %shard_map.298 = (f32[4,2176]{1,0:T(4,128)S(1)}, f32[4,128]{1,0:T(4,128)S(1)}) custom-call(s32[1,64]{1,0:T(1,128)} %bitcast.22, s32[3,64]{1,0:T(4,128)} %corner_in.1, s32[3,2048]{1,0:T(4,128)} %cell_in.1, f32[3,2048]{1,0:T(4,128)} %fraction_in.1, f32[1,2048]{1,0:T(1,128)} %bitcast.21), custom_call_target="tpu_custom_call" | custom-call | flops 1000000 | bytes 1000000 | tf_op jit(solution)/shard_map/pallas_call | solution.py:506
  1.1 0.0 copy-start.27
  1.1 2.5 %collective-permute-start = (f32[4,2176]{1,0:T(4,128)S(1)}, f32[4,2176]{1,0:T(4,128)S(1)}, u32[]{:S(2)}, u32[]{:S(2)}) collective-permute-start(f32[4,2176]{1,0:T(4,128)S(1)} %get-tuple-element.11.atoms), channel_id=1, source_target_pairs={{0,32},{32,64},{64,96},{96,128},{128,160},{160,192},{192,224},{224... | collective-permute-start | bytes 104456 | tf_op jit(solution)/shard_map/ppermute | solution.py:523
  3.6 0.0 copy-done.27
  3.6 0.7 fusion.2.ya
  4.3 0.0 copy-start.13
  4.3 1.4 %shard_map.299.own = f32[98,8,128]{2,1,0:T(8,128)S(1)} custom-call(s32[64]{0:T(128)S(1)} %fusion.2.ya, f32[4,2176]{1,0:T(4,128)S(1)} %get-tuple-element.11.atoms), custom_call_target="tpu_custom_call" | custom-call | flops 3000000000 | bytes 1000000 | tf_op jit(solution)/shard_map/pallas_call | solution.py:506
  5.8 3.1 %collective-permute-done.atoms = f32[4,2176]{1,0:T(4,128)S(1)} collective-permute-done((f32[4,2176]{1,0:T(4,128)S(1)}, f32[4,2176]{1,0:T(4,128)S(1)}, u32[]{:S(2)}, u32[]{:S(2)}) %collective-permute-start) | collective-permute-done | bytes 34848 | tf_op jit(solution)/shard_map/ppermute | solution.py:523
  8.9 0.0 copy-done.10
  8.9 0.0 copy-done.11
  8.9 0.0 copy-done.12
  8.9 0.0 copy-done.13
  8.9 0.0 copy-start.2
  8.9 0.0 copy-start.3
  9.0 0.0 copy-start.4
  9.0 0.0 copy-start.5
  9.0 0.0 copy-start.16
  9.0 0.0 copy-start.17
  9.0 0.0 copy-start.18
  9.0 0.0 copy-start.19
  9.0 0.0 copy-start.20
  9.0 0.0 copy-start.21
  9.1 0.0 copy-start.22
  9.1 0.0 copy-start.23
  9.1 0.0 copy-start.24
  9.1 0.0 copy-start.25
  9.1 1.9 %shard_map.300 = f32[768,128]{1,0:T(8,128)S(1)} custom-call(s32[64]{0:T(128)S(1)} %fusion.1.ya, f32[4,2176]{1,0:T(4,128)S(1)} %collective-permute-done.atoms, f32[98,8,128]{2,1,0:T(8,128)S(1)} %shard_map.299.own, bf16[384,384]{1,0:T(8,128)(2,1)S(1)} %copy-done.10, bf16[384,384]{1,0:T(8,128)(2,1)S(1)} %copy-done.11, bf16[384,384]{1,0:T(8,128)(2,1)S(1)} %copy-done.12, ...), custom_call_target="tpu_custom_call" | custom-call | flops 1000000 | bytes 1000000 | tf_op jit(solution)/shard_map/pallas_call | solution.py:506
  11.0 0.0 copy-start
  11.0 0.0 copy-start.1
  11.0 31.2 %all_to_all.10 = f32[256,1,384]{2,1,0:T(1,128)S(1)} all-to-all(f32[256,1,384]{2,1,0:T(1,128)S(1)} %bitcast.18), channel_id=1, replica_groups=mesh['pme'=8,'dom'=32] {'dom','pme'}, dimensions={0} | all-to-all | bytes 786432 | tf_op jit(solution)/shard_map/all_to_all | solution.py:528
  42.3 0.0 copy-done.2
  42.3 0.0 copy-done.3
  42.3 0.0 copy-done.4
  42.3 0.0 copy-done.5
  42.3 0.0 copy-done.16
  42.3 0.0 copy-done.17
  42.3 0.0 copy-done.18
  42.3 0.0 copy-done.19
  42.3 0.0 copy-done.20
  42.3 0.0 copy-done.21
  42.3 0.0 copy-done.22
  42.3 0.0 copy-done.23
  42.4 3.4 %shard_map.301 = f32[768,128]{1,0:T(8,128)} custom-call(f32[256,128]{1,0:T(8,128)S(1)} %copy-done.16, f32[768,128]{1,0:T(8,128)S(1)} %bitcast.16, bf16[512,384]{1,0:T(8,128)(2,1)S(1)} %copy-done, bf16[512,384]{1,0:T(8,128)(2,1)S(1)} %copy-done.1, bf16[512,384]{1,0:T(8,128)(2,1)S(1)} %copy-done.2, bf16[512,384]{1,0:T(8,128)(2,1)S(1)} %copy-done.3, ...), custom_call_target="tpu_custom_call" | custom-call | flops 1000000 | bytes 1000000 | tf_op jit(solution)/shard_map/pallas_call | solution.py:506
  45.7 5.8 %all-to-all-start.1 = ((f32[256,1,384]{2,1,0:T(1,128)}), f32[256,1,384]{2,1,0:T(1,128)S(1)}, u32[]{:S(2)}, u32[]{:S(2)}) async-start(f32[256,1,384]{2,1,0:T(1,128)} %bitcast.7), calls=%async_computation.1 | async-start | bytes 786432 | tf_op jit(solution)/shard_map/all_to_all | solution.py:528
  51.5 2.4 %collective-permute-start.1 = (f32[4,128]{1,0:T(4,128)S(1)}, f32[4,128]{1,0:T(4,128)S(1)}, u32[]{:S(2)}, u32[]{:S(2)}) collective-permute-start(f32[4,128]{1,0:T(4,128)S(1)} %get-tuple-element.13), channel_id=1, source_target_pairs={{0,31},{1,0},{2,1},{3,2},{4,3},{5,4},{6,5},{7,6},{8,7},{9,8},{10,9... | collective-permute-start | bytes 6152 | tf_op jit(solution)/shard_map/ppermute | solution.py:523
  53.9 0.1 reshape.35
  54.0 0.1 copy.37
  54.1 0.8 %collective-permute-done.1.beyond = f32[4,128]{1,0:T(4,128)S(1)} collective-permute-done((f32[4,128]{1,0:T(4,128)S(1)}, f32[4,128]{1,0:T(4,128)S(1)}, u32[]{:S(2)}, u32[]{:S(2)}) %collective-permute-start.1) | collective-permute-done | bytes 2080 | tf_op jit(solution)/shard_map/ppermute | solution.py:523
  54.9 0.0 copy-start.9
  55.0 0.0 copy-start.14
  55.0 0.0 copy-start.15
  55.0 3.2 %shard_map.303 = (f32[3,2048]{1,0:T(4,128)S(1)}, f32[8,128]{1,0:T(8,128)S(1)}) custom-call(f32[4,2176]{1,0:T(4,128)S(1)} %get-tuple-element.11.atoms, f32[128,64]{1,0:T(8,128)S(1)} %bitcast.19, s32[2,1024]{1,0:T(2,128)S(1)} %copy-done.26, f32[4,128]{1,0:T(4,128)S(1)} %collective-permute-done.1.beyond), custom_call_target="tpu_custom_call" | custom-call | flops 8000000000 | bytes 1000000 | tf_op jit(solution)/shard_map/pallas_call | solution.py:506
  58.2 0.3 collective-permute-start.2
  58.4 11.6 %all-to-all-done.1 = f32[256,1,384]{2,1,0:T(1,128)S(1)} async-done(((f32[256,1,384]{2,1,0:T(1,128)}), f32[256,1,384]{2,1,0:T(1,128)S(1)}, u32[]{:S(2)}, u32[]{:S(2)}) %all-to-all-start.1) | async-done | bytes 393248 | tf_op jit(solution)/shard_map/all_to_all | solution.py:528
  70.0 0.0 copy-done.8
  70.0 0.0 copy-done.9
  70.0 0.0 copy-done.14
  70.1 0.0 copy-done.15
  70.1 2.5 %shard_map.302 = (f32[98,8,128]{2,1,0:T(8,128)S(1)}, f32[3,2048]{1,0:T(4,128)S(1)}) custom-call(s32[64]{0:T(128)S(1)} %fusion.1.ya, f32[4,2176]{1,0:T(4,128)S(1)} %collective-permute-done.atoms, f32[768,128]{1,0:T(8,128)S(1)} %bitcast.17, bf16[384,384]{1,0:T(8,128)(2,1)S(1)} %copy-done.6, bf16[384,384]{1,0:T(8,128)(2,1)S(1)} %copy-done.7, ...), custom_call_target="tpu_custom_call" | custom-call | flops 1000000 | bytes 1000000 | tf_op jit(solution)/shard_map/pallas_call | solution.py:506
  72.6 0.2 collective-permute-start.3
  72.8 0.0 collective-permute-done.2.halo
  72.8 1.9 %shard_map.304 = f32[3,2048]{1,0:T(4,128)S(1)} custom-call(s32[64]{0:T(128)S(1)} %fusion.2.ya, f32[4,2176]{1,0:T(4,128)S(1)} %get-tuple-element.11.atoms, f32[98,8,128]{2,1,0:T(8,128)S(1)} %get-tuple-element.12.grid, f32[3,2048]{1,0:T(4,128)S(1)} %get-tuple-element.14.near, f32[8,128]{1,0:T(8,128)S(1)} %collective-permute-done.2.halo), custom_call_target="tpu_custom_call" | custom-call | flops 3000000000 | bytes 1000000 | tf_op jit(solution)/shard_map/pallas_call | solution.py:506
  74.7 0.7 collective-permute-done.3
  75.4 0.6 add.7
  (16 shorter events, 0.0 us)
Async XLA Ops:
  1.1 2.6 %copy-start.27 = (s32[64,1]{0,1:T(1,128)S(1)}, s32[64,1]{0,1:T(1,128)}, u32[]{:S(2)}) copy-start(s32[64,1]{0,1:T(1,128)} %param.32) | copy-start | bytes 772
  1.1 7.8 %collective-permute-start = (f32[4,2176]{1,0:T(4,128)S(1)}, f32[4,2176]{1,0:T(4,128)S(1)}, u32[]{:S(2)}, u32[]{:S(2)}) collective-permute-start(f32[4,2176]{1,0:T(4,128)S(1)} %get-tuple-element.11.atoms), channel_id=1, source_target_pairs={{0,32},{32,64},{64,96},{96,128},{128,160},{160,192},{192,224},{224... | collective-permute-start | bytes 104456 | tf_op jit(solution)/shard_map/ppermute | solution.py:523
  4.3 4.6 %copy-start.10 = (bf16[384,384]{1,0:T(8,128)(2,1)S(1)}, bf16[384,384]{1,0:T(8,128)(2,1)}, u32[]{:S(2)}) copy-start(bf16[384,384]{1,0:T(8,128)(2,1)} %constant.56.clone.even_high) | copy-start | bytes 884740
  4.3 4.6 %copy-start.11 = (bf16[384,384]{1,0:T(8,128)(2,1)S(1)}, bf16[384,384]{1,0:T(8,128)(2,1)}, u32[]{:S(2)}) copy-start(bf16[384,384]{1,0:T(8,128)(2,1)} %constant.57.clone.even_low) | copy-start | bytes 884740
  4.3 4.6 %copy-start.12 = (bf16[384,384]{1,0:T(8,128)(2,1)S(1)}, bf16[384,384]{1,0:T(8,128)(2,1)}, u32[]{:S(2)}) copy-start(bf16[384,384]{1,0:T(8,128)(2,1)} %constant.58.clone.odd_high) | copy-start | bytes 884740
  4.3 4.6 %copy-start.13 = (bf16[384,384]{1,0:T(8,128)(2,1)S(1)}, bf16[384,384]{1,0:T(8,128)(2,1)}, u32[]{:S(2)}) copy-start(bf16[384,384]{1,0:T(8,128)(2,1)} %constant.59.clone.odd_low) | copy-start | bytes 884740
  8.9 33.3 %copy-start.2 = (bf16[512,384]{1,0:T(8,128)(2,1)S(1)}, bf16[512,384]{1,0:T(8,128)(2,1)}, u32[]{:S(2)}) copy-start(bf16[512,384]{1,0:T(8,128)(2,1)} %constant.63.clone.odd_high) | copy-start | bytes 1179652
  8.9 33.3 %copy-start.3 = (bf16[512,384]{1,0:T(8,128)(2,1)S(1)}, bf16[512,384]{1,0:T(8,128)(2,1)}, u32[]{:S(2)}) copy-start(bf16[512,384]{1,0:T(8,128)(2,1)} %constant.64.clone.odd_low) | copy-start | bytes 1179652
  9.0 33.3 %copy-start.4 = (bf16[512,384]{1,0:T(8,128)(2,1)S(1)}, bf16[512,384]{1,0:T(8,128)(2,1)}, u32[]{:S(2)}) copy-start(bf16[512,384]{1,0:T(8,128)(2,1)} %constant.65.clone.even_fine) | copy-start | bytes 1179652
  9.0 33.3 %copy-start.5 = (bf16[512,384]{1,0:T(8,128)(2,1)S(1)}, bf16[512,384]{1,0:T(8,128)(2,1)}, u32[]{:S(2)}) copy-start(bf16[512,384]{1,0:T(8,128)(2,1)} %constant.66.clone.odd_fine) | copy-start | bytes 1179652
  9.0 33.3 %copy-start.16 = (f32[256,128]{1,0:T(8,128)S(1)}, f32[256,128]{1,0:T(8,128)}, u32[]{:S(2)}) copy-start(f32[256,128]{1,0:T(8,128)} %constant.60.clone.y_info) | copy-start | bytes 393220
  9.0 33.3 %copy-start.17 = (bf16[96,288]{1,0:T(8,128)(2,1)S(1)}, bf16[96,288]{1,0:T(8,128)(2,1)}, u32[]{:S(2)}) copy-start(bf16[96,288]{1,0:T(8,128)(2,1)} %constant.71.clone.tz_fine) | copy-start | bytes 165892
  9.0 33.3 %copy-start.18 = (bf16[96,96]{1,0:T(8,128)(2,1)S(1)}, bf16[96,96]{1,0:T(8,128)(2,1)}, u32[]{:S(2)}) copy-start(bf16[96,96]{1,0:T(8,128)(2,1)} %constant.67.clone.kz_high) | copy-start | bytes 55300
  9.0 33.3 %copy-start.19 = (bf16[96,96]{1,0:T(8,128)(2,1)S(1)}, bf16[96,96]{1,0:T(8,128)(2,1)}, u32[]{:S(2)}) copy-start(bf16[96,96]{1,0:T(8,128)(2,1)} %constant.68.clone.kz_low) | copy-start | bytes 55300
  9.0 33.3 %copy-start.20 = (bf16[96,96]{1,0:T(8,128)(2,1)S(1)}, bf16[96,96]{1,0:T(8,128)(2,1)}, u32[]{:S(2)}) copy-start(bf16[96,96]{1,0:T(8,128)(2,1)} %constant.69.clone.tz_high) | copy-start | bytes 55300
  9.0 33.3 %copy-start.21 = (bf16[96,96]{1,0:T(8,128)(2,1)S(1)}, bf16[96,96]{1,0:T(8,128)(2,1)}, u32[]{:S(2)}) copy-start(bf16[96,96]{1,0:T(8,128)(2,1)} %constant.70.clone.tz_low) | copy-start | bytes 55300
  9.1 33.3 %copy-start.22 = (f32[32,128]{1,0:T(8,128)S(1)}, f32[32,128]{1,0:T(8,128)}, u32[]{:S(2)}) copy-start(f32[32,128]{1,0:T(8,128)} %constant.74.clone.z_square) | copy-start | bytes 49156
  9.1 33.3 %copy-start.23 = (f32[32,128]{1,0:T(8,128)S(1)}, f32[32,128]{1,0:T(8,128)}, u32[]{:S(2)}) copy-start(f32[32,128]{1,0:T(8,128)} %constant.75.clone.z_factor) | copy-start | bytes 49156
  9.1 33.3 %copy-start.24 = (f32[1,768]{1,0:T(1,128)S(1)}, f32[1,768]{1,0:T(1,128)}, u32[]{:S(2)}) copy-start(f32[1,768]{1,0:T(1,128)} %constant.72.clone.x_square) | copy-start | bytes 9220
  9.1 33.3 %copy-start.25 = (f32[1,768]{1,0:T(1,128)S(1)}, f32[1,768]{1,0:T(1,128)}, u32[]{:S(2)}) copy-start(f32[1,768]{1,0:T(1,128)} %constant.73.clone.x_factor) | copy-start | bytes 9220
  11.0 31.4 %copy-start = (bf16[512,384]{1,0:T(8,128)(2,1)S(1)}, bf16[512,384]{1,0:T(8,128)(2,1)}, u32[]{:S(2)}) copy-start(bf16[512,384]{1,0:T(8,128)(2,1)} %constant.61.clone.even_high) | copy-start | bytes 1179652
  11.0 31.4 %copy-start.1 = (bf16[512,384]{1,0:T(8,128)(2,1)S(1)}, bf16[512,384]{1,0:T(8,128)(2,1)}, u32[]{:S(2)}) copy-start(bf16[512,384]{1,0:T(8,128)(2,1)} %constant.62.clone.even_low) | copy-start | bytes 1179652
  45.7 24.3 %all-to-all-start.1 = ((f32[256,1,384]{2,1,0:T(1,128)}), f32[256,1,384]{2,1,0:T(1,128)S(1)}, u32[]{:S(2)}, u32[]{:S(2)}) async-start(f32[256,1,384]{2,1,0:T(1,128)} %bitcast.7), calls=%async_computation.1 | async-start | bytes 786432 | tf_op jit(solution)/shard_map/all_to_all | solution.py:528
  51.5 3.4 %collective-permute-start.1 = (f32[4,128]{1,0:T(4,128)S(1)}, f32[4,128]{1,0:T(4,128)S(1)}, u32[]{:S(2)}, u32[]{:S(2)}) collective-permute-start(f32[4,128]{1,0:T(4,128)S(1)} %get-tuple-element.13), channel_id=1, source_target_pairs={{0,31},{1,0},{2,1},{3,2},{4,3},{5,4},{6,5},{7,6},{8,7},{9,8},{10,9... | collective-permute-start | bytes 6152 | tf_op jit(solution)/shard_map/ppermute | solution.py:523
  54.0 0.9 %copy-start.26 = (s32[2,1024]{1,0:T(2,128)S(1)}, s32[2,1024]{1,0:T(2,128)}, u32[]{:S(2)}) copy-start(s32[2,1024]{1,0:T(2,128)} %pairs.1) | copy-start | bytes 24580
  54.9 15.1 %copy-start.6 = (bf16[384,384]{1,0:T(8,128)(2,1)S(1)}, bf16[384,384]{1,0:T(8,128)(2,1)}, u32[]{:S(2)}) copy-start(bf16[384,384]{1,0:T(8,128)(2,1)} %constant.76.clone.even_high) | copy-start | bytes 884740
  54.9 15.1 %copy-start.7 = (bf16[384,384]{1,0:T(8,128)(2,1)S(1)}, bf16[384,384]{1,0:T(8,128)(2,1)}, u32[]{:S(2)}) copy-start(bf16[384,384]{1,0:T(8,128)(2,1)} %constant.77.clone.even_low) | copy-start | bytes 884740
  54.9 15.1 %copy-start.8 = (bf16[384,384]{1,0:T(8,128)(2,1)S(1)}, bf16[384,384]{1,0:T(8,128)(2,1)}, u32[]{:S(2)}) copy-start(bf16[384,384]{1,0:T(8,128)(2,1)} %constant.79.clone.odd_high) | copy-start | bytes 884740
  54.9 15.1 %copy-start.9 = (bf16[384,384]{1,0:T(8,128)(2,1)S(1)}, bf16[384,384]{1,0:T(8,128)(2,1)}, u32[]{:S(2)}) copy-start(bf16[384,384]{1,0:T(8,128)(2,1)} %constant.80.clone.odd_low) | copy-start | bytes 884740
  55.0 15.1 %copy-start.14 = (bf16[384,192]{1,0:T(8,128)(2,1)S(1)}, bf16[384,192]{1,0:T(8,128)(2,1)}, u32[]{:S(2)}) copy-start(bf16[384,192]{1,0:T(8,128)(2,1)} %constant.78.clone.even_fine) | copy-start | bytes 442372
  55.0 15.1 %copy-start.15 = (bf16[384,192]{1,0:T(8,128)(2,1)S(1)}, bf16[384,192]{1,0:T(8,128)(2,1)}, u32[]{:S(2)}) copy-start(bf16[384,192]{1,0:T(8,128)(2,1)} %constant.81.clone.odd_fine) | copy-start | bytes 442372
  58.2 14.6 %collective-permute-start.2 = (f32[8,128]{1,0:T(8,128)S(1)}, f32[8,128]{1,0:T(8,128)S(1)}, u32[]{:S(2)}, u32[]{:S(2)}) collective-permute-start(f32[8,128]{1,0:T(8,128)S(1)} %get-tuple-element.15), channel_id=1, source_target_pairs={{0,1},{1,2},{2,3},{3,4},{4,5},{5,6},{6,7},{7,8},{8,9},{9,10},{10,1... | collective-permute-start | bytes 12296 | tf_op jit(solution)/shard_map/ppermute | solution.py:523
  72.6 2.8 %collective-permute-start.3 = (f32[3,2048]{1,0:T(4,128)S(1)}, f32[3,2048]{1,0:T(4,128)S(1)}, u32[]{:S(2)}, u32[]{:S(2)}) collective-permute-start(f32[3,2048]{1,0:T(4,128)S(1)} %get-tuple-element.16), channel_id=1, source_target_pairs={{0,224},{32,0},{64,32},{96,64},{128,96},{160,128},{192,160},{224,1... | collective-permute-start | bytes 73736 | tf_op jit(solution)/shard_map/ppermute | solution.py:523

commit v3 on v2

--- a/solution.py
+++ b/solution.py
@@ -29,7 +29,8 @@
 MODES = 3
 LOW_Y = 64
 LOW_X = 128
-BLOCKS = 98
+ROWS = NY + 16
+SPAN = 16
 BETA = 0.35
 VMEM_LIMIT = 24 * 1024 * 1024
 
@@ -183,14 +184,14 @@
     edge[...] = atoms[:, 0:128]
 
 
-def y_blocks(ya, batch, lane):
+def y_starts(ya, batch, lane):
     starts = [ya[4 * batch + j] for j in range(4)]
     row = jnp.where(
         lane < 64,
         jnp.where(lane < 32, starts[0], starts[1]),
         jnp.where(lane < 96, starts[2], starts[3]),
     )
-    return starts, (row * 8).astype(F32)
+    return starts, row.astype(F32)
 
 
 def masked_blocks(weights, lane):
@@ -202,11 +203,11 @@
 def spread_batches(origin_x, origin_z, planes, ya, atoms, grid):
     lane = iota((1, 128), 1)
     step_x = iota((XW, 128), 0).astype(F32)
-    step_y = iota((24, 128), 0).astype(F32)
+    step_y = iota((SPAN, 128), 0).astype(F32)
     step_z = iota((8, 128), 0).astype(F32)
     for batch in range(ATOMS // 128):
         own = slice(128 * batch, 128 * batch + 128)
-        starts, base_y = y_blocks(ya, batch, lane)
+        starts, base_y = y_starts(ya, batch, lane)
         xs = (atoms[0:1, own] - origin_x) + 1.0
         ys = (atoms[1:2, own] - base_y) + 1.0
         zs = (atoms[2:3, own] - origin_z) + 1.0
@@ -220,13 +221,12 @@
             jnp.concatenate([y_high, y_low], axis=1), jnp.concatenate([c_high, c_high], axis=1)
         ) + dot_nt(y_high, c_low)
         for j in range(4):
-            part = added[24 * j : 24 * j + 24].reshape(3, 8, XW * planes)
-            where = (pl.ds(starts[j], 3), slice(None), slice(0, XW * planes))
-            grid[where] = grid[where] + part
+            where = (pl.ds(starts[j], SPAN), slice(0, XW * planes))
+            grid[where] = grid[where] + added[SPAN * j : SPAN * j + SPAN]
 
 
 def spread_own_kernel(ya, atoms, grid):
-    grid[...] = jnp.zeros((BLOCKS, 8, 128), F32)
+    grid[...] = jnp.zeros((ROWS, 128), F32)
     origin_x = (lax.axis_index("dom") * XD).astype(F32)
     origin_z = (lax.axis_index("pme") * ZP).astype(F32)
     spread_batches(origin_x, origin_z, ZP, ya, atoms, grid)
@@ -241,9 +241,9 @@
     grid[...] = own[...]
     origin_x, origin_z = neighbour_origin()
     spread_batches(origin_x, origin_z, ZP - 1, ya, atoms, grid)
-    grid[0:2] = grid[0:2] + grid[96:98]
-    lower = grid[0:48].reshape(NY // 2, 128)
-    upper = grid[48:96].reshape(NY // 2, 128)
+    grid[0:16, :] = grid[0:16, :] + grid[NY:ROWS, :]
+    lower = grid[0 : NY // 2, :]
+    upper = grid[NY // 2 : NY, :]
     out[0 : NY // 2, :] = times_table(even_high[...], even_low[...], lower + upper)
     out[NY // 2 :, :] = times_table(odd_high[...], odd_low[...], lower - upper)
 
@@ -255,7 +255,9 @@
     lane = iota((8, 128), 1) >> 5
     for m in range(MODES):
         for a in range(8):
-            blocks = [held[pl.ds((4 * a + b) * 24 + m, 8, stride=3), :] for b in range(4)]
+            blocks = [
+                held[pl.ds((4 * a + b) * MODES + m, 8, stride=N_DOM * MODES), :] for b in range(4)
+            ]
             for z in range(ZP):
                 tile = None
                 for b in range(4):
@@ -274,7 +276,7 @@
         waves.append(both[:rows] + (both[rows:] + dot(v_high, low[...])))
     w_high, w_low = split(jnp.concatenate(waves, axis=1))
     full = dot(kz_high[...], w_high) + (dot(kz_high[...], w_low) + dot(kz_low[...], w_high))
-    device = lax.axis_index("dom") * N_PME + lax.axis_index("pme")
+    device = lax.axis_index("pme") * N_DOM + lax.axis_index("dom")
     info = y_info[pl.ds(device, 1), :]
     scaled = []
     for m in range(MODES):
@@ -312,17 +314,17 @@
                     shift = (32 * (z - b)) % 128
                     moved = tiles[z] if shift == 0 else pltpu.roll(tiles[z], shift, 1)
                     block = moved if block is None else jnp.where(lane == z, moved, block)
-                out[pl.ds((4 * a + b) * 24 + m, 8, stride=3), :] = block
+                out[pl.ds((4 * a + b) * MODES + m, 8, stride=N_DOM * MODES), :] = block
 
 
 def gather_batches(origin_x, origin_z, planes, ya, atoms, grid, store):
     lane = iota((1, 128), 1)
     step_x = iota((XW, 128), 0).astype(F32)
-    step_y = iota((24, 128), 0).astype(F32)
+    step_y = iota((SPAN, 128), 0).astype(F32)
     step_z = iota((8, 128), 0).astype(F32)
     for batch in range(ATOMS // 128):
         own = slice(128 * batch, 128 * batch + 128)
-        starts, base_y = y_blocks(ya, batch, lane)
+        starts, base_y = y_starts(ya, batch, lane)
         xs = (atoms[0:1, own] - origin_x) + 1.0
         ys = (atoms[1:2, own] - base_y) + 1.0
         zs = (atoms[2:3, own] - origin_z) + 1.0
@@ -332,7 +334,7 @@
         blocks = []
         level = jnp.zeros((1, 128), F32)
         for j in range(4):
-            block = grid[pl.ds(starts[j], 3)].reshape(24, 128)
+            block = grid[pl.ds(starts[j], SPAN), :]
             middle = block[8:9, 44:45]
             level = jnp.where((lane >> 5) == j, middle, level)
             blocks.append((block - middle)[:, : XW * planes])
@@ -340,8 +342,9 @@
         y_both = jnp.concatenate([masked_blocks(wy, lane), masked_blocks(sy, lane)], axis=1)
         y_high, y_low = split(y_both)
         sampled = dot_tn(
-            jnp.concatenate([b_high, b_low], axis=0), jnp.concatenate([y_high, y_high], axis=0)
-        ) + dot_tn(b_high, y_low)
+            jnp.concatenate([b_high, b_low, b_high], axis=0),
+            jnp.concatenate([y_high, y_high, y_low], axis=0),
+        )
         along_x = along_y = along_z = jnp.zeros((XW, 128), F32)
         for z in range(planes):
             value = sampled[XW * z : XW * z + XW, :128]
@@ -370,9 +373,9 @@
     odd = times_table(odd_high[...], odd_low[...], held[NY // 2 :, :]) + dot(
         odd_fine[...], finest(held[NY // 2 : NY // 2 + LOW_Y, :], 0)
     )
-    grid[0:48] = (even + odd).reshape(48, 8, 128)
-    grid[48:96] = (even - odd).reshape(48, 8, 128)
-    grid[96:98] = grid[0:2]
+    grid[0 : NY // 2, :] = even + odd
+    grid[NY // 2 : NY, :] = even - odd
+    grid[NY:ROWS, :] = (even + odd)[0:16]
     origin_x, origin_z = neighbour_origin()
 
     def store(own, fx, fy, fz):
@@ -525,7 +528,7 @@
 
 def exchange(x):
     sent = x.reshape(DEVICES, 1, MODES * 128)
-    return lax.all_to_all(sent, ("dom", "pme"), 0, 0).reshape(DEVICES * MODES, 128)
+    return lax.all_to_all(sent, ("pme", "dom"), 0, 0).reshape(DEVICES * MODES, 128)
 
 
 def tables():
@@ -590,14 +593,14 @@
         )
         behind = permuted(atoms, "pme", 1)
         beyond = permuted(edge, "dom", -1)
-        ya = (column[0] * YP + group_corner[1]) >> 3
+        ya = column[0] * YP + group_corner[1]
         own_grid = call(
             spread_own_kernel,
-            shape(BLOCKS, 8, 128),
+            shape(ROWS, 128),
             [("s", ya), ("v", atoms)],
             flops=3_000_000_000,
         )
-        ya_behind = behind[0, ATOMS : ATOMS + GROUPS].astype(jnp.int32) >> 3
+        ya_behind = behind[0, ATOMS : ATOMS + GROUPS].astype(jnp.int32)
         spectrum = call(
             spread_rest_kernel,
             shape(NY, 128),
@@ -605,7 +608,7 @@
                 ("s", ya_behind), ("v", behind), ("v", own_grid),
                 *[("v", x) for x in table["y_even"] + table["y_odd"]],
             ],
-            scratch=[pltpu.VMEM((BLOCKS, 8, 128), F32)],
+            scratch=[pltpu.VMEM((ROWS, 128), F32)],
         )
         held = exchange(spectrum)
         turned = atoms[:, :ATOMS].reshape(4, GROUPS, 32).transpose(0, 2, 1).reshape(128, GROUPS)
@@ -637,7 +640,7 @@
         returned = exchange(filtered)
         grid, rest = call(
             gather_rest_kernel,
-            [shape(BLOCKS, 8, 128), shape(3, ATOMS)],
+            [shape(ROWS, 128), shape(3, ATOMS)],
             [
                 ("s", ya_behind), ("v", behind), ("v", returned),
                 *[("v", x) for x in table["y_even_back"] + table["y_odd_back"]],

time: 76.3 us -> 74.4 us (0.975)
  waiting for transfers between devices: 16.3 us -> 14.4 us
  starting transfers between devices: 11.1 us -> 12.8 us
  blocking collectives: 31.2 us -> 30 us
    all_to_all x1, waiting for transfers between devices: 11.6 us -> 10.2 us  [exchange(): lax.all_to_all(sent, ('pme', 'dom'), 0, 0).reshape(DEVICES * MODES, 128)]
    all_to_all x1, blocking collectives: 31.2 us -> 30 us  [exchange(): lax.all_to_all(sent, ('pme', 'dom'), 0, 0).reshape(DEVICES * MODES, 128)]
    ppermute x4, starting transfers between devices: 5.36 us -> 6.56 us  [permuted(): lax.ppermute(x, axis, [(i, (i + by) % length) for i in range(length)])]
  transfers between devices with their start and end apart: 5 -> 5, of which waited for: 4 -> 3; matrix products, arithmetic and copies ran while one was open for 1% -> 1% of each run, Pallas kernels for 12% -> 11%
where the time goes in v3:
time: 74.4 us; the launch traced here: 74 us
  blocking collectives  30 us (40%)
  Pallas kernels  14.8 us (20%)
  waiting for transfers between devices  14.4 us (19%)
  starting transfers between devices  12.8 us (17%)
  other arithmetic  1.31 us (2%)
    all_to_all x1, blocking collectives, exchange(): lax.all_to_all(sent, ('pme', 'dom'), 0, 0).reshape(DEVICES * MODES, 128)  30 us
    pallas_call x7, Pallas kernels, call(): pl.pallas_call(kernel, out_shape=outs, in_specs=in_specs, out_specs=[vmem...  14.8 us
    all_to_all x1, waiting for transfers between devices, exchange(): lax.all_to_all(sent, ('pme', 'dom'), 0, 0).reshape(DEVICES * MODES, 128)  10.2 us
    ppermute x4, starting transfers between devices, permuted(): lax.ppermute(x, axis, [(i, (i + by) % length) for i in range(length)])  6.56 us
    all_to_all x1, starting transfers between devices, exchange(): lax.all_to_all(sent, ('pme', 'dom'), 0, 0).reshape(DEVICES * MODES, 128)  6.21 us
    ppermute x4, waiting for transfers between devices, permuted(): lax.ppermute(x, axis, [(i, (i + by) % length) for i in range(length)])  4.12 us
  transfers between devices with their start and end apart: 5, of which 3 were waited for; matrix products, arithmetic and copies ran while one was open for 1% of the time, Pallas kernels for 11%

profile of v3, /device:TPU:1, one launch (start us, length us, event | category | flops | bytes accessed | tf_op | source)
XLA Modules:
  0.0 74.0 jit_solution(13788067530514867318)
XLA Ops:
  0.0 1.1 %shard_map.298 = (f32[4,2176]{1,0:T(4,128)S(1)}, f32[4,128]{1,0:T(4,128)S(1)}) custom-call(s32[1,64]{1,0:T(1,128)} %bitcast.20, s32[3,64]{1,0:T(4,128)} %corner_in.1, s32[3,2048]{1,0:T(4,128)} %cell_in.1, f32[3,2048]{1,0:T(4,128)} %fraction_in.1, f32[1,2048]{1,0:T(1,128)} %bitcast.19), custom_call_target="tpu_custom_call" | custom-call | flops 1000000 | bytes 1000000 | tf_op jit(solution)/shard_map/pallas_call | solution.py:509
  1.1 0.0 copy-start.27
  1.1 2.5 %collective-permute-start = (f32[4,2176]{1,0:T(4,128)S(1)}, f32[4,2176]{1,0:T(4,128)S(1)}, u32[]{:S(2)}, u32[]{:S(2)}) collective-permute-start(f32[4,2176]{1,0:T(4,128)S(1)} %get-tuple-element.11.atoms), channel_id=1, source_target_pairs={{0,32},{32,64},{64,96},{96,128},{128,160},{160,192},{192,224},{224... | collective-permute-start | bytes 104456 | tf_op jit(solution)/shard_map/ppermute | solution.py:526
  3.6 0.0 copy-done.27
  3.6 0.7 bitcast_add_fusion.ya
  4.3 0.0 copy-start.13
  4.3 1.4 %shard_map.299.own = f32[784,128]{1,0:T(8,128)S(1)} custom-call(s32[64]{0:T(128)S(1)} %bitcast_add_fusion.ya, f32[4,2176]{1,0:T(4,128)S(1)} %get-tuple-element.11.atoms), custom_call_target="tpu_custom_call" | custom-call | flops 3000000000 | bytes 1000000 | tf_op jit(solution)/shard_map/pallas_call | solution.py:509
  5.8 3.1 %collective-permute-done.atoms = f32[4,2176]{1,0:T(4,128)S(1)} collective-permute-done((f32[4,2176]{1,0:T(4,128)S(1)}, f32[4,2176]{1,0:T(4,128)S(1)}, u32[]{:S(2)}, u32[]{:S(2)}) %collective-permute-start) | collective-permute-done | bytes 34848 | tf_op jit(solution)/shard_map/ppermute | solution.py:526
  8.9 0.0 copy-done.10
  8.9 0.0 copy-done.11
  8.9 0.0 copy-done.12
  8.9 0.0 copy-done.13
  8.9 0.0 copy-start.2
  8.9 0.0 copy-start.3
  9.0 0.0 copy-start.4
  9.0 0.0 copy-start.5
  9.0 0.0 copy-start.16
  9.0 0.0 copy-start.17
  9.0 0.0 copy-start.18
  9.0 0.0 copy-start.19
  9.0 0.0 copy-start.20
  9.0 0.0 copy-start.21
  9.1 0.0 copy-start.22
  9.1 0.0 copy-start.23
  9.1 0.0 copy-start.24
  9.1 0.0 copy-start.25
  9.1 1.8 %shard_map.300 = f32[768,128]{1,0:T(8,128)S(1)} custom-call(s32[64]{0:T(128)S(1)} %fusion.ya, f32[4,2176]{1,0:T(4,128)S(1)} %collective-permute-done.atoms, f32[784,128]{1,0:T(8,128)S(1)} %shard_map.299.own, bf16[384,384]{1,0:T(8,128)(2,1)S(1)} %copy-done.10, bf16[384,384]{1,0:T(8,128)(2,1)S(1)} %copy-done.11, bf16[384,384]{1,0:T(8,128)(2,1)S(1)} %copy-done.12, ...), custom_call_target="tpu_custom_call" | custom-call | flops 1000000 | bytes 1000000 | tf_op jit(solution)/shard_map/pallas_call | solution.py:509
  10.9 0.0 copy-start
  11.0 0.0 copy-start.1
  11.0 30.0 %all_to_all.10 = f32[256,1,384]{2,1,0:T(1,128)S(1)} all-to-all(f32[256,1,384]{2,1,0:T(1,128)S(1)} %bitcast.16), channel_id=1, replica_groups=mesh['pme'=8,'dom'=32] {'pme','dom'}, dimensions={0} | all-to-all | bytes 786432 | tf_op jit(solution)/shard_map/all_to_all | solution.py:531
  41.0 0.0 copy-done.2
  41.0 0.0 copy-done.3
  41.0 0.0 copy-done.4
  41.0 0.0 copy-done.5
  41.0 0.0 copy-done.16
  41.0 0.0 copy-done.17
  41.0 0.0 copy-done.18
  41.0 0.0 copy-done.19
  41.1 0.0 copy-done.20
  41.1 0.0 copy-done.21
  41.1 0.0 copy-done.22
  41.1 0.0 copy-done.23
  41.1 0.0 copy-done.24
  41.1 0.0 copy-done.25
  41.1 0.0 copy-done
  41.1 3.5 %shard_map.301 = f32[768,128]{1,0:T(8,128)} custom-call(f32[256,128]{1,0:T(8,128)S(1)} %copy-done.16, f32[768,128]{1,0:T(8,128)S(1)} %bitcast.14, bf16[512,384]{1,0:T(8,128)(2,1)S(1)} %copy-done, bf16[512,384]{1,0:T(8,128)(2,1)S(1)} %copy-done.1, bf16[512,384]{1,0:T(8,128)(2,1)S(1)} %copy-done.2, bf16[512,384]{1,0:T(8,128)(2,1)S(1)} %copy-done.3, ...), custom_call_target="tpu_custom_call" | custom-call | flops 1000000 | bytes 1000000 | tf_op jit(solution)/shard_map/pallas_call | solution.py:509
  44.7 6.2 %all-to-all-start.1 = ((f32[256,1,384]{2,1,0:T(1,128)}), f32[256,1,384]{2,1,0:T(1,128)S(1)}, u32[]{:S(2)}, u32[]{:S(2)}) async-start(f32[256,1,384]{2,1,0:T(1,128)} %bitcast.7), calls=%async_computation.1 | async-start | bytes 786432 | tf_op jit(solution)/shard_map/all_to_all | solution.py:531
  50.9 2.2 %collective-permute-start.1 = (f32[4,128]{1,0:T(4,128)S(1)}, f32[4,128]{1,0:T(4,128)S(1)}, u32[]{:S(2)}, u32[]{:S(2)}) collective-permute-start(f32[4,128]{1,0:T(4,128)S(1)} %get-tuple-element.13), channel_id=1, source_target_pairs={{0,31},{1,0},{2,1},{3,2},{4,3},{5,4},{6,5},{7,6},{8,7},{9,8},{10,9... | collective-permute-start | bytes 6152 | tf_op jit(solution)/shard_map/ppermute | solution.py:526
  53.1 0.1 reshape.33
  53.2 0.1 copy.37
  53.3 1.0 %collective-permute-done.1.beyond = f32[4,128]{1,0:T(4,128)S(1)} collective-permute-done((f32[4,128]{1,0:T(4,128)S(1)}, f32[4,128]{1,0:T(4,128)S(1)}, u32[]{:S(2)}, u32[]{:S(2)}) %collective-permute-start.1) | collective-permute-done | bytes 2080 | tf_op jit(solution)/shard_map/ppermute | solution.py:526
  54.3 0.0 copy-done.26
  54.3 0.0 copy-start.9
  54.3 0.0 copy-start.14
  54.3 0.0 copy-start.15
  54.3 3.2 %shard_map.303 = (f32[3,2048]{1,0:T(4,128)S(1)}, f32[8,128]{1,0:T(8,128)S(1)}) custom-call(f32[4,2176]{1,0:T(4,128)S(1)} %get-tuple-element.11.atoms, f32[128,64]{1,0:T(8,128)S(1)} %bitcast.17, s32[2,1024]{1,0:T(2,128)S(1)} %copy-done.26, f32[4,128]{1,0:T(4,128)S(1)} %collective-permute-done.1.beyond), custom_call_target="tpu_custom_call" | custom-call | flops 8000000000 | bytes 1000000 | tf_op jit(solution)/shard_map/pallas_call | solution.py:509
  57.5 0.3 collective-permute-start.2
  57.8 10.2 %all-to-all-done.1 = f32[256,1,384]{2,1,0:T(1,128)S(1)} async-done(((f32[256,1,384]{2,1,0:T(1,128)}), f32[256,1,384]{2,1,0:T(1,128)S(1)}, u32[]{:S(2)}, u32[]{:S(2)}) %all-to-all-start.1) | async-done | bytes 393248 | tf_op jit(solution)/shard_map/all_to_all | solution.py:531
  68.0 2.2 %shard_map.302 = (f32[784,128]{1,0:T(8,128)S(1)}, f32[3,2048]{1,0:T(4,128)S(1)}) custom-call(s32[64]{0:T(128)S(1)} %fusion.ya, f32[4,2176]{1,0:T(4,128)S(1)} %collective-permute-done.atoms, f32[768,128]{1,0:T(8,128)S(1)} %bitcast.15, bf16[384,384]{1,0:T(8,128)(2,1)S(1)} %copy-done.6, bf16[384,384]{1,0:T(8,128)(2,1)S(1)} %copy-done.7, ...), custom_call_target="tpu_custom_call" | custom-call | flops 1000000 | bytes 1000000 | tf_op jit(solution)/shard_map/pallas_call | solution.py:509
  70.3 1.5 %collective-permute-start.3 = (f32[3,2048]{1,0:T(4,128)S(1)}, f32[3,2048]{1,0:T(4,128)S(1)}, u32[]{:S(2)}, u32[]{:S(2)}) collective-permute-start(f32[3,2048]{1,0:T(4,128)S(1)} %get-tuple-element.16), channel_id=1, source_target_pairs={{0,224},{32,0},{64,32},{96,64},{128,96},{160,128},{192,160},{224,1... | collective-permute-start | bytes 73736 | tf_op jit(solution)/shard_map/ppermute | solution.py:526
  71.8 0.0 collective-permute-done.2.halo
  71.8 1.6 %shard_map.304 = f32[3,2048]{1,0:T(4,128)S(1)} custom-call(s32[64]{0:T(128)S(1)} %bitcast_add_fusion.ya, f32[4,2176]{1,0:T(4,128)S(1)} %get-tuple-element.11.atoms, f32[784,128]{1,0:T(8,128)S(1)} %get-tuple-element.12.grid, f32[3,2048]{1,0:T(4,128)S(1)} %get-tuple-element.14.near, f32[8,128]{1,0:T(8,128)S(1)} %collective-permute-done.2.halo), custom_call_target="tpu_custom_call" | custom-call | flops 3000000000 | bytes 1000000 | tf_op jit(solution)/shard_map/pallas_call | solution.py:509
  73.4 0.0 collective-permute-done.3
  73.4 0.6 add.7
  (16 shorter events, 0.0 us)
Async XLA Ops:
  1.1 2.6 %copy-start.27 = (s32[64,1]{0,1:T(1,128)S(1)}, s32[64,1]{0,1:T(1,128)}, u32[]{:S(2)}) copy-start(s32[64,1]{0,1:T(1,128)} %param.32) | copy-start | bytes 772
  1.1 7.8 %collective-permute-start = (f32[4,2176]{1,0:T(4,128)S(1)}, f32[4,2176]{1,0:T(4,128)S(1)}, u32[]{:S(2)}, u32[]{:S(2)}) collective-permute-start(f32[4,2176]{1,0:T(4,128)S(1)} %get-tuple-element.11.atoms), channel_id=1, source_target_pairs={{0,32},{32,64},{64,96},{96,128},{128,160},{160,192},{192,224},{224... | collective-permute-start | bytes 104456 | tf_op jit(solution)/shard_map/ppermute | solution.py:526
  4.3 4.6 %copy-start.10 = (bf16[384,384]{1,0:T(8,128)(2,1)S(1)}, bf16[384,384]{1,0:T(8,128)(2,1)}, u32[]{:S(2)}) copy-start(bf16[384,384]{1,0:T(8,128)(2,1)} %constant.54.clone.even_high) | copy-start | bytes 884740
  4.3 4.6 %copy-start.11 = (bf16[384,384]{1,0:T(8,128)(2,1)S(1)}, bf16[384,384]{1,0:T(8,128)(2,1)}, u32[]{:S(2)}) copy-start(bf16[384,384]{1,0:T(8,128)(2,1)} %constant.55.clone.even_low) | copy-start | bytes 884740
  4.3 4.6 %copy-start.12 = (bf16[384,384]{1,0:T(8,128)(2,1)S(1)}, bf16[384,384]{1,0:T(8,128)(2,1)}, u32[]{:S(2)}) copy-start(bf16[384,384]{1,0:T(8,128)(2,1)} %constant.56.clone.odd_high) | copy-start | bytes 884740
  4.3 4.6 %copy-start.13 = (bf16[384,384]{1,0:T(8,128)(2,1)S(1)}, bf16[384,384]{1,0:T(8,128)(2,1)}, u32[]{:S(2)}) copy-start(bf16[384,384]{1,0:T(8,128)(2,1)} %constant.57.clone.odd_low) | copy-start | bytes 884740
  8.9 32.1 %copy-start.2 = (bf16[512,384]{1,0:T(8,128)(2,1)S(1)}, bf16[512,384]{1,0:T(8,128)(2,1)}, u32[]{:S(2)}) copy-start(bf16[512,384]{1,0:T(8,128)(2,1)} %constant.61.clone.odd_high) | copy-start | bytes 1179652
  8.9 32.1 %copy-start.3 = (bf16[512,384]{1,0:T(8,128)(2,1)S(1)}, bf16[512,384]{1,0:T(8,128)(2,1)}, u32[]{:S(2)}) copy-start(bf16[512,384]{1,0:T(8,128)(2,1)} %constant.62.clone.odd_low) | copy-start | bytes 1179652
  9.0 32.0 %copy-start.4 = (bf16[512,384]{1,0:T(8,128)(2,1)S(1)}, bf16[512,384]{1,0:T(8,128)(2,1)}, u32[]{:S(2)}) copy-start(bf16[512,384]{1,0:T(8,128)(2,1)} %constant.63.clone.even_fine) | copy-start | bytes 1179652
  9.0 32.0 %copy-start.5 = (bf16[512,384]{1,0:T(8,128)(2,1)S(1)}, bf16[512,384]{1,0:T(8,128)(2,1)}, u32[]{:S(2)}) copy-start(bf16[512,384]{1,0:T(8,128)(2,1)} %constant.64.clone.odd_fine) | copy-start | bytes 1179652
  9.0 32.0 %copy-start.16 = (f32[256,128]{1,0:T(8,128)S(1)}, f32[256,128]{1,0:T(8,128)}, u32[]{:S(2)}) copy-start(f32[256,128]{1,0:T(8,128)} %constant.58.clone.y_info) | copy-start | bytes 393220
  9.0 32.0 %copy-start.17 = (bf16[96,288]{1,0:T(8,128)(2,1)S(1)}, bf16[96,288]{1,0:T(8,128)(2,1)}, u32[]{:S(2)}) copy-start(bf16[96,288]{1,0:T(8,128)(2,1)} %constant.69.clone.tz_fine) | copy-start | bytes 165892
  9.0 32.0 %copy-start.18 = (bf16[96,96]{1,0:T(8,128)(2,1)S(1)}, bf16[96,96]{1,0:T(8,128)(2,1)}, u32[]{:S(2)}) copy-start(bf16[96,96]{1,0:T(8,128)(2,1)} %constant.65.clone.kz_high) | copy-start | bytes 55300
  9.0 32.0 %copy-start.19 = (bf16[96,96]{1,0:T(8,128)(2,1)S(1)}, bf16[96,96]{1,0:T(8,128)(2,1)}, u32[]{:S(2)}) copy-start(bf16[96,96]{1,0:T(8,128)(2,1)} %constant.66.clone.kz_low) | copy-start | bytes 55300
  9.0 32.0 %copy-start.20 = (bf16[96,96]{1,0:T(8,128)(2,1)S(1)}, bf16[96,96]{1,0:T(8,128)(2,1)}, u32[]{:S(2)}) copy-start(bf16[96,96]{1,0:T(8,128)(2,1)} %constant.67.clone.tz_high) | copy-start | bytes 55300
  9.0 32.0 %copy-start.21 = (bf16[96,96]{1,0:T(8,128)(2,1)S(1)}, bf16[96,96]{1,0:T(8,128)(2,1)}, u32[]{:S(2)}) copy-start(bf16[96,96]{1,0:T(8,128)(2,1)} %constant.68.clone.tz_low) | copy-start | bytes 55300
  9.1 32.0 %copy-start.22 = (f32[32,128]{1,0:T(8,128)S(1)}, f32[32,128]{1,0:T(8,128)}, u32[]{:S(2)}) copy-start(f32[32,128]{1,0:T(8,128)} %constant.72.clone.z_square) | copy-start | bytes 49156
  9.1 32.0 %copy-start.23 = (f32[32,128]{1,0:T(8,128)S(1)}, f32[32,128]{1,0:T(8,128)}, u32[]{:S(2)}) copy-start(f32[32,128]{1,0:T(8,128)} %constant.73.clone.z_factor) | copy-start | bytes 49156
  9.1 32.0 %copy-start.24 = (f32[1,768]{1,0:T(1,128)S(1)}, f32[1,768]{1,0:T(1,128)}, u32[]{:S(2)}) copy-start(f32[1,768]{1,0:T(1,128)} %constant.70.clone.x_square) | copy-start | bytes 9220
  9.1 32.0 %copy-start.25 = (f32[1,768]{1,0:T(1,128)S(1)}, f32[1,768]{1,0:T(1,128)}, u32[]{:S(2)}) copy-start(f32[1,768]{1,0:T(1,128)} %constant.71.clone.x_factor) | copy-start | bytes 9220
  10.9 30.2 %copy-start = (bf16[512,384]{1,0:T(8,128)(2,1)S(1)}, bf16[512,384]{1,0:T(8,128)(2,1)}, u32[]{:S(2)}) copy-start(bf16[512,384]{1,0:T(8,128)(2,1)} %constant.59.clone.even_high) | copy-start | bytes 1179652
  11.0 30.2 %copy-start.1 = (bf16[512,384]{1,0:T(8,128)(2,1)S(1)}, bf16[512,384]{1,0:T(8,128)(2,1)}, u32[]{:S(2)}) copy-start(bf16[512,384]{1,0:T(8,128)(2,1)} %constant.60.clone.even_low) | copy-start | bytes 1179652
  44.7 23.3 %all-to-all-start.1 = ((f32[256,1,384]{2,1,0:T(1,128)}), f32[256,1,384]{2,1,0:T(1,128)S(1)}, u32[]{:S(2)}, u32[]{:S(2)}) async-start(f32[256,1,384]{2,1,0:T(1,128)} %bitcast.7), calls=%async_computation.1 | async-start | bytes 786432 | tf_op jit(solution)/shard_map/all_to_all | solution.py:531
  50.9 3.4 %collective-permute-start.1 = (f32[4,128]{1,0:T(4,128)S(1)}, f32[4,128]{1,0:T(4,128)S(1)}, u32[]{:S(2)}, u32[]{:S(2)}) collective-permute-start(f32[4,128]{1,0:T(4,128)S(1)} %get-tuple-element.13), channel_id=1, source_target_pairs={{0,31},{1,0},{2,1},{3,2},{4,3},{5,4},{6,5},{7,6},{8,7},{9,8},{10,9... | collective-permute-start | bytes 6152 | tf_op jit(solution)/shard_map/ppermute | solution.py:526
  53.2 1.1 %copy-start.26 = (s32[2,1024]{1,0:T(2,128)S(1)}, s32[2,1024]{1,0:T(2,128)}, u32[]{:S(2)}) copy-start(s32[2,1024]{1,0:T(2,128)} %pairs.1) | copy-start | bytes 24580
  54.3 13.7 %copy-start.6 = (bf16[384,384]{1,0:T(8,128)(2,1)S(1)}, bf16[384,384]{1,0:T(8,128)(2,1)}, u32[]{:S(2)}) copy-start(bf16[384,384]{1,0:T(8,128)(2,1)} %constant.74.clone.even_high) | copy-start | bytes 884740
  54.3 13.7 %copy-start.7 = (bf16[384,384]{1,0:T(8,128)(2,1)S(1)}, bf16[384,384]{1,0:T(8,128)(2,1)}, u32[]{:S(2)}) copy-start(bf16[384,384]{1,0:T(8,128)(2,1)} %constant.75.clone.even_low) | copy-start | bytes 884740
  54.3 13.7 %copy-start.8 = (bf16[384,384]{1,0:T(8,128)(2,1)S(1)}, bf16[384,384]{1,0:T(8,128)(2,1)}, u32[]{:S(2)}) copy-start(bf16[384,384]{1,0:T(8,128)(2,1)} %constant.77.clone.odd_high) | copy-start | bytes 884740
  54.3 13.7 %copy-start.9 = (bf16[384,384]{1,0:T(8,128)(2,1)S(1)}, bf16[384,384]{1,0:T(8,128)(2,1)}, u32[]{:S(2)}) copy-start(bf16[384,384]{1,0:T(8,128)(2,1)} %constant.78.clone.odd_low) | copy-start | bytes 884740
  54.3 13.7 %copy-start.14 = (bf16[384,192]{1,0:T(8,128)(2,1)S(1)}, bf16[384,192]{1,0:T(8,128)(2,1)}, u32[]{:S(2)}) copy-start(bf16[384,192]{1,0:T(8,128)(2,1)} %constant.76.clone.even_fine) | copy-start | bytes 442372
  54.3 13.7 %copy-start.15 = (bf16[384,192]{1,0:T(8,128)(2,1)S(1)}, bf16[384,192]{1,0:T(8,128)(2,1)}, u32[]{:S(2)}) copy-start(bf16[384,192]{1,0:T(8,128)(2,1)} %constant.79.clone.odd_fine) | copy-start | bytes 442372
  57.5 14.3 %collective-permute-start.2 = (f32[8,128]{1,0:T(8,128)S(1)}, f32[8,128]{1,0:T(8,128)S(1)}, u32[]{:S(2)}, u32[]{:S(2)}) collective-permute-start(f32[8,128]{1,0:T(8,128)S(1)} %get-tuple-element.15), channel_id=1, source_target_pairs={{0,1},{1,2},{2,3},{3,4},{4,5},{5,6},{6,7},{7,8},{8,9},{9,10},{10,1... | collective-permute-start | bytes 12296 | tf_op jit(solution)/shard_map/ppermute | solution.py:526
  70.3 3.1 %collective-permute-start.3 = (f32[3,2048]{1,0:T(4,128)S(1)}, f32[3,2048]{1,0:T(4,128)S(1)}, u32[]{:S(2)}, u32[]{:S(2)}) collective-permute-start(f32[3,2048]{1,0:T(4,128)S(1)} %get-tuple-element.16), channel_id=1, source_target_pairs={{0,224},{32,0},{64,32},{96,64},{128,96},{160,128},{192,160},{224,1... | collective-permute-start | bytes 73736 | tf_op jit(solution)/shard_map/ppermute | solution.py:526

commit v4 on v3

--- a/solution.py
+++ b/solution.py
@@ -218,8 +218,9 @@
         c_high, c_low = split(charged)
         y_high, y_low = split(wy)
         added = dot_nt(
-            jnp.concatenate([y_high, y_low], axis=1), jnp.concatenate([c_high, c_high], axis=1)
-        ) + dot_nt(y_high, c_low)
+            jnp.concatenate([y_high, y_low, y_high], axis=1),
+            jnp.concatenate([c_high, c_high, c_low], axis=1),
+        )
         for j in range(4):
             where = (pl.ds(starts[j], SPAN), slice(0, XW * planes))
             grid[where] = grid[where] + added[SPAN * j : SPAN * j + SPAN]
@@ -249,7 +250,8 @@
 
 
 def filter_kernel(
-    y_info, held, even_high, even_low, odd_high, odd_low, even_fine, odd_fine, kz_high, kz_low, tz_high, tz_low, tz_fine,
+    y_info, held, even_high, even_low, odd_high, odd_low, even_back_high, even_back_low, even_fine,
+    odd_back_high, odd_back_low, odd_fine, kz_high, kz_low, tz_high, tz_low, tz_fine,
     x_square, x_factor, z_square, z_factor, out, work,
 ):
     lane = iota((8, 128), 1) >> 5
@@ -293,12 +295,12 @@
     )
     parts = []
     for value, high, low, fine in (
-        (back[:, : NX // 2], even_high, even_low, even_fine),
-        (back[:, NX // 2 :], odd_high, odd_low, odd_fine),
+        (back[:, : NX // 2], even_back_high, even_back_low, even_fine),
+        (back[:, NX // 2 :], odd_back_high, odd_back_low, odd_fine),
     ):
         v_high, v_low = split(value)
-        both = dot_nt(jnp.concatenate([v_high, v_low], axis=0), high[...])
-        small = dot_nt(v_high, low[...]) + dot_nt(finest(value[:, :LOW_X], 1), fine[...])
+        both = dot(jnp.concatenate([v_high, v_low], axis=0), high[...])
+        small = dot(v_high, low[...]) + dot(finest(value[:, :LOW_X], 1), fine[...])
         parts.append(both[:rows] + (both[rows:] + small))
     work[:, :half] = parts[0] + parts[1]
     work[:, half:] = parts[0] - parts[1]
@@ -548,6 +550,8 @@
     x_square, x_factor = wave_factors(x_waves, NX)
     z_square, z_factor = wave_factors(z_waves, NZ)
     f32 = np.float32
+    even = folded[: N_DOM // 2 * XW, : NX // 2]
+    odd = folded[: N_DOM // 2 * XW, NX // 2 :]
 
     def back(table, low):
         return (*halves(table), thirds(table[:, :low], 1))
@@ -557,8 +561,10 @@
         "y_odd": halves(along_y[NY // 2 :, : NY // 2]),
         "y_even_back": back(along_y[: NY // 2, : NY // 2].T, LOW_Y),
         "y_odd_back": back(along_y[NY // 2 :, : NY // 2].T, LOW_Y),
-        "x_even": back(folded[: N_DOM // 2 * XW, : NX // 2], LOW_X),
-        "x_odd": back(folded[: N_DOM // 2 * XW, NX // 2 :], LOW_X),
+        "x_even": halves(even),
+        "x_odd": halves(odd),
+        "x_even_back": (*halves(even.T), thirds(even.T[:LOW_X], 0)),
+        "x_odd_back": (*halves(odd.T), thirds(odd.T[:LOW_X], 0)),
         "z": halves(z_rows),
         "z_back": back(z_rows.T, MODES * NZ),
         "y_info": y_info.astype(f32),
@@ -629,8 +635,8 @@
             shape(DEVICES * MODES, 128),
             [
                 ("v", table["y_info"]), ("v", held),
-                *[("v", x) for x in table["x_even"][:2] + table["x_odd"][:2]],
-                ("v", table["x_even"][2]), ("v", table["x_odd"][2]),
+                *[("v", x) for x in table["x_even"] + table["x_odd"]],
+                *[("v", x) for x in table["x_even_back"] + table["x_odd_back"]],
                 *[("v", x) for x in table["z"] + table["z_back"]],
                 ("v", table["x_square"]), ("v", table["x_factor"]),
                 ("v", table["z_square"]), ("v", table["z_factor"]),

time: 74.4 us -> 74.1 us (level)
  no operation moved by 1% of the time
where the time goes in v4:
time: 74.1 us; the launch traced here: 73.8 us
  blocking collectives  30 us (40%)
  Pallas kernels  14.6 us (20%)
  waiting for transfers between devices  14.2 us (19%)
  starting transfers between devices  12.8 us (17%)
  other arithmetic  1.31 us (2%)
    all_to_all x1, blocking collectives, exchange(): lax.all_to_all(sent, ('pme', 'dom'), 0, 0).reshape(DEVICES * MODES, 128)  30 us
    pallas_call x7, Pallas kernels, call(): pl.pallas_call(kernel, out_shape=outs, in_specs=in_specs, out_specs=[vmem...  14.6 us
    all_to_all x1, waiting for transfers between devices, exchange(): lax.all_to_all(sent, ('pme', 'dom'), 0, 0).reshape(DEVICES * MODES, 128)  10.3 us
    ppermute x4, starting transfers between devices, permuted(): lax.ppermute(x, axis, [(i, (i + by) % length) for i in range(length)])  6.56 us
    all_to_all x1, starting transfers between devices, exchange(): lax.all_to_all(sent, ('pme', 'dom'), 0, 0).reshape(DEVICES * MODES, 128)  6.22 us
    ppermute x4, waiting for transfers between devices, permuted(): lax.ppermute(x, axis, [(i, (i + by) % length) for i in range(length)])  3.99 us
  transfers between devices with their start and end apart: 5, of which 3 were waited for; matrix products, arithmetic and copies ran while one was open for 1% of the time, Pallas kernels for 11%

profile of v4, /device:TPU:1, one launch (start us, length us, event | category | flops | bytes accessed | tf_op | source)
XLA Modules:
  0.0 73.8 jit_solution(821812714063207772)
XLA Ops:
  0.0 1.1 %shard_map.334 = (f32[4,2176]{1,0:T(4,128)S(1)}, f32[4,128]{1,0:T(4,128)S(1)}) custom-call(s32[1,64]{1,0:T(1,128)} %bitcast.20, s32[3,64]{1,0:T(4,128)} %corner_in.1, s32[3,2048]{1,0:T(4,128)} %cell_in.1, f32[3,2048]{1,0:T(4,128)} %fraction_in.1, f32[1,2048]{1,0:T(1,128)} %bitcast.19), custom_call_target="tpu_custom_call" | custom-call | flops 1000000 | bytes 1000000 | tf_op jit(solution)/shard_map/pallas_call | solution.py:511
  1.1 0.0 copy-start.31
  1.1 2.5 %collective-permute-start = (f32[4,2176]{1,0:T(4,128)S(1)}, f32[4,2176]{1,0:T(4,128)S(1)}, u32[]{:S(2)}, u32[]{:S(2)}) collective-permute-start(f32[4,2176]{1,0:T(4,128)S(1)} %get-tuple-element.11.atoms), channel_id=1, source_target_pairs={{0,32},{32,64},{64,96},{96,128},{128,160},{160,192},{192,224},{224... | collective-permute-start | bytes 104456 | tf_op jit(solution)/shard_map/ppermute | solution.py:528
  3.6 0.0 copy-done.31
  3.6 0.7 bitcast_add_fusion.ya
  4.3 0.0 copy-start.17
  4.3 0.0 copy-start.7
  4.4 0.0 copy-start.8
  4.4 0.0 copy-start.9
  4.4 0.0 copy-start.20
  4.4 0.0 copy-start.21
  4.4 0.0 copy-start.23
  4.4 0.0 copy-start.24
  4.4 0.0 copy-start.25
  4.4 0.0 copy-start.27
  4.5 1.4 %shard_map.335.own = f32[784,128]{1,0:T(8,128)S(1)} custom-call(s32[64]{0:T(128)S(1)} %bitcast_add_fusion.ya, f32[4,2176]{1,0:T(4,128)S(1)} %get-tuple-element.11.atoms), custom_call_target="tpu_custom_call" | custom-call | flops 3000000000 | bytes 1000000 | tf_op jit(solution)/shard_map/pallas_call | solution.py:511
  5.9 3.0 %collective-permute-done.atoms = f32[4,2176]{1,0:T(4,128)S(1)} collective-permute-done((f32[4,2176]{1,0:T(4,128)S(1)}, f32[4,2176]{1,0:T(4,128)S(1)}, u32[]{:S(2)}, u32[]{:S(2)}) %collective-permute-start) | collective-permute-done | bytes 34848 | tf_op jit(solution)/shard_map/ppermute | solution.py:528
  8.9 0.0 copy-done.14
  8.9 0.0 copy-done.15
  8.9 0.0 copy-done.16
  8.9 0.0 copy-done.17
  8.9 0.0 copy-start.2
  8.9 0.0 copy-start.3
  9.0 0.0 copy-start.4
  9.0 0.0 copy-start.5
  9.0 0.0 copy-start.6
  9.0 0.0 copy-start.22
  9.0 0.0 copy-start.26
  9.0 0.0 copy-start.28
  9.0 0.0 copy-start.29
  9.0 1.8 %shard_map.336 = f32[768,128]{1,0:T(8,128)S(1)} custom-call(s32[64]{0:T(128)S(1)} %fusion.ya, f32[4,2176]{1,0:T(4,128)S(1)} %collective-permute-done.atoms, f32[784,128]{1,0:T(8,128)S(1)} %shard_map.335.own, bf16[384,384]{1,0:T(8,128)(2,1)S(1)} %copy-done.14, bf16[384,384]{1,0:T(8,128)(2,1)S(1)} %copy-done.15, bf16[384,384]{1,0:T(8,128)(2,1)S(1)} %copy-done.16, ...), custom_call_target="tpu_custom_call" | custom-call | flops 1000000 | bytes 1000000 | tf_op jit(solution)/shard_map/pallas_call | solution.py:511
  10.9 0.0 copy-start
  10.9 0.0 copy-start.1
  10.9 30.0 %all_to_all.10 = f32[256,1,384]{2,1,0:T(1,128)S(1)} all-to-all(f32[256,1,384]{2,1,0:T(1,128)S(1)} %bitcast.15), channel_id=1, replica_groups=mesh['pme'=8,'dom'=32] {'pme','dom'}, dimensions={0} | all-to-all | bytes 786432 | tf_op jit(solution)/shard_map/all_to_all | solution.py:533
  40.9 0.0 copy-done.7
  40.9 0.0 copy-done.8
  40.9 0.0 copy-done.9
  40.9 0.0 copy-done.20
  41.0 0.0 copy-done.21
  41.0 0.0 copy-done.23
  41.0 0.0 copy-done.24
  41.0 0.0 copy-done.25
  41.0 0.0 copy-done.27
  41.0 0.0 copy-done.2
  41.0 0.0 copy-done.3
  41.1 3.3 %shard_map.337 = f32[768,128]{1,0:T(8,128)} custom-call(f32[256,128]{1,0:T(8,128)S(1)} %copy-done.20, f32[768,128]{1,0:T(8,128)S(1)} %bitcast.16, bf16[512,384]{1,0:T(8,128)(2,1)S(1)} %copy-done, bf16[512,384]{1,0:T(8,128)(2,1)S(1)} %copy-done.1, bf16[512,384]{1,0:T(8,128)(2,1)S(1)} %copy-done.2, bf16[512,384]{1,0:T(8,128)(2,1)S(1)} %copy-done.3, ...), custom_call_target="tpu_custom_call" | custom-call | flops 1000000 | bytes 1000000 | tf_op jit(solution)/shard_map/pallas_call | solution.py:511
  44.4 6.2 %all-to-all-start.1 = ((f32[256,1,384]{2,1,0:T(1,128)}), f32[256,1,384]{2,1,0:T(1,128)S(1)}, u32[]{:S(2)}, u32[]{:S(2)}) async-start(f32[256,1,384]{2,1,0:T(1,128)} %bitcast.7), calls=%async_computation.1 | async-start | bytes 786432 | tf_op jit(solution)/shard_map/all_to_all | solution.py:533
  50.6 2.2 %collective-permute-start.1 = (f32[4,128]{1,0:T(4,128)S(1)}, f32[4,128]{1,0:T(4,128)S(1)}, u32[]{:S(2)}, u32[]{:S(2)}) collective-permute-start(f32[4,128]{1,0:T(4,128)S(1)} %get-tuple-element.13), channel_id=1, source_target_pairs={{0,31},{1,0},{2,1},{3,2},{4,3},{5,4},{6,5},{7,6},{8,7},{9,8},{10,9... | collective-permute-start | bytes 6152 | tf_op jit(solution)/shard_map/ppermute | solution.py:528
  52.9 0.1 reshape.33
  53.0 0.1 copy.41
  53.1 1.0 %collective-permute-done.1.beyond = f32[4,128]{1,0:T(4,128)S(1)} collective-permute-done((f32[4,128]{1,0:T(4,128)S(1)}, f32[4,128]{1,0:T(4,128)S(1)}, u32[]{:S(2)}, u32[]{:S(2)}) %collective-permute-start.1) | collective-permute-done | bytes 2080 | tf_op jit(solution)/shard_map/ppermute | solution.py:528
  54.0 0.0 copy-start.13
  54.0 0.0 copy-start.18
  54.1 0.0 copy-start.19
  54.1 3.2 %shard_map.339 = (f32[3,2048]{1,0:T(4,128)S(1)}, f32[8,128]{1,0:T(8,128)S(1)}) custom-call(f32[4,2176]{1,0:T(4,128)S(1)} %get-tuple-element.11.atoms, f32[128,64]{1,0:T(8,128)S(1)} %bitcast.17, s32[2,1024]{1,0:T(2,128)S(1)} %copy-done.30, f32[4,128]{1,0:T(4,128)S(1)} %collective-permute-done.1.beyond), custom_call_target="tpu_custom_call" | custom-call | flops 8000000000 | bytes 1000000 | tf_op jit(solution)/shard_map/pallas_call | solution.py:511
  57.2 0.3 collective-permute-start.2
  57.5 10.3 %all-to-all-done.1 = f32[256,1,384]{2,1,0:T(1,128)S(1)} async-done(((f32[256,1,384]{2,1,0:T(1,128)}), f32[256,1,384]{2,1,0:T(1,128)S(1)}, u32[]{:S(2)}, u32[]{:S(2)}) %all-to-all-start.1) | async-done | bytes 393248 | tf_op jit(solution)/shard_map/all_to_all | solution.py:533
  67.8 0.0 copy-done.11
  67.8 2.2 %shard_map.338 = (f32[784,128]{1,0:T(8,128)S(1)}, f32[3,2048]{1,0:T(4,128)S(1)}) custom-call(s32[64]{0:T(128)S(1)} %fusion.ya, f32[4,2176]{1,0:T(4,128)S(1)} %collective-permute-done.atoms, f32[768,128]{1,0:T(8,128)S(1)} %bitcast.14, bf16[384,384]{1,0:T(8,128)(2,1)S(1)} %copy-done.10, bf16[384,384]{1,0:T(8,128)(2,1)S(1)} %copy-done.11, ...), custom_call_target="tpu_custom_call" | custom-call | flops 1000000 | bytes 1000000 | tf_op jit(solution)/shard_map/pallas_call | solution.py:511
  70.0 1.5 %collective-permute-start.3 = (f32[3,2048]{1,0:T(4,128)S(1)}, f32[3,2048]{1,0:T(4,128)S(1)}, u32[]{:S(2)}, u32[]{:S(2)}) collective-permute-start(f32[3,2048]{1,0:T(4,128)S(1)} %get-tuple-element.16), channel_id=1, source_target_pairs={{0,224},{32,0},{64,32},{96,64},{128,96},{160,128},{192,160},{224,1... | collective-permute-start | bytes 73736 | tf_op jit(solution)/shard_map/ppermute | solution.py:528
  71.6 0.0 collective-permute-done.2.halo
  71.6 1.6 %shard_map.340 = f32[3,2048]{1,0:T(4,128)S(1)} custom-call(s32[64]{0:T(128)S(1)} %bitcast_add_fusion.ya, f32[4,2176]{1,0:T(4,128)S(1)} %get-tuple-element.11.atoms, f32[784,128]{1,0:T(8,128)S(1)} %get-tuple-element.12.grid, f32[3,2048]{1,0:T(4,128)S(1)} %get-tuple-element.14.near, f32[8,128]{1,0:T(8,128)S(1)} %collective-permute-done.2.halo), custom_call_target="tpu_custom_call" | custom-call | flops 3000000000 | bytes 1000000 | tf_op jit(solution)/shard_map/pallas_call | solution.py:511
  73.2 0.0 collective-permute-done.3
  73.2 0.6 add.7
  (24 shorter events, 0.0 us)
Async XLA Ops:
  1.1 2.6 %copy-start.31 = (s32[64,1]{0,1:T(1,128)S(1)}, s32[64,1]{0,1:T(1,128)}, u32[]{:S(2)}) copy-start(s32[64,1]{0,1:T(1,128)} %param.36) | copy-start | bytes 772
  1.1 7.8 %collective-permute-start = (f32[4,2176]{1,0:T(4,128)S(1)}, f32[4,2176]{1,0:T(4,128)S(1)}, u32[]{:S(2)}, u32[]{:S(2)}) collective-permute-start(f32[4,2176]{1,0:T(4,128)S(1)} %get-tuple-element.11.atoms), channel_id=1, source_target_pairs={{0,32},{32,64},{64,96},{96,128},{128,160},{160,192},{192,224},{224... | collective-permute-start | bytes 104456 | tf_op jit(solution)/shard_map/ppermute | solution.py:528
  4.3 4.6 %copy-start.14 = (bf16[384,384]{1,0:T(8,128)(2,1)S(1)}, bf16[384,384]{1,0:T(8,128)(2,1)}, u32[]{:S(2)}) copy-start(bf16[384,384]{1,0:T(8,128)(2,1)} %constant.62.clone.even_high) | copy-start | bytes 884740
  4.3 4.6 %copy-start.15 = (bf16[384,384]{1,0:T(8,128)(2,1)S(1)}, bf16[384,384]{1,0:T(8,128)(2,1)}, u32[]{:S(2)}) copy-start(bf16[384,384]{1,0:T(8,128)(2,1)} %constant.63.clone.even_low) | copy-start | bytes 884740
  4.3 4.6 %copy-start.16 = (bf16[384,384]{1,0:T(8,128)(2,1)S(1)}, bf16[384,384]{1,0:T(8,128)(2,1)}, u32[]{:S(2)}) copy-start(bf16[384,384]{1,0:T(8,128)(2,1)} %constant.64.clone.odd_high) | copy-start | bytes 884740
  4.3 4.6 %copy-start.17 = (bf16[384,384]{1,0:T(8,128)(2,1)S(1)}, bf16[384,384]{1,0:T(8,128)(2,1)}, u32[]{:S(2)}) copy-start(bf16[384,384]{1,0:T(8,128)(2,1)} %constant.65.clone.odd_low) | copy-start | bytes 884740
  4.3 36.6 %copy-start.7 = (bf16[384,512]{1,0:T(8,128)(2,1)S(1)}, bf16[384,512]{1,0:T(8,128)(2,1)}, u32[]{:S(2)}) copy-start(bf16[384,512]{1,0:T(8,128)(2,1)} %constant.74.clone.odd_back_high) | copy-start | bytes 1179652
  4.4 36.6 %copy-start.8 = (bf16[384,512]{1,0:T(8,128)(2,1)S(1)}, bf16[384,512]{1,0:T(8,128)(2,1)}, u32[]{:S(2)}) copy-start(bf16[384,512]{1,0:T(8,128)(2,1)} %constant.75.clone.odd_back_low) | copy-start | bytes 1179652
  4.4 36.6 %copy-start.9 = (bf16[384,512]{1,0:T(8,128)(2,1)S(1)}, bf16[384,512]{1,0:T(8,128)(2,1)}, u32[]{:S(2)}) copy-start(bf16[384,512]{1,0:T(8,128)(2,1)} %constant.76.clone.odd_fine) | copy-start | bytes 1179652
  4.4 36.6 %copy-start.20 = (f32[256,128]{1,0:T(8,128)S(1)}, f32[256,128]{1,0:T(8,128)}, u32[]{:S(2)}) copy-start(f32[256,128]{1,0:T(8,128)} %constant.66.clone.y_info) | copy-start | bytes 393220
  4.4 36.6 %copy-start.21 = (bf16[96,288]{1,0:T(8,128)(2,1)S(1)}, bf16[96,288]{1,0:T(8,128)(2,1)}, u32[]{:S(2)}) copy-start(bf16[96,288]{1,0:T(8,128)(2,1)} %constant.81.clone.tz_fine) | copy-start | bytes 165892
  4.4 36.6 %copy-start.23 = (bf16[96,96]{1,0:T(8,128)(2,1)S(1)}, bf16[96,96]{1,0:T(8,128)(2,1)}, u32[]{:S(2)}) copy-start(bf16[96,96]{1,0:T(8,128)(2,1)} %constant.78.clone.kz_low) | copy-start | bytes 55300
  4.4 36.6 %copy-start.24 = (bf16[96,96]{1,0:T(8,128)(2,1)S(1)}, bf16[96,96]{1,0:T(8,128)(2,1)}, u32[]{:S(2)}) copy-start(bf16[96,96]{1,0:T(8,128)(2,1)} %constant.79.clone.tz_high) | copy-start | bytes 55300
  4.4 36.6 %copy-start.25 = (bf16[96,96]{1,0:T(8,128)(2,1)S(1)}, bf16[96,96]{1,0:T(8,128)(2,1)}, u32[]{:S(2)}) copy-start(bf16[96,96]{1,0:T(8,128)(2,1)} %constant.80.clone.tz_low) | copy-start | bytes 55300
  4.4 36.6 %copy-start.27 = (f32[32,128]{1,0:T(8,128)S(1)}, f32[32,128]{1,0:T(8,128)}, u32[]{:S(2)}) copy-start(f32[32,128]{1,0:T(8,128)} %constant.85.clone.z_factor) | copy-start | bytes 49156
  8.9 32.1 %copy-start.2 = (bf16[512,384]{1,0:T(8,128)(2,1)S(1)}, bf16[512,384]{1,0:T(8,128)(2,1)}, u32[]{:S(2)}) copy-start(bf16[512,384]{1,0:T(8,128)(2,1)} %constant.69.clone.odd_high) | copy-start | bytes 1179652
  8.9 32.1 %copy-start.3 = (bf16[512,384]{1,0:T(8,128)(2,1)S(1)}, bf16[512,384]{1,0:T(8,128)(2,1)}, u32[]{:S(2)}) copy-start(bf16[512,384]{1,0:T(8,128)(2,1)} %constant.70.clone.odd_low) | copy-start | bytes 1179652
  9.0 32.1 %copy-start.4 = (bf16[384,512]{1,0:T(8,128)(2,1)S(1)}, bf16[384,512]{1,0:T(8,128)(2,1)}, u32[]{:S(2)}) copy-start(bf16[384,512]{1,0:T(8,128)(2,1)} %constant.71.clone.even_back_high) | copy-start | bytes 1179652
  9.0 32.1 %copy-start.5 = (bf16[384,512]{1,0:T(8,128)(2,1)S(1)}, bf16[384,512]{1,0:T(8,128)(2,1)}, u32[]{:S(2)}) copy-start(bf16[384,512]{1,0:T(8,128)(2,1)} %constant.72.clone.even_back_low) | copy-start | bytes 1179652
  9.0 32.1 %copy-start.6 = (bf16[384,512]{1,0:T(8,128)(2,1)S(1)}, bf16[384,512]{1,0:T(8,128)(2,1)}, u32[]{:S(2)}) copy-start(bf16[384,512]{1,0:T(8,128)(2,1)} %constant.73.clone.even_fine) | copy-start | bytes 1179652
  9.0 32.1 %copy-start.22 = (bf16[96,96]{1,0:T(8,128)(2,1)S(1)}, bf16[96,96]{1,0:T(8,128)(2,1)}, u32[]{:S(2)}) copy-start(bf16[96,96]{1,0:T(8,128)(2,1)} %constant.77.clone.kz_high) | copy-start | bytes 55300
  9.0 32.1 %copy-start.26 = (f32[32,128]{1,0:T(8,128)S(1)}, f32[32,128]{1,0:T(8,128)}, u32[]{:S(2)}) copy-start(f32[32,128]{1,0:T(8,128)} %constant.84.clone.z_square) | copy-start | bytes 49156
  9.0 32.1 %copy-start.28 = (f32[1,768]{1,0:T(1,128)S(1)}, f32[1,768]{1,0:T(1,128)}, u32[]{:S(2)}) copy-start(f32[1,768]{1,0:T(1,128)} %constant.82.clone.x_square) | copy-start | bytes 9220
  9.0 32.1 %copy-start.29 = (f32[1,768]{1,0:T(1,128)S(1)}, f32[1,768]{1,0:T(1,128)}, u32[]{:S(2)}) copy-start(f32[1,768]{1,0:T(1,128)} %constant.83.clone.x_factor) | copy-start | bytes 9220
  10.9 30.2 %copy-start = (bf16[512,384]{1,0:T(8,128)(2,1)S(1)}, bf16[512,384]{1,0:T(8,128)(2,1)}, u32[]{:S(2)}) copy-start(bf16[512,384]{1,0:T(8,128)(2,1)} %constant.67.clone.even_high) | copy-start | bytes 1179652
  10.9 30.2 %copy-start.1 = (bf16[512,384]{1,0:T(8,128)(2,1)S(1)}, bf16[512,384]{1,0:T(8,128)(2,1)}, u32[]{:S(2)}) copy-start(bf16[512,384]{1,0:T(8,128)(2,1)} %constant.68.clone.even_low) | copy-start | bytes 1179652
  44.4 23.4 %all-to-all-start.1 = ((f32[256,1,384]{2,1,0:T(1,128)}), f32[256,1,384]{2,1,0:T(1,128)S(1)}, u32[]{:S(2)}, u32[]{:S(2)}) async-start(f32[256,1,384]{2,1,0:T(1,128)} %bitcast.7), calls=%async_computation.1 | async-start | bytes 786432 | tf_op jit(solution)/shard_map/all_to_all | solution.py:533
  50.6 3.4 %collective-permute-start.1 = (f32[4,128]{1,0:T(4,128)S(1)}, f32[4,128]{1,0:T(4,128)S(1)}, u32[]{:S(2)}, u32[]{:S(2)}) collective-permute-start(f32[4,128]{1,0:T(4,128)S(1)} %get-tuple-element.13), channel_id=1, source_target_pairs={{0,31},{1,0},{2,1},{3,2},{4,3},{5,4},{6,5},{7,6},{8,7},{9,8},{10,9... | collective-permute-start | bytes 6152 | tf_op jit(solution)/shard_map/ppermute | solution.py:528
  53.0 1.1 %copy-start.30 = (s32[2,1024]{1,0:T(2,128)S(1)}, s32[2,1024]{1,0:T(2,128)}, u32[]{:S(2)}) copy-start(s32[2,1024]{1,0:T(2,128)} %pairs.1) | copy-start | bytes 24580
  54.0 13.7 %copy-start.10 = (bf16[384,384]{1,0:T(8,128)(2,1)S(1)}, bf16[384,384]{1,0:T(8,128)(2,1)}, u32[]{:S(2)}) copy-start(bf16[384,384]{1,0:T(8,128)(2,1)} %constant.86.clone.even_high) | copy-start | bytes 884740
  54.0 13.8 %copy-start.11 = (bf16[384,384]{1,0:T(8,128)(2,1)S(1)}, bf16[384,384]{1,0:T(8,128)(2,1)}, u32[]{:S(2)}) copy-start(bf16[384,384]{1,0:T(8,128)(2,1)} %constant.87.clone.even_low) | copy-start | bytes 884740
  54.0 13.8 %copy-start.12 = (bf16[384,384]{1,0:T(8,128)(2,1)S(1)}, bf16[384,384]{1,0:T(8,128)(2,1)}, u32[]{:S(2)}) copy-start(bf16[384,384]{1,0:T(8,128)(2,1)} %constant.89.clone.odd_high) | copy-start | bytes 884740
  54.0 13.7 %copy-start.13 = (bf16[384,384]{1,0:T(8,128)(2,1)S(1)}, bf16[384,384]{1,0:T(8,128)(2,1)}, u32[]{:S(2)}) copy-start(bf16[384,384]{1,0:T(8,128)(2,1)} %constant.90.clone.odd_low) | copy-start | bytes 884740
  54.0 13.7 %copy-start.18 = (bf16[384,192]{1,0:T(8,128)(2,1)S(1)}, bf16[384,192]{1,0:T(8,128)(2,1)}, u32[]{:S(2)}) copy-start(bf16[384,192]{1,0:T(8,128)(2,1)} %constant.88.clone.even_fine) | copy-start | bytes 442372
  54.1 13.7 %copy-start.19 = (bf16[384,192]{1,0:T(8,128)(2,1)S(1)}, bf16[384,192]{1,0:T(8,128)(2,1)}, u32[]{:S(2)}) copy-start(bf16[384,192]{1,0:T(8,128)(2,1)} %constant.91.clone.odd_fine) | copy-start | bytes 442372
  57.2 14.3 %collective-permute-start.2 = (f32[8,128]{1,0:T(8,128)S(1)}, f32[8,128]{1,0:T(8,128)S(1)}, u32[]{:S(2)}, u32[]{:S(2)}) collective-permute-start(f32[8,128]{1,0:T(8,128)S(1)} %get-tuple-element.15), channel_id=1, source_target_pairs={{0,1},{1,2},{2,3},{3,4},{4,5},{5,6},{6,7},{7,8},{8,9},{9,10},{10,1... | collective-permute-start | bytes 12296 | tf_op jit(solution)/shard_map/ppermute | solution.py:528
  70.0 3.1 %collective-permute-start.3 = (f32[3,2048]{1,0:T(4,128)S(1)}, f32[3,2048]{1,0:T(4,128)S(1)}, u32[]{:S(2)}, u32[]{:S(2)}) collective-permute-start(f32[3,2048]{1,0:T(4,128)S(1)} %get-tuple-element.16), channel_id=1, source_target_pairs={{0,224},{32,0},{64,32},{96,64},{128,96},{160,128},{192,160},{224,1... | collective-permute-start | bytes 73736 | tf_op jit(solution)/shard_map/ppermute | solution.py:528

commit v5 on v4

--- a/solution.py
+++ b/solution.py
@@ -251,7 +251,7 @@
 
 def filter_kernel(
     y_info, held, even_high, even_low, odd_high, odd_low, even_back_high, even_back_low, even_fine,
-    odd_back_high, odd_back_low, odd_fine, kz_high, kz_low, tz_high, tz_low, tz_fine,
+    odd_back_high, odd_back_low, odd_fine, kz, tz,
     x_square, x_factor, z_square, z_factor, out, work,
 ):
     lane = iota((8, 128), 1) >> 5
@@ -277,7 +277,7 @@
         both = dot(jnp.concatenate([v_high, v_low], axis=0), high[...])
         waves.append(both[:rows] + (both[rows:] + dot(v_high, low[...])))
     w_high, w_low = split(jnp.concatenate(waves, axis=1))
-    full = dot(kz_high[...], w_high) + (dot(kz_high[...], w_low) + dot(kz_low[...], w_high))
+    full = dot(kz[...], jnp.concatenate([w_high, w_low, w_high], axis=0))
     device = lax.axis_index("pme") * N_DOM + lax.axis_index("dom")
     info = y_info[pl.ds(device, 1), :]
     scaled = []
@@ -289,9 +289,8 @@
         scaled.append(full[m * NZ : m * NZ + NZ] * influence)
     scaled = jnp.concatenate(scaled, axis=0)
     s_high, s_low = split(scaled)
-    back = dot(tz_high[...], s_high) + (
-        dot(tz_high[...], s_low)
-        + (dot(tz_low[...], s_high) + dot(tz_fine[...], finest(scaled, 0)))
+    back = dot(
+        tz[...], jnp.concatenate([s_high, s_low, s_high, finest(scaled, 0)], axis=0)
     )
     parts = []
     for value, high, low, fine in (
@@ -553,6 +552,10 @@
     even = folded[: N_DOM // 2 * XW, : NX // 2]
     odd = folded[: N_DOM // 2 * XW, NX // 2 :]
 
+    def along(table):
+        high, low = halves(table)
+        return np.concatenate([high, high, low], axis=1)
+
     def back(table, low):
         return (*halves(table), thirds(table[:, :low], 1))
 
@@ -565,8 +568,8 @@
         "x_odd": halves(odd),
         "x_even_back": (*halves(even.T), thirds(even.T[:LOW_X], 0)),
         "x_odd_back": (*halves(odd.T), thirds(odd.T[:LOW_X], 0)),
-        "z": halves(z_rows),
-        "z_back": back(z_rows.T, MODES * NZ),
+        "z": along(z_rows),
+        "z_back": np.concatenate([along(z_rows.T), thirds(z_rows.T, 1)], axis=1),
         "y_info": y_info.astype(f32),
         "x_square": x_square.astype(f32)[None, :],
         "x_factor": (x_factor / math.pi).astype(f32)[None, :],
@@ -637,7 +640,7 @@
                 ("v", table["y_info"]), ("v", held),
                 *[("v", x) for x in table["x_even"] + table["x_odd"]],
                 *[("v", x) for x in table["x_even_back"] + table["x_odd_back"]],
-                *[("v", x) for x in table["z"] + table["z_back"]],
+                ("v", table["z"]), ("v", table["z_back"]),
                 ("v", table["x_square"]), ("v", table["x_factor"]),
                 ("v", table["z_square"]), ("v", table["z_factor"]),
             ],

time: 74.1 us -> 73.9 us (level)
  no operation moved by 1% of the time
where the time goes in v5:
time: 73.9 us; the launch traced here: 73.5 us
  blocking collectives  30 us (41%)
  Pallas kernels  14.4 us (19%)
  waiting for transfers between devices  14.3 us (19%)
  starting transfers between devices  12.8 us (17%)
  other arithmetic  1.31 us (2%)
    all_to_all x1, blocking collectives, exchange(): lax.all_to_all(sent, ('pme', 'dom'), 0, 0).reshape(DEVICES * MODES, 128)  30 us
    pallas_call x7, Pallas kernels, call(): pl.pallas_call(kernel, out_shape=outs, in_specs=in_specs, out_specs=[vmem...  14.4 us
    all_to_all x1, waiting for transfers between devices, exchange(): lax.all_to_all(sent, ('pme', 'dom'), 0, 0).reshape(DEVICES * MODES, 128)  10.2 us
    ppermute x4, starting transfers between devices, permuted(): lax.ppermute(x, axis, [(i, (i + by) % length) for i in range(length)])  6.56 us
    all_to_all x1, starting transfers between devices, exchange(): lax.all_to_all(sent, ('pme', 'dom'), 0, 0).reshape(DEVICES * MODES, 128)  6.22 us
    ppermute x4, waiting for transfers between devices, permuted(): lax.ppermute(x, axis, [(i, (i + by) % length) for i in range(length)])  4.04 us
  transfers between devices with their start and end apart: 5, of which 3 were waited for; matrix products, arithmetic and copies ran while one was open for 1% of the time, Pallas kernels for 11%

profile of v5, /device:TPU:1, one launch (start us, length us, event | category | flops | bytes accessed | tf_op | source)
XLA Modules:
  0.0 73.5 jit_solution(12442286984761144053)
XLA Ops:
  0.0 1.1 %shard_map.307 = (f32[4,2176]{1,0:T(4,128)S(1)}, f32[4,128]{1,0:T(4,128)S(1)}) custom-call(s32[1,64]{1,0:T(1,128)} %bitcast.20, s32[3,64]{1,0:T(4,128)} %corner_in.1, s32[3,2048]{1,0:T(4,128)} %cell_in.1, f32[3,2048]{1,0:T(4,128)} %fraction_in.1, f32[1,2048]{1,0:T(1,128)} %bitcast.19), custom_call_target="tpu_custom_call" | custom-call | flops 1000000 | bytes 1000000 | tf_op jit(solution)/shard_map/pallas_call | solution.py:510
  1.1 0.0 copy-start.28
  1.1 2.5 %collective-permute-start = (f32[4,2176]{1,0:T(4,128)S(1)}, f32[4,2176]{1,0:T(4,128)S(1)}, u32[]{:S(2)}, u32[]{:S(2)}) collective-permute-start(f32[4,2176]{1,0:T(4,128)S(1)} %get-tuple-element.11.atoms), channel_id=1, source_target_pairs={{0,32},{32,64},{64,96},{96,128},{128,160},{160,192},{192,224},{224... | collective-permute-start | bytes 104456 | tf_op jit(solution)/shard_map/ppermute | solution.py:527
  3.6 0.0 copy-done.28
  3.6 0.7 bitcast_add_fusion.ya
  4.3 0.0 copy-start.17
  4.3 0.0 copy-start.7
  4.4 0.0 copy-start.8
  4.4 0.0 copy-start.9
  4.4 0.0 copy-start.20
  4.4 0.0 copy-start.21
  4.4 0.0 copy-start.22
  4.4 1.4 %shard_map.308.own = f32[784,128]{1,0:T(8,128)S(1)} custom-call(s32[64]{0:T(128)S(1)} %bitcast_add_fusion.ya, f32[4,2176]{1,0:T(4,128)S(1)} %get-tuple-element.11.atoms), custom_call_target="tpu_custom_call" | custom-call | flops 3000000000 | bytes 1000000 | tf_op jit(solution)/shard_map/pallas_call | solution.py:510
  5.8 3.1 %collective-permute-done.atoms = f32[4,2176]{1,0:T(4,128)S(1)} collective-permute-done((f32[4,2176]{1,0:T(4,128)S(1)}, f32[4,2176]{1,0:T(4,128)S(1)}, u32[]{:S(2)}, u32[]{:S(2)}) %collective-permute-start) | collective-permute-done | bytes 34848 | tf_op jit(solution)/shard_map/ppermute | solution.py:527
  8.9 0.0 copy-done.14
  8.9 0.0 copy-done.15
  8.9 0.0 copy-done.16
  8.9 0.0 copy-done.17
  8.9 0.0 copy-start.2
  8.9 0.0 copy-start.3
  9.0 0.0 copy-start.4
  9.0 0.0 copy-start.5
  9.0 0.0 copy-start.6
  9.0 0.0 copy-start.23
  9.0 0.0 copy-start.24
  9.0 0.0 copy-start.25
  9.0 0.0 copy-start.26
  9.0 1.8 %shard_map.309 = f32[768,128]{1,0:T(8,128)S(1)} custom-call(s32[64]{0:T(128)S(1)} %fusion.ya, f32[4,2176]{1,0:T(4,128)S(1)} %collective-permute-done.atoms, f32[784,128]{1,0:T(8,128)S(1)} %shard_map.308.own, bf16[384,384]{1,0:T(8,128)(2,1)S(1)} %copy-done.14, bf16[384,384]{1,0:T(8,128)(2,1)S(1)} %copy-done.15, bf16[384,384]{1,0:T(8,128)(2,1)S(1)} %copy-done.16, ...), custom_call_target="tpu_custom_call" | custom-call | flops 1000000 | bytes 1000000 | tf_op jit(solution)/shard_map/pallas_call | solution.py:510
  10.9 0.0 copy-start
  10.9 0.0 copy-start.1
  10.9 30.0 %all_to_all.10 = f32[256,1,384]{2,1,0:T(1,128)S(1)} all-to-all(f32[256,1,384]{2,1,0:T(1,128)S(1)} %bitcast.15), channel_id=1, replica_groups=mesh['pme'=8,'dom'=32] {'pme','dom'}, dimensions={0} | all-to-all | bytes 786432 | tf_op jit(solution)/shard_map/all_to_all | solution.py:532
  40.9 0.0 copy-done.7
  40.9 0.0 copy-done.8
  40.9 0.0 copy-done.9
  40.9 0.0 copy-done.20
  41.0 0.0 copy-done.21
  41.0 0.0 copy-done.22
  41.0 0.0 copy-done.2
  41.0 0.0 copy-done.3
  41.0 0.0 copy-done.4
  41.0 0.0 copy-done.5
  41.0 0.0 copy-done.6
  41.0 0.0 copy-done.23
  41.0 0.0 copy-done.24
  41.1 3.0 %shard_map.310 = f32[768,128]{1,0:T(8,128)} custom-call(f32[256,128]{1,0:T(8,128)S(1)} %copy-done.20, f32[768,128]{1,0:T(8,128)S(1)} %bitcast.16, bf16[512,384]{1,0:T(8,128)(2,1)S(1)} %copy-done, bf16[512,384]{1,0:T(8,128)(2,1)S(1)} %copy-done.1, bf16[512,384]{1,0:T(8,128)(2,1)S(1)} %copy-done.2, bf16[512,384]{1,0:T(8,128)(2,1)S(1)} %copy-done.3, ...), custom_call_target="tpu_custom_call" | custom-call | flops 1000000 | bytes 1000000 | tf_op jit(solution)/shard_map/pallas_call | solution.py:510
  44.1 6.2 %all-to-all-start.1 = ((f32[256,1,384]{2,1,0:T(1,128)}), f32[256,1,384]{2,1,0:T(1,128)S(1)}, u32[]{:S(2)}, u32[]{:S(2)}) async-start(f32[256,1,384]{2,1,0:T(1,128)} %bitcast.7), calls=%async_computation.1 | async-start | bytes 786432 | tf_op jit(solution)/shard_map/all_to_all | solution.py:532
  50.3 2.2 %collective-permute-start.1 = (f32[4,128]{1,0:T(4,128)S(1)}, f32[4,128]{1,0:T(4,128)S(1)}, u32[]{:S(2)}, u32[]{:S(2)}) collective-permute-start(f32[4,128]{1,0:T(4,128)S(1)} %get-tuple-element.13), channel_id=1, source_target_pairs={{0,31},{1,0},{2,1},{3,2},{4,3},{5,4},{6,5},{7,6},{8,7},{9,8},{10,9... | collective-permute-start | bytes 6152 | tf_op jit(solution)/shard_map/ppermute | solution.py:527
  52.6 0.1 reshape.33
  52.7 0.1 copy.38
  52.8 1.0 %collective-permute-done.1.beyond = f32[4,128]{1,0:T(4,128)S(1)} collective-permute-done((f32[4,128]{1,0:T(4,128)S(1)}, f32[4,128]{1,0:T(4,128)S(1)}, u32[]{:S(2)}, u32[]{:S(2)}) %collective-permute-start.1) | collective-permute-done | bytes 2080 | tf_op jit(solution)/shard_map/ppermute | solution.py:527
  53.8 0.0 copy-start.13
  53.8 0.0 copy-start.18
  53.8 0.0 copy-start.19
  53.8 3.2 %shard_map.312 = (f32[3,2048]{1,0:T(4,128)S(1)}, f32[8,128]{1,0:T(8,128)S(1)}) custom-call(f32[4,2176]{1,0:T(4,128)S(1)} %get-tuple-element.11.atoms, f32[128,64]{1,0:T(8,128)S(1)} %bitcast.17, s32[2,1024]{1,0:T(2,128)S(1)} %copy-done.27, f32[4,128]{1,0:T(4,128)S(1)} %collective-permute-done.1.beyond), custom_call_target="tpu_custom_call" | custom-call | flops 8000000000 | bytes 1000000 | tf_op jit(solution)/shard_map/pallas_call | solution.py:510
  57.0 0.3 collective-permute-start.2
  57.2 10.2 %all-to-all-done.1 = f32[256,1,384]{2,1,0:T(1,128)S(1)} async-done(((f32[256,1,384]{2,1,0:T(1,128)}), f32[256,1,384]{2,1,0:T(1,128)S(1)}, u32[]{:S(2)}, u32[]{:S(2)}) %all-to-all-start.1) | async-done | bytes 393248 | tf_op jit(solution)/shard_map/all_to_all | solution.py:532
  67.5 0.0 copy-done.10
  67.5 0.0 copy-done.12
  67.5 2.2 %shard_map.311 = (f32[784,128]{1,0:T(8,128)S(1)}, f32[3,2048]{1,0:T(4,128)S(1)}) custom-call(s32[64]{0:T(128)S(1)} %fusion.ya, f32[4,2176]{1,0:T(4,128)S(1)} %collective-permute-done.atoms, f32[768,128]{1,0:T(8,128)S(1)} %bitcast.14, bf16[384,384]{1,0:T(8,128)(2,1)S(1)} %copy-done.10, bf16[384,384]{1,0:T(8,128)(2,1)S(1)} %copy-done.11, ...), custom_call_target="tpu_custom_call" | custom-call | flops 1000000 | bytes 1000000 | tf_op jit(solution)/shard_map/pallas_call | solution.py:510
  69.8 1.5 %collective-permute-start.3 = (f32[3,2048]{1,0:T(4,128)S(1)}, f32[3,2048]{1,0:T(4,128)S(1)}, u32[]{:S(2)}, u32[]{:S(2)}) collective-permute-start(f32[3,2048]{1,0:T(4,128)S(1)} %get-tuple-element.16), channel_id=1, source_target_pairs={{0,224},{32,0},{64,32},{96,64},{128,96},{160,128},{192,160},{224,1... | collective-permute-start | bytes 73736 | tf_op jit(solution)/shard_map/ppermute | solution.py:527
  71.3 0.0 collective-permute-done.2.halo
  71.3 1.6 %shard_map.313 = f32[3,2048]{1,0:T(4,128)S(1)} custom-call(s32[64]{0:T(128)S(1)} %bitcast_add_fusion.ya, f32[4,2176]{1,0:T(4,128)S(1)} %get-tuple-element.11.atoms, f32[784,128]{1,0:T(8,128)S(1)} %get-tuple-element.12.grid, f32[3,2048]{1,0:T(4,128)S(1)} %get-tuple-element.14.near, f32[8,128]{1,0:T(8,128)S(1)} %collective-permute-done.2.halo), custom_call_target="tpu_custom_call" | custom-call | flops 3000000000 | bytes 1000000 | tf_op jit(solution)/shard_map/pallas_call | solution.py:510
  72.9 0.0 collective-permute-done.3
  72.9 0.6 add.7
  (18 shorter events, 0.0 us)
Async XLA Ops:
  1.1 2.6 %copy-start.28 = (s32[64,1]{0,1:T(1,128)S(1)}, s32[64,1]{0,1:T(1,128)}, u32[]{:S(2)}) copy-start(s32[64,1]{0,1:T(1,128)} %param.33) | copy-start | bytes 772
  1.1 7.8 %collective-permute-start = (f32[4,2176]{1,0:T(4,128)S(1)}, f32[4,2176]{1,0:T(4,128)S(1)}, u32[]{:S(2)}, u32[]{:S(2)}) collective-permute-start(f32[4,2176]{1,0:T(4,128)S(1)} %get-tuple-element.11.atoms), channel_id=1, source_target_pairs={{0,32},{32,64},{64,96},{96,128},{128,160},{160,192},{192,224},{224... | collective-permute-start | bytes 104456 | tf_op jit(solution)/shard_map/ppermute | solution.py:527
  4.3 4.6 %copy-start.14 = (bf16[384,384]{1,0:T(8,128)(2,1)S(1)}, bf16[384,384]{1,0:T(8,128)(2,1)}, u32[]{:S(2)}) copy-start(bf16[384,384]{1,0:T(8,128)(2,1)} %constant.56.clone.even_high) | copy-start | bytes 884740
  4.3 4.6 %copy-start.15 = (bf16[384,384]{1,0:T(8,128)(2,1)S(1)}, bf16[384,384]{1,0:T(8,128)(2,1)}, u32[]{:S(2)}) copy-start(bf16[384,384]{1,0:T(8,128)(2,1)} %constant.57.clone.even_low) | copy-start | bytes 884740
  4.3 4.6 %copy-start.16 = (bf16[384,384]{1,0:T(8,128)(2,1)S(1)}, bf16[384,384]{1,0:T(8,128)(2,1)}, u32[]{:S(2)}) copy-start(bf16[384,384]{1,0:T(8,128)(2,1)} %constant.58.clone.odd_high) | copy-start | bytes 884740
  4.3 4.6 %copy-start.17 = (bf16[384,384]{1,0:T(8,128)(2,1)S(1)}, bf16[384,384]{1,0:T(8,128)(2,1)}, u32[]{:S(2)}) copy-start(bf16[384,384]{1,0:T(8,128)(2,1)} %constant.59.clone.odd_low) | copy-start | bytes 884740
  4.3 36.6 %copy-start.7 = (bf16[384,512]{1,0:T(8,128)(2,1)S(1)}, bf16[384,512]{1,0:T(8,128)(2,1)}, u32[]{:S(2)}) copy-start(bf16[384,512]{1,0:T(8,128)(2,1)} %constant.68.clone.odd_back_high) | copy-start | bytes 1179652
  4.4 36.6 %copy-start.8 = (bf16[384,512]{1,0:T(8,128)(2,1)S(1)}, bf16[384,512]{1,0:T(8,128)(2,1)}, u32[]{:S(2)}) copy-start(bf16[384,512]{1,0:T(8,128)(2,1)} %constant.69.clone.odd_back_low) | copy-start | bytes 1179652
  4.4 36.6 %copy-start.9 = (bf16[384,512]{1,0:T(8,128)(2,1)S(1)}, bf16[384,512]{1,0:T(8,128)(2,1)}, u32[]{:S(2)}) copy-start(bf16[384,512]{1,0:T(8,128)(2,1)} %constant.70.clone.odd_fine) | copy-start | bytes 1179652
  4.4 36.6 %copy-start.20 = (f32[256,128]{1,0:T(8,128)S(1)}, f32[256,128]{1,0:T(8,128)}, u32[]{:S(2)}) copy-start(f32[256,128]{1,0:T(8,128)} %constant.60.clone.y_info) | copy-start | bytes 393220
  4.4 36.6 %copy-start.21 = (bf16[96,576]{1,0:T(8,128)(2,1)S(1)}, bf16[96,576]{1,0:T(8,128)(2,1)}, u32[]{:S(2)}) copy-start(bf16[96,576]{1,0:T(8,128)(2,1)} %constant.72.clone.tz) | copy-start | bytes 331780
  4.4 36.6 %copy-start.22 = (bf16[96,288]{1,0:T(8,128)(2,1)S(1)}, bf16[96,288]{1,0:T(8,128)(2,1)}, u32[]{:S(2)}) copy-start(bf16[96,288]{1,0:T(8,128)(2,1)} %constant.71.clone.kz) | copy-start | bytes 165892
  8.9 32.0 %copy-start.2 = (bf16[512,384]{1,0:T(8,128)(2,1)S(1)}, bf16[512,384]{1,0:T(8,128)(2,1)}, u32[]{:S(2)}) copy-start(bf16[512,384]{1,0:T(8,128)(2,1)} %constant.63.clone.odd_high) | copy-start | bytes 1179652
  8.9 32.0 %copy-start.3 = (bf16[512,384]{1,0:T(8,128)(2,1)S(1)}, bf16[512,384]{1,0:T(8,128)(2,1)}, u32[]{:S(2)}) copy-start(bf16[512,384]{1,0:T(8,128)(2,1)} %constant.64.clone.odd_low) | copy-start | bytes 1179652
  9.0 32.0 %copy-start.4 = (bf16[384,512]{1,0:T(8,128)(2,1)S(1)}, bf16[384,512]{1,0:T(8,128)(2,1)}, u32[]{:S(2)}) copy-start(bf16[384,512]{1,0:T(8,128)(2,1)} %constant.65.clone.even_back_high) | copy-start | bytes 1179652
  9.0 32.0 %copy-start.5 = (bf16[384,512]{1,0:T(8,128)(2,1)S(1)}, bf16[384,512]{1,0:T(8,128)(2,1)}, u32[]{:S(2)}) copy-start(bf16[384,512]{1,0:T(8,128)(2,1)} %constant.66.clone.even_back_low) | copy-start | bytes 1179652
  9.0 32.0 %copy-start.6 = (bf16[384,512]{1,0:T(8,128)(2,1)S(1)}, bf16[384,512]{1,0:T(8,128)(2,1)}, u32[]{:S(2)}) copy-start(bf16[384,512]{1,0:T(8,128)(2,1)} %constant.67.clone.even_fine) | copy-start | bytes 1179652
  9.0 32.0 %copy-start.23 = (f32[32,128]{1,0:T(8,128)S(1)}, f32[32,128]{1,0:T(8,128)}, u32[]{:S(2)}) copy-start(f32[32,128]{1,0:T(8,128)} %constant.75.clone.z_square) | copy-start | bytes 49156
  9.0 32.0 %copy-start.24 = (f32[32,128]{1,0:T(8,128)S(1)}, f32[32,128]{1,0:T(8,128)}, u32[]{:S(2)}) copy-start(f32[32,128]{1,0:T(8,128)} %constant.76.clone.z_factor) | copy-start | bytes 49156
  9.0 32.0 %copy-start.25 = (f32[1,768]{1,0:T(1,128)S(1)}, f32[1,768]{1,0:T(1,128)}, u32[]{:S(2)}) copy-start(f32[1,768]{1,0:T(1,128)} %constant.73.clone.x_square) | copy-start | bytes 9220
  9.0 32.0 %copy-start.26 = (f32[1,768]{1,0:T(1,128)S(1)}, f32[1,768]{1,0:T(1,128)}, u32[]{:S(2)}) copy-start(f32[1,768]{1,0:T(1,128)} %constant.74.clone.x_factor) | copy-start | bytes 9220
  10.9 30.2 %copy-start = (bf16[512,384]{1,0:T(8,128)(2,1)S(1)}, bf16[512,384]{1,0:T(8,128)(2,1)}, u32[]{:S(2)}) copy-start(bf16[512,384]{1,0:T(8,128)(2,1)} %constant.61.clone.even_high) | copy-start | bytes 1179652
  10.9 30.2 %copy-start.1 = (bf16[512,384]{1,0:T(8,128)(2,1)S(1)}, bf16[512,384]{1,0:T(8,128)(2,1)}, u32[]{:S(2)}) copy-start(bf16[512,384]{1,0:T(8,128)(2,1)} %constant.62.clone.even_low) | copy-start | bytes 1179652
  44.1 23.4 %all-to-all-start.1 = ((f32[256,1,384]{2,1,0:T(1,128)}), f32[256,1,384]{2,1,0:T(1,128)S(1)}, u32[]{:S(2)}, u32[]{:S(2)}) async-start(f32[256,1,384]{2,1,0:T(1,128)} %bitcast.7), calls=%async_computation.1 | async-start | bytes 786432 | tf_op jit(solution)/shard_map/all_to_all | solution.py:532
  50.3 3.4 %collective-permute-start.1 = (f32[4,128]{1,0:T(4,128)S(1)}, f32[4,128]{1,0:T(4,128)S(1)}, u32[]{:S(2)}, u32[]{:S(2)}) collective-permute-start(f32[4,128]{1,0:T(4,128)S(1)} %get-tuple-element.13), channel_id=1, source_target_pairs={{0,31},{1,0},{2,1},{3,2},{4,3},{5,4},{6,5},{7,6},{8,7},{9,8},{10,9... | collective-permute-start | bytes 6152 | tf_op jit(solution)/shard_map/ppermute | solution.py:527
  52.7 1.1 %copy-start.27 = (s32[2,1024]{1,0:T(2,128)S(1)}, s32[2,1024]{1,0:T(2,128)}, u32[]{:S(2)}) copy-start(s32[2,1024]{1,0:T(2,128)} %pairs.1) | copy-start | bytes 24580
  53.8 13.7 %copy-start.10 = (bf16[384,384]{1,0:T(8,128)(2,1)S(1)}, bf16[384,384]{1,0:T(8,128)(2,1)}, u32[]{:S(2)}) copy-start(bf16[384,384]{1,0:T(8,128)(2,1)} %constant.77.clone.even_high) | copy-start | bytes 884740
  53.8 13.7 %copy-start.11 = (bf16[384,384]{1,0:T(8,128)(2,1)S(1)}, bf16[384,384]{1,0:T(8,128)(2,1)}, u32[]{:S(2)}) copy-start(bf16[384,384]{1,0:T(8,128)(2,1)} %constant.78.clone.even_low) | copy-start | bytes 884740
  53.8 13.7 %copy-start.12 = (bf16[384,384]{1,0:T(8,128)(2,1)S(1)}, bf16[384,384]{1,0:T(8,128)(2,1)}, u32[]{:S(2)}) copy-start(bf16[384,384]{1,0:T(8,128)(2,1)} %constant.80.clone.odd_high) | copy-start | bytes 884740
  53.8 13.7 %copy-start.13 = (bf16[384,384]{1,0:T(8,128)(2,1)S(1)}, bf16[384,384]{1,0:T(8,128)(2,1)}, u32[]{:S(2)}) copy-start(bf16[384,384]{1,0:T(8,128)(2,1)} %constant.81.clone.odd_low) | copy-start | bytes 884740
  53.8 13.7 %copy-start.18 = (bf16[384,192]{1,0:T(8,128)(2,1)S(1)}, bf16[384,192]{1,0:T(8,128)(2,1)}, u32[]{:S(2)}) copy-start(bf16[384,192]{1,0:T(8,128)(2,1)} %constant.79.clone.even_fine) | copy-start | bytes 442372
  53.8 13.7 %copy-start.19 = (bf16[384,192]{1,0:T(8,128)(2,1)S(1)}, bf16[384,192]{1,0:T(8,128)(2,1)}, u32[]{:S(2)}) copy-start(bf16[384,192]{1,0:T(8,128)(2,1)} %constant.82.clone.odd_fine) | copy-start | bytes 442372
  57.0 14.3 %collective-permute-start.2 = (f32[8,128]{1,0:T(8,128)S(1)}, f32[8,128]{1,0:T(8,128)S(1)}, u32[]{:S(2)}, u32[]{:S(2)}) collective-permute-start(f32[8,128]{1,0:T(8,128)S(1)} %get-tuple-element.15), channel_id=1, source_target_pairs={{0,1},{1,2},{2,3},{3,4},{4,5},{5,6},{6,7},{7,8},{8,9},{9,10},{10,1... | collective-permute-start | bytes 12296 | tf_op jit(solution)/shard_map/ppermute | solution.py:527
  69.8 3.1 %collective-permute-start.3 = (f32[3,2048]{1,0:T(4,128)S(1)}, f32[3,2048]{1,0:T(4,128)S(1)}, u32[]{:S(2)}, u32[]{:S(2)}) collective-permute-start(f32[3,2048]{1,0:T(4,128)S(1)} %get-tuple-element.16), channel_id=1, source_target_pairs={{0,224},{32,0},{64,32},{96,64},{128,96},{160,128},{192,160},{224,1... | collective-permute-start | bytes 73736 | tf_op jit(solution)/shard_map/ppermute | solution.py:527
